TPU v7x, 768 devices: a whole 4x8x12 slice. The times are simulated.
768 devices in a mesh: row: 96 (over x, z, core), col: 8 (over y).
Axes of the slice: x: 4, y: 8, z: 12, core: 2. Of those that a mesh axis runs over, the one named last changes fastest.
Arguments:
- nodes: bfloat16 [196608, 128], P(('row', 'col')), may hold values from -6 to 6
- edge_feats: bfloat16 [786432, 128], P(('row', 'col')), may hold values from -6 to 6
- edge_blocks: int32 [786432, 2], P(('row', 'col')), may hold values from 0 to 19, as said below
- edge_nodes: int32 [786432, 2], P(('row', 'col')), may hold values from 0 to 127
- send_blocks: int32 [768, 8, 2], P(('row', 'col')), may hold values from 0 to 1
- send_counts: int32 [768, 8], P(('row', 'col')), may hold values from 1 to 2, as said below
- edge_w1: bfloat16 [384, 128], replicated, may hold values from -0.3125 to 0.3125
- edge_b1: float32 [128], replicated, may hold values from -3 to 3
- edge_w2: bfloat16 [128, 128], replicated, may hold values from -0.5 to 0.5
- edge_gain: float32 [128], replicated, may hold values from 0.25 to 1.75
- node_w1: bfloat16 [256, 128], replicated, may hold values from -0.375 to 0.375
- node_b1: float32 [128], replicated, may hold values from -3 to 3
- node_w2: bfloat16 [128, 128], replicated, may hold values from -0.5 to 0.5
- node_gain: float32 [128], replicated, may hold values from 0.25 to 1.75
- node_cot: bfloat16 [196608, 128], P(('row', 'col')), may hold values from -6 to 6
- edge_cot: bfloat16 [786432, 128], P(('row', 'col')), may hold values from -6 to 6
Outputs:
- node_new: bfloat16 [196608, 128], P(('row', 'col'))
- edge_new: bfloat16 [786432, 128], P(('row', 'col'))
- node_grad: float32 [196608, 128], P(('row', 'col'))
- edge_grad: bfloat16 [786432, 128], P(('row', 'col'))
- edge_w1_grad: float32 [384, 128], replicated
- edge_w2_grad: float32 [128, 128], replicated
- node_w1_grad: float32 [256, 128], replicated
- node_w2_grad: float32 [128, 128], replicated
Inputs may be any that keep to these rules, and one draw needn't show every extreme that they name: `send_counts`: every device sends at least one live slot to each device of its group; some device has all 2 slots live toward every device of its group. `edge_blocks`: values below 4 name rim and own blocks; higher ones name live received slots only. Devices at the first and last row index use no missing rim block. The second column is below 2.
All inputs are finite; a program needn't handle non-finite values.
Results may differ from a plain program's by a relative error of at most 0.018.
Values may be sent and summed in bfloat16 or wider, within the bound.
No kernel may reach another device: no remote copies, remote signals or barrier semaphores. Data moves between devices by JAX's collectives and lax.ppermute only.
A program may use at most 32 MiB of HBM per device.

v0:
```python
import jax
import jax.numpy as jnp
from jax import lax
from jax.sharding import PartitionSpec as P

BLOCK = 128
BND = 1


EPS = 1e-05


def padded(cells, sides, width):
    for axis, dim in sides:
        count = lax.axis_size(axis)
        ends = count - 1
        head = lax.slice_in_dim(cells, 0, width, axis=dim)
        tail = lax.slice_in_dim(cells, cells.shape[dim] - width, cells.shape[dim], axis=dim)
        cells = jnp.concatenate(
            [
                lax.ppermute(tail, axis, [(i, (i + 1) % count) for i in range(ends)]),
                cells,
                lax.ppermute(head, axis, [((i + 1) % count, i) for i in range(ends)]),
            ],
            axis=dim,
        )
    return cells


def norm_rows(value, gain):
    mean = jnp.mean(value, axis=-1, keepdims=True)
    centred = value - mean
    spread = jnp.mean(centred * centred, axis=-1, keepdims=True)
    scale = lax.rsqrt(spread + EPS)
    unit = centred * scale
    return (unit * gain, unit, scale)


def norm_back(upstream, unit, scale, gain):
    along = upstream * gain
    return scale * (
        along
        - jnp.mean(along, axis=-1, keepdims=True)
        - unit * jnp.mean(along * unit, axis=-1, keepdims=True)
    )


def silu_slope(first):
    sig = jax.nn.sigmoid(first)
    return sig * (1.0 + first * (1.0 - sig))


def mlp_forward(joined, w_first, b_first, w_second, gain):
    first = jnp.dot(joined, w_first, preferred_element_type=jnp.float32) + b_first
    active = jax.nn.silu(first).astype(jnp.bfloat16)
    second = jnp.dot(active, w_second, preferred_element_type=jnp.float32)
    out, unit, scale = norm_rows(second, gain)
    return (out, (first, active, unit, scale))


def mlp_backward(upstream, joined, saved, w_first, w_second, gain):
    first, active, unit, scale = saved
    d_second = norm_back(upstream, unit, scale, gain).astype(jnp.bfloat16)
    g_second = jnp.dot(active.T, d_second, preferred_element_type=jnp.float32)
    d_active = jnp.dot(d_second, w_second.T, preferred_element_type=jnp.float32)
    d_first = (d_active * silu_slope(first)).astype(jnp.bfloat16)
    g_first = jnp.dot(joined.T, d_first, preferred_element_type=jnp.float32)
    d_joined = jnp.dot(d_first, w_first.T, preferred_element_type=jnp.float32)
    return (d_joined, g_first, g_second)


def local(
    nodes,
    edge_feats,
    edge_blocks,
    edge_nodes,
    send_blocks,
    send_counts,
    edge_w1,
    edge_b1,
    edge_w2,
    edge_gain,
    node_w1,
    node_b1,
    node_w2,
    node_gain,
    node_cot,
    edge_cot,
):
    width = nodes.shape[1]
    local_rows = nodes.shape[0]
    nblk = local_rows // BLOCK
    n_col = lax.axis_size("col")
    n_row = lax.axis_size("row")
    slots = send_blocks.shape[2]
    rim = BND * BLOCK
    rimmed_rows = local_rows + 2 * rim
    rimmed = padded(nodes, (("row", 0),), rim)
    block_src = edge_blocks[:, 0]
    keep = jnp.arange(slots, dtype=jnp.int32)[None, :] < send_counts[0][:, None]
    chosen = nodes.reshape(nblk, BLOCK, width)[send_blocks[0]]
    outgoing = jnp.where(keep[:, :, None, None], chosen, jnp.zeros_like(chosen)).reshape(
        n_col, slots * BLOCK, width
    )
    incoming = lax.all_to_all(outgoing, "col", split_axis=0, concat_axis=0, tiled=True)
    extended = jnp.concatenate([rimmed, incoming.reshape(n_col * slots * BLOCK, width)], axis=0)
    source = block_src * BLOCK + edge_nodes[:, 0]
    target = edge_blocks[:, 1] * BLOCK + edge_nodes[:, 1]
    edge_joined = jnp.concatenate([extended[source], nodes[target], edge_feats], axis=1)
    edge_out, edge_saved = mlp_forward(edge_joined, edge_w1, edge_b1, edge_w2, edge_gain)
    message = edge_out.astype(jnp.bfloat16)
    edge_new = (edge_feats.astype(jnp.float32) + message.astype(jnp.float32)).astype(jnp.bfloat16)
    summed = jax.ops.segment_sum(
        message.astype(jnp.float32), target, num_segments=local_rows
    ).astype(jnp.bfloat16)
    node_joined = jnp.concatenate([nodes, summed], axis=1)
    node_out, node_saved = mlp_forward(node_joined, node_w1, node_b1, node_w2, node_gain)
    node_new = (nodes.astype(jnp.float32) + node_out).astype(jnp.bfloat16)
    upstream = node_cot.astype(jnp.float32)
    d_node_joined, node_g1, node_g2 = mlp_backward(
        upstream, node_joined, node_saved, node_w1, node_w2, node_gain
    )
    d_message = d_node_joined[:, width:][target] + edge_cot.astype(jnp.float32)
    d_edge_joined, edge_g1, edge_g2 = mlp_backward(
        d_message, edge_joined, edge_saved, edge_w1, edge_w2, edge_gain
    )
    edge_grad = (edge_cot.astype(jnp.float32) + d_edge_joined[:, 2 * width :]).astype(jnp.bfloat16)
    grad_ext = jax.ops.segment_sum(d_edge_joined[:, :width], source, num_segments=extended.shape[0])
    back = jnp.concatenate(
        [grad_ext[:rim], grad_ext[rim + local_rows : 2 * rim + local_rows]], axis=0
    )
    returned = padded(back.astype(jnp.bfloat16), (("row", 0),), rim).astype(back.dtype)
    from_slots = grad_ext[rimmed_rows:].reshape(n_col, slots * BLOCK, width)
    slot_back = lax.all_to_all(
        from_slots.astype(jnp.bfloat16), "col", split_axis=0, concat_axis=0, tiled=True
    ).astype(from_slots.dtype)
    picker = (
        send_blocks[0][None, :, :] == jnp.arange(nblk, dtype=jnp.int32)[:, None, None]
    ) & keep[None, :, :]
    picker = picker.astype(jnp.float32).reshape(nblk, n_col * slots)
    from_peers = jnp.dot(
        picker, slot_back.reshape(n_col * slots, BLOCK * width), precision=lax.Precision.HIGHEST
    ).reshape(local_rows, width)
    node_grad = (
        upstream
        + d_node_joined[:, :width]
        + jax.ops.segment_sum(d_edge_joined[:, width : 2 * width], target, num_segments=local_rows)
    )
    node_grad = node_grad + grad_ext[rim : rim + local_rows] + from_peers
    node_grad = (
        node_grad.at[:rim].add(returned[:rim]).at[local_rows - rim :].add(returned[3 * rim :])
    )
    edge_g1, edge_g2, node_g1, node_g2 = lax.psum(
        (edge_g1, edge_g2, node_g1, node_g2), ("row", "col")
    )
    devices = n_row * n_col
    edge_scale = float(edge_feats.shape[0] * devices) ** (-0.5)
    node_scale = float(local_rows * devices) ** (-0.5)
    return (
        node_new,
        edge_new,
        node_grad,
        edge_grad,
        edge_g1 * edge_scale,
        edge_g2 * edge_scale,
        node_g1 * node_scale,
        node_g2 * node_scale,
    )


def solution(mesh):
    placed = (
        P(("row", "col"), None),
        P(("row", "col"), None),
        P(("row", "col"), None),
        P(("row", "col"), None),
        P(("row", "col"), None, None),
        P(("row", "col"), None),
        P(),
        P(),
        P(),
        P(),
        P(),
        P(),
        P(),
        P(),
        P(("row", "col"), None),
        P(("row", "col"), None),
    )
    return jax.shard_map(
        local,
        mesh=mesh,
        in_specs=placed,
        out_specs=(
            P(("row", "col"), None),
            P(("row", "col"), None),
            P(("row", "col"), None),
            P(("row", "col"), None),
            P(),
            P(),
            P(),
            P(),
        ),
        check_vma=False,
    )
```

profile of v0, /device:TPU:1, one launch (start us, length us, event | category | flops | bytes accessed | tf_op | source)
XLA Modules:
  0.0 555.4 jit_solution(3491048139006239205)
XLA Ops:
  8.8 1.5 gather_fusion
  10.4 1.1 bitcast_select_fusion
  11.5 7.7 %all-to-all-start = ((bf16[8,256,128]{2,1,0:T(8,128)(2,1)}), bf16[8,256,128]{2,1,0:T(8,128)(2,1)S(1)}, u32[]{:S(2)}, u32[]{:S(2)}) async-start(bf16[8,256,128]{2,1,0:T(8,128)(2,1)} %bitcast_select_fusion), calls=%async_computation | async-start | bytes 1048576 | tf_op jit(solution)/shard_map/all_to_all | solution.py:105
  19.2 4.8 collective-permute-start
  24.1 4.7 collective-permute-start.1
  30.8 3.2 gather_fusion.2
  34.8 3.2 gather_fusion.1
  38.7 1.2 multiply_convert_fusion.2
  41.6 6.2 %scatter_custom_fusion = f32[256,128]{1,0:T(8,128)S(1)} fusion(s32[1024]{0:T(1024)} %bitcast.47, f32[1024,128]{1,0:T(8,128)S(1)} %copy.41, f32[]{:T(128)} %constant.86.clone.1), kind=kCustom, calls=%fused_computation.57 | custom fusion | flops 131072 | bytes 131584 | tf_op jit(solution)/shard_map/scatter-add | solution.py:113
  51.3 2.8 gather_fusion.3
  56.0 1.1 fusion.41
  58.5 6.5 %scatter_custom_fusion.1 = f32[2560,128]{1,0:T(8,128)S(1)} fusion(s32[1024]{0:T(1024)} %bitcast.49, f32[]{:T(128)} %constant.86.clone.1, f32[1024,384]{1,0:T(8,128)S(1)} %fusion.40), kind=kCustom, calls=%fused_computation.16 | custom fusion | flops 131072 | bytes 1835520 | tf_op jit(solution)/shard_map/scatter-add | solution.py:128
  65.0 0.9 convert.7
  67.5 1.0 copy.55
  68.5 1.8 copy.54
  71.9 6.8 %all-to-all-start.1 = ((bf16[8,256,128]{2,1,0:T(8,128)(2,1)}), bf16[8,256,128]{2,1,0:T(8,128)(2,1)S(1)}, u32[]{:S(2)}, u32[]{:S(2)}) async-start(bf16[8,256,128]{2,1,0:T(8,128)(2,1)} %bitcast.10), calls=%async_computation.1 | async-start | bytes 1048576 | tf_op jit(solution)/shard_map/all_to_all | solution.py:134
  78.7 3.4 collective-permute-start.2
  82.1 1.9 collective-permute-start.3
  84.1 450.5 %all-reduce.3.cloned.1.call-done = (f32[384,128]{1,0:T(8,128)}, f32[128,128]{1,0:T(8,128)}, f32[256,128]{1,0:T(8,128)}, f32[128,128]{1,0:T(8,128)}) async-done(((f32[384,128]{1,0:T(8,128)}, f32[128,128]{1,0:T(8,128)}, f32[256,128]{1,0:T(8,128)}, f32[128,128]{1,0:T(8,128)}), (f32[384,128]{1,0:T(8,128)}, f32[128,128]{1,0:T(8,128)}, f32[256,128]{1,0:T(8,128)}, ...) | async-done | bytes 458768 | tf_op jit(solution)/shard_map/psum | solution.py:153
  534.6 1.5 broadcast_multiply_fusion.3
  536.0 1.5 broadcast_multiply_fusion.2
  537.5 1.6 broadcast_multiply_fusion.1
  539.1 1.7 broadcast_multiply_fusion
  541.6 6.3 %scatter_custom_fusion.2 = f32[256,128]{1,0:T(8,128)S(1)} fusion(f32[256,128]{1,0:T(8,128)S(1)} %copy.50, s32[1024]{0:T(1024)} %bitcast.48, f32[1024,384]{1,0:T(8,128)S(1)} %fusion.40), kind=kCustom, calls=%fused_computation.20 | custom fusion | flops 131072 | bytes 655360 | tf_op jit(solution)/shard_map/scatter-add | solution.py:147
  (126 shorter events, 17.9 us)
Async XLA Ops:
  7.2 31.1 %copy-start = (bf16[384,128]{1,0:T(8,128)(2,1)S(1)}, bf16[384,128]{1,0:T(8,128)(2,1)}, u32[]{:S(2)}) copy-start(bf16[384,128]{1,0:T(8,128)(2,1)} %param.26) | copy-start | bytes 294916
  10.3 8.9 %copy-start.1 = (bf16[256,128]{1,0:T(8,128)(2,1)S(1)}, bf16[256,128]{1,0:T(8,128)(2,1)}, u32[]{:S(2)}) copy-start(bf16[256,128]{1,0:T(8,128)(2,1)} %param.20) | copy-start | bytes 196612
  10.3 18.5 %copy-start.13 = (s32[1024,2]{0,1:T(2,128)S(1)}, s32[1024,2]{0,1:T(2,128)}, u32[]{:S(2)}) copy-start(s32[1024,2]{0,1:T(2,128)} %param.23) | copy-start | bytes 24580
  10.3 18.5 %copy-start.14 = (s32[1024,2]{0,1:T(2,128)S(1)}, s32[1024,2]{0,1:T(2,128)}, u32[]{:S(2)}) copy-start(s32[1024,2]{0,1:T(2,128)} %param.22) | copy-start | bytes 24580
  10.3 19.1 %copy-start.16 = (s32[1,8,2]{1,2,0:T(2,128)S(1)}, s32[1,8,2]{1,2,0:T(2,128)}, u32[]{:S(2)}) copy-start(s32[1,8,2]{1,2,0:T(2,128)} %param.24) | copy-start | bytes 196
  10.4 19.3 %copy-start.20 = (s32[1,8]{1,0:T(1,128)S(1)}, s32[1,8]{1,0:T(1,128)}, u32[]{:S(2)}) copy-start(s32[1,8]{1,0:T(1,128)} %param.25) | copy-start | bytes 100
  10.4 20.2 %copy-start.8 = (bf16[256,128]{1,0:T(8,128)(2,1)S(1)}, bf16[256,128]{1,0:T(8,128)(2,1)}, u32[]{:S(2)}) copy-start(bf16[256,128]{1,0:T(8,128)(2,1)} %param.34) | copy-start | bytes 196612
  10.4 20.3 %copy-start.7 = (bf16[1024,128]{1,0:T(8,128)(2,1)S(1)}, bf16[1024,128]{1,0:T(8,128)(2,1)}, u32[]{:S(2)}) copy-start(bf16[1024,128]{1,0:T(8,128)(2,1)} %param.35) | copy-start | bytes 786436
  11.5 23.3 %all-to-all-start = ((bf16[8,256,128]{2,1,0:T(8,128)(2,1)}), bf16[8,256,128]{2,1,0:T(8,128)(2,1)S(1)}, u32[]{:S(2)}, u32[]{:S(2)}) async-start(bf16[8,256,128]{2,1,0:T(8,128)(2,1)} %bitcast_select_fusion), calls=%async_computation | async-start | bytes 1048576 | tf_op jit(solution)/shard_map/all_to_all | solution.py:105
  19.2 515.4 %all-reduce.3.cloned.1.call-start = ((), (), s32[]{:S(2)}) async-start(), calls=%async_computation.2 | async-start | bytes 917504 | tf_op jit(solution)/shard_map/psum | solution.py:153
  19.2 15.5 %collective-permute-start = (bf16[128,128]{1,0:T(8,128)(2,1)S(1)}, bf16[128,128]{1,0:T(8,128)(2,1)S(1)}, u32[]{:S(2)}, u32[]{:S(2)}) collective-permute-start(bf16[128,128]{1,0:T(8,128)(2,1)S(1)} %get-tuple-element.68), channel_id=1, source_target_pairs={{0,8},{8,16},{16,24},{24,32},{32,40},{40,48},{48,56},{56,64},{64,7... | collective-permute-start | bytes 98312 | tf_op jit(solution)/shard_map/ppermute | solution.py:21
  24.1 10.7 %collective-permute-start.1 = (bf16[128,128]{1,0:T(8,128)(2,1)S(1)}, bf16[128,128]{1,0:T(8,128)(2,1)S(1)}, u32[]{:S(2)}, u32[]{:S(2)}) collective-permute-start(bf16[128,128]{1,0:T(8,128)(2,1)S(1)} %get-tuple-element.69), channel_id=1, source_target_pairs={{8,0},{16,8},{24,16},{32,24},{40,32},{48,40},{56,48},{64,56},{72,6... | collective-permute-start | bytes 98312 | tf_op jit(solution)/shard_map/ppermute | solution.py:23
  30.8 3.2 copy-start.3
  40.5 7.2 %copy-start.9 = (bf16[256,128]{1,0:T(8,128)(2,1)S(1)}, bf16[256,128]{1,0:T(8,128)(2,1)}, u32[]{:S(2)}) copy-start(bf16[256,128]{1,0:T(8,128)(2,1)} %param.30) | copy-start | bytes 196612
  41.4 6.4 %copy-start.22 = (f32[128]{0:T(128)S(1)}, f32[128]{0:T(128)}, u32[]{:S(2)}) copy-start(f32[128]{0:T(128)} %param.31) | copy-start | bytes 1540
  41.4 6.6 %copy-start.11 = (bf16[128,128]{1,0:T(8,128)(2,1)S(1)}, bf16[128,128]{1,0:T(8,128)(2,1)}, u32[]{:S(2)}) copy-start(bf16[128,128]{1,0:T(8,128)(2,1)} %param.32) | copy-start | bytes 98308
  41.4 6.9 %copy-start.17 = (f32[128]{0:T(128)S(1)}, f32[128]{0:T(128)}, u32[]{:S(2)}) copy-start(f32[128]{0:T(128)} %param.33) | copy-start | bytes 1540
  48.0 2.5 copy-start.10
  65.9 5.1 copy-start.2
  71.9 468.9 %all-to-all-start.1 = ((bf16[8,256,128]{2,1,0:T(8,128)(2,1)}), bf16[8,256,128]{2,1,0:T(8,128)(2,1)S(1)}, u32[]{:S(2)}, u32[]{:S(2)}) async-start(bf16[8,256,128]{2,1,0:T(8,128)(2,1)} %bitcast.10), calls=%async_computation.1 | async-start | bytes 1048576 | tf_op jit(solution)/shard_map/all_to_all | solution.py:134
  78.7 462.3 %copy-start.18 = (s32[16]{0:T(128)S(1)}, s32[16]{0:T(128)}, u32[]{:S(2)}) copy-start(s32[16]{0:T(128)} %eq.16) | copy-start | bytes 196
  78.7 462.3 %copy-start.19 = (pred[16]{0:T(512)(128)(4,1)S(1)}, pred[16]{0:T(512)(128)(4,1)}, u32[]{:S(2)}) copy-start(pred[16]{0:T(512)(128)(4,1)} %lt.63) | copy-start | bytes 52
  78.7 469.2 %collective-permute-start.2 = (bf16[128,128]{1,0:T(8,128)(2,1)S(1)}, bf16[128,128]{1,0:T(8,128)(2,1)S(1)}, u32[]{:S(2)}, u32[]{:S(2)}) collective-permute-start(bf16[128,128]{1,0:T(8,128)(2,1)S(1)} %get-tuple-element.62), channel_id=1, source_target_pairs={{0,8},{8,16},{16,24},{24,32},{32,40},{40,48},{48,56},{56,64},{64,7... | collective-permute-start | bytes 98312 | tf_op jit(solution)/shard_map/ppermute | solution.py:21
  82.1 465.7 %collective-permute-start.3 = (bf16[128,128]{1,0:T(8,128)(2,1)S(1)}, bf16[128,128]{1,0:T(8,128)(2,1)S(1)}, u32[]{:S(2)}, u32[]{:S(2)}) collective-permute-start(bf16[128,128]{1,0:T(8,128)(2,1)S(1)} %get-tuple-element.63), channel_id=1, source_target_pairs={{8,0},{16,8},{24,16},{32,24},{40,32},{48,40},{56,48},{64,56},{72,6... | collective-permute-start | bytes 98312 | tf_op jit(solution)/shard_map/ppermute | solution.py:23
  (7 other events, 7.6 us)
Sparse Core Ops, SparseCore 0:
  57.8 476.7 all-reduce.2
where the time goes:
time: 558 us; the launch traced here: 555 us
  waiting for transfers between devices  451 us (81%)
  other arithmetic  32.1 us (6%)
  starting transfers between devices  29.4 us (5%)
  local copies, waits for them, and re-layouts  21.8 us (4%)
  between operations  14.7 us (3%)
  matrix products  6.82 us (1%)
    psum x1, waiting for transfers between devices, local(): lax.psum((edge_g1, edge_g2, node_g1, node_g2), ('row', 'col'))  450 us
  transfers between devices with their start and end apart: 7, of which 1 were waited for; matrix products, arithmetic and copies ran while one was open for 6% of the time, Pallas kernels for 0%

commit v1 on v0

v1 whole, which is shorter than its diff:
```python
import jax
import jax.numpy as jnp
from jax import lax
from jax.experimental import pallas as pl
from jax.experimental.pallas import tpu as pltpu
from jax.sharding import Mesh, PartitionSpec as P

BLOCK = 128
W = 128
EPS = 1e-05
BF = jnp.bfloat16
F32 = jnp.float32

SPLIT = {"x": 4, "z": 12, "c": 2, "y": 8}
ALL = ("x", "z", "c", "y")
ROW = ("x", "z", "c")
SCATTER = ("x", "y")
SPREAD = ("z", "c")
CHUNK = 256
WROWS = 1024


def dot(a, b, dims=((1,), (0,))):
    return lax.dot_general(a, b, (dims, ((), ())), preferred_element_type=F32)


TN = ((0,), (0,))
NT = ((1,), (1,))


def full(shape):
    return pl.BlockSpec(shape, memory_space=pltpu.VMEM)


SMEM = pl.BlockSpec(memory_space=pltpu.SMEM)


def row_mean(v):
    return jnp.mean(v, axis=-1, keepdims=True)


def norm_rows(second):
    centred = second - row_mean(second)
    scale = lax.rsqrt(row_mean(centred * centred) + EPS)
    return centred * scale, scale


def norm_back(along, unit, scale):
    return scale * (along - row_mean(along) - unit * row_mean(along * unit))


def silu_parts(first):
    sig = jax.nn.sigmoid(first)
    return (first * sig).astype(BF), sig * (1.0 + first * (1.0 - sig))


def two_halves(v):
    high = v.astype(BF)
    low = (v - high.astype(F32)).astype(BF)
    return high, low


def marks(node, block, shape, dim):
    spot = lax.broadcasted_iota(jnp.int32, shape, dim).astype(F32)
    return jnp.where(node == spot, block, -1.0).astype(BF)


def one_hot(mark, block):
    return jnp.where(mark == block, 1.0, 0.0).astype(BF)


def pack_kernel(blocks, counts, nodes, out):
    for p in range(out.shape[0]):
        for s in range(out.shape[1] // BLOCK):
            at = pl.multiple_of(blocks[s, p] * BLOCK, BLOCK)
            live = jnp.where(s < counts[0, p], 1.0, 0.0).astype(BF)
            out[p, s * BLOCK : (s + 1) * BLOCK, :] = nodes[pl.ds(at, BLOCK), :] * live


def main_kernel(
    lower, upper, incoming, nodes, eb, en, feats, ecot, ncot,
    ew1, eb1, ew2, egain, nw1, nb1, nw2, ngain,
    node_new, edge_new, wsum, d_first_out, base,
    ext, cols, joined, active, unit, slope, scales, tmark, summed, dsum, g1, g2,
    *, edge_scale, node_scale,
):
    rows = feats.shape[0]
    nblk = nodes.shape[0] // BLOCK
    ext[0:BLOCK, :] = lower[...]
    ext[BLOCK : BLOCK + nblk * BLOCK, :] = nodes[...]
    top = BLOCK + nblk * BLOCK
    ext[top : top + BLOCK, :] = upper[...]
    ext[top + BLOCK :, :] = incoming[...]
    n_ext = ext.shape[0] // BLOCK
    index = jnp.concatenate([eb[...], en[...], eb[...], en[...]], axis=0).astype(F32)
    cols[...] = index.T
    summed[...] = jnp.zeros_like(summed)
    g1[...] = jnp.zeros_like(g1)
    g2[...] = jnp.zeros_like(g2)

    def forward(i, carry):
        at = pl.ds(pl.multiple_of(i * CHUNK, CHUNK), CHUNK)
        col = cols[at, :]
        smark = marks(col[:, 2:3], col[:, 0:1], (CHUNK, BLOCK), 1)
        hot = jnp.concatenate([one_hot(smark, b) for b in range(n_ext)], axis=1)
        joined[at, 0:W] = dot(hot, ext[...]).astype(BF)
        tm = marks(col[:, 3:4], col[:, 1:2], (CHUNK, BLOCK), 1)
        tmark[at, :] = tm
        hot_t = jnp.concatenate([one_hot(tm, b) for b in range(nblk)], axis=1)
        joined[at, W : 2 * W] = dot(hot_t, nodes[...]).astype(BF)
        feat = feats[at, :]
        joined[at, 2 * W : 3 * W] = feat
        first = dot(joined[at, :], ew1[...]) + eb1[...]
        act, slp = silu_parts(first)
        active[at, :] = act
        slope[at, :] = slp
        second = dot(act, ew2[...])
        u, s = norm_rows(second)
        unit[at, :] = u
        scales[at, :] = jnp.broadcast_to(s, (CHUNK, W))
        message = (u * egain[...]).astype(BF)
        edge_new[at, :] = (feat.astype(F32) + message.astype(F32)).astype(BF)
        summed[...] += dot(hot_t, message, TN)
        return carry

    lax.fori_loop(0, rows // CHUNK, forward, 0)

    joined_n = jnp.concatenate([nodes[...], summed[...].astype(BF)], axis=1)
    first = dot(joined_n, nw1[...]) + nb1[...]
    act, slp = silu_parts(first)
    u, s = norm_rows(dot(act, nw2[...]))
    node_new[...] = (nodes[...].astype(F32) + u * ngain[...]).astype(BF)
    upstream = ncot[...].astype(F32)
    d_second = norm_back(upstream * ngain[...], u, s).astype(BF)
    wsum[768:896, :] = (dot(act, d_second, TN) * node_scale).astype(BF)
    d_first = (dot(d_second, nw2[...], NT) * slp).astype(BF)
    wsum[512:768, :] = (dot(joined_n, d_first, TN) * node_scale).astype(BF)
    d_joined = dot(d_first, nw1[...], NT)
    base[...] = upstream + d_joined[:, 0:W]
    high, low = two_halves(d_joined[:, W:])
    dsum[:, 0:W] = high
    dsum[:, W:] = low

    def backward(i, carry):
        at = pl.ds(pl.multiple_of(i * CHUNK, CHUNK), CHUNK)
        tm = tmark[at, :]
        hot_t = jnp.concatenate([one_hot(tm, b) for b in range(nblk)], axis=1)
        both = dot(hot_t, dsum[...])
        d_message = both[:, 0:W] + both[:, W:] + ecot[at, :].astype(F32)
        d_second = norm_back(d_message * egain[...], unit[at, :], scales[at, :]).astype(BF)
        g2[...] += dot(active[at, :], d_second, TN)
        d_first = (dot(d_second, ew2[...], NT) * slope[at, :]).astype(BF)
        d_first_out[at, :] = d_first
        g1[...] += dot(joined[at, :], d_first, TN)
        return carry

    lax.fori_loop(0, rows // CHUNK, backward, 0)
    wsum[0:384, :] = (g1[...] * edge_scale).astype(BF)
    wsum[384:512, :] = (g2[...] * edge_scale).astype(BF)
    wsum[896:, :] = jnp.zeros_like(wsum[896:, :])


def back_kernel(eb, en, d_first, ecot, ew1, slots, to_lower, to_upper, own, target, edge_grad):
    rows = d_first.shape[0]
    d = d_first[...]
    nblk = own.shape[0] // BLOCK
    block = eb[...].astype(F32)
    node = en[...].astype(F32)
    smark = marks(node[0:1, :], block[0:1, :], (BLOCK, rows), 0)

    def part(b, count):
        return dot(jnp.concatenate([one_hot(smark, b + k) for k in range(count)], axis=0), d)

    for p in range(slots.shape[0]):
        slots[p] = part(nblk + 2 + 2 * p, 2).astype(BF)
    to_lower[...] = part(0, 1).astype(BF)
    to_upper[...] = part(nblk + 1, 1).astype(BF)
    own[...] = part(1, nblk)
    tmark = marks(node[1:2, :], block[1:2, :], (BLOCK, rows), 0)
    target[...] = dot(jnp.concatenate([one_hot(tmark, b) for b in range(nblk)], axis=0), d)
    edge_grad[...] = (ecot[...].astype(F32) + dot(d, ew1[2 * W :, :], NT)).astype(BF)


def finish_kernel(blocks, counts, slots, from_lower, from_upper, own, target, base, ew1, out, total):
    nblk = own.shape[0] // BLOCK
    total[...] = own[...]
    total[0:BLOCK, :] += from_lower[...].astype(F32)
    total[(nblk - 1) * BLOCK :, :] += from_upper[...].astype(F32)
    for p in range(slots.shape[0]):
        for s in range(slots.shape[1] // BLOCK):
            at = pl.ds(pl.multiple_of(blocks[s, p] * BLOCK, BLOCK), BLOCK)
            live = jnp.where(s < counts[0, p], 1.0, 0.0)
            total[at, :] += slots[p, s * BLOCK : (s + 1) * BLOCK, :].astype(F32) * live
    source_high, source_low = two_halves(total[...])
    target_high, target_low = two_halves(target[...])
    weights = ew1[...]
    out[...] = (
        base[...]
        + dot(source_high, weights[0:W, :], NT)
        + dot(source_low, weights[0:W, :], NT)
        + dot(target_high, weights[W : 2 * W, :], NT)
        + dot(target_low, weights[W : 2 * W, :], NT)
    )


def add_kernel(pieces, out):
    total = jnp.sum(pieces[...].astype(F32), axis=0).astype(BF)
    for k in range(out.shape[0]):
        out[k] = total


def exchange(value, axes):
    return lax.all_to_all(value, axes, split_axis=0, concat_axis=0, tiled=True)


def call(kernel, outs, scratch=(), in_specs=None, cost=None):
    return pl.pallas_call(
        kernel,
        out_shape=outs,
        in_specs=in_specs,
        out_specs=jax.tree.map(lambda o: pl.BlockSpec(memory_space=pltpu.VMEM), outs),
        scratch_shapes=scratch,
        compiler_params=pltpu.CompilerParams(vmem_limit_bytes=40 << 20),
        cost_estimate=cost,
    )


VM = pl.BlockSpec(memory_space=pltpu.VMEM)


def arr(shape, dtype):
    return jax.ShapeDtypeStruct(shape, dtype)


def local(
    nodes, edge_feats, edge_blocks, edge_nodes, send_blocks, send_counts,
    edge_w1, edge_b1, edge_w2, edge_gain, node_w1, node_b1, node_w2, node_gain,
    node_cot, edge_cot,
):
    own_rows = nodes.shape[0]
    edges = edge_feats.shape[0]
    n_col, slots = send_blocks.shape[1:]
    n_row = lax.axis_size(ROW)
    devices = n_row * n_col
    edge_scale = float(edges * devices) ** (-0.5)
    node_scale = float(own_rows * devices) ** (-0.5)
    blocks = send_blocks[0].T
    up = [(i, i + 1) for i in range(n_row - 1)]
    down = [(i + 1, i) for i in range(n_row - 1)]
    eb = edge_blocks.T
    en = edge_nodes.T

    outgoing = call(
        pack_kernel,
        arr((n_col, slots * BLOCK, W), BF),
        in_specs=[SMEM, SMEM, VM],
        cost=pl.CostEstimate(flops=0, bytes_accessed=600000, transcendentals=0),
    )(blocks, send_counts, nodes)
    incoming = exchange(outgoing, "y")
    lower = lax.ppermute(nodes[own_rows - BLOCK :], ROW, up)
    upper = lax.ppermute(nodes[:BLOCK], ROW, down)

    n_ext = own_rows + 2 * BLOCK + n_col * slots * BLOCK
    node_new, edge_new, wsum, d_first, base = call(
        lambda *refs: main_kernel(*refs, edge_scale=edge_scale, node_scale=node_scale),
        (
            arr((own_rows, W), BF),
            arr((edges, W), BF),
            arr((WROWS, W), BF),
            arr((edges, W), BF),
            arr((own_rows, W), F32),
        ),
        scratch=[
            pltpu.VMEM((n_ext, W), BF),
            pltpu.VMEM((edges, 8), F32),
            pltpu.VMEM((edges, 3 * W), BF),
            pltpu.VMEM((edges, W), BF),
            pltpu.VMEM((edges, W), F32),
            pltpu.VMEM((edges, W), F32),
            pltpu.VMEM((edges, W), F32),
            pltpu.VMEM((edges, W), BF),
            pltpu.VMEM((own_rows, W), F32),
            pltpu.VMEM((own_rows, 2 * W), BF),
            pltpu.VMEM((3 * W, W), F32),
            pltpu.VMEM((W, W), F32),
        ],
        in_specs=[VM] * 17,
        cost=pl.CostEstimate(flops=4 * 10**9, bytes_accessed=4000000, transcendentals=200000),
    )(
        lower, upper, incoming.reshape(n_col * slots * BLOCK, W), nodes, eb, en,
        edge_feats, edge_cot, node_cot,
        edge_w1, edge_b1[None], edge_w2, edge_gain[None],
        node_w1, node_b1[None], node_w2, node_gain[None],
    )

    members = lax.axis_size(SCATTER)
    share = WROWS // members
    pieces = exchange(wsum.reshape(members, share, W), SCATTER)
    spread = lax.axis_size(SPREAD)
    part = call(add_kernel, arr((spread, share, W), BF), in_specs=[VM])(pieces)
    pieces = exchange(part, SPREAD)
    part = call(add_kernel, arr((members, share, W), BF), in_specs=[VM])(pieces)
    weights = exchange(part, SCATTER)
    weights = weights.reshape(WROWS, W).astype(F32)

    slots_out, to_lower, to_upper, own, target, edge_grad = call(
        back_kernel,
        (
            arr((n_col, slots * BLOCK, W), BF),
            arr((BLOCK, W), BF),
            arr((BLOCK, W), BF),
            arr((own_rows, W), F32),
            arr((own_rows, W), F32),
            arr((edges, W), BF),
        ),
        in_specs=[VM] * 5,
        cost=pl.CostEstimate(flops=10**9, bytes_accessed=2000000, transcendentals=0),
    )(eb, en, d_first, edge_cot, edge_w1)
    slot_back = exchange(slots_out, "y")
    from_lower = lax.ppermute(to_upper, ROW, up)
    from_upper = lax.ppermute(to_lower, ROW, down)
    node_grad = call(
        finish_kernel,
        arr((own_rows, W), F32),
        scratch=[pltpu.VMEM((own_rows, W), F32)],
        in_specs=[SMEM, SMEM] + [VM] * 7,
        cost=pl.CostEstimate(flops=10**8, bytes_accessed=1000000, transcendentals=0),
    )(blocks, send_counts, slot_back, from_lower, from_upper, own, target, base, edge_w1)
    return (
        node_new,
        edge_new,
        node_grad,
        edge_grad,
        weights[0:384],
        weights[384:512],
        weights[512:768],
        weights[768:896],
    )


def solution(mesh):
    fine = Mesh(mesh.devices.reshape(tuple(SPLIT.values())), tuple(SPLIT))
    whole = P()
    owned = P(ALL)
    return jax.shard_map(
        local,
        mesh=fine,
        in_specs=(owned,) * 6 + (whole,) * 8 + (owned,) * 2,
        out_specs=(owned,) * 4 + (whole,) * 4,
        check_vma=False,
    )
```

time: 558 us -> 127 us (0.23)
  waiting for transfers between devices: 451 us -> 34.5 us
  other arithmetic: 32.1 us -> 0 us
  blocking collectives: 0 us -> 19.6 us
  starting transfers between devices: 29.4 us -> 48 us
  Pallas kernels: 0 us -> 17.7 us
  local copies, waits for them, and re-layouts: 21.8 us -> 4.17 us
  between operations: 14.7 us -> 0.89 us
  matrix products: 6.82 us -> 0 us
    psum x1 -> x0, waiting for transfers between devices: 450 us -> none  [local(): lax.psum((edge_g1, edge_g2, node_g1, node_g2), ('row', 'col'))]
    all_to_all x2 -> x4, waiting for transfers between devices: 0.01 us -> 30.5 us  [exchange(): return lax.all_to_all(value, axes, split_axis=0, concat_axis=0, tiled=True)]
    all_to_all x0 -> x1, blocking collectives: none -> 19.6 us  [exchange(): return lax.all_to_all(value, axes, split_axis=0, concat_axis=0, tiled=True)]
    all_to_all x2 -> x4, starting transfers between devices: 14.5 us -> 34 us  [exchange(): return lax.all_to_all(value, axes, split_axis=0, concat_axis=0, tiled=True)]
    scatter-add x5 -> x0, other arithmetic: 19 us -> none  [the longest x1 6.5 us: local(): jax.ops.segment_sum(d_edge_joined[:, :width], source, num_segments=extend...]
    pallas_call x0 -> x6, Pallas kernels: none -> 17.7 us  [the longest x1 10.2 us: local(): call(lambda *refs: main_kernel(*refs, edge_scale=edge_scale, node_scale=n...]
    gather x5 -> x0, local copies, waits for them, and re-layouts: 10.9 us -> none  [the longest x1 3.21 us: local(): extended[source]]
    dot_general x13 -> x0, matrix products: 6.82 us -> none  [the longest x2 1.98 us: mlp_backward(): g_first = jnp.dot(joined.T, d_first, preferred_element_type=jnp.float32)]
  transfers between devices with their start and end apart: 7 -> 8, of which waited for: 1 -> 6; matrix products, arithmetic and copies ran while one was open for 6% -> 0% of each run, Pallas kernels for 0% -> 4%
where the time goes in v1:
time: 127 us; the launch traced here: 125 us
  starting transfers between devices  48 us (38%)
  waiting for transfers between devices  34.5 us (27%)
  blocking collectives  19.6 us (15%)
  Pallas kernels  17.7 us (14%)
  local copies, waits for them, and re-layouts  4.17 us (3%)
    all_to_all x4, starting transfers between devices, exchange(): return lax.all_to_all(value, axes, split_axis=0, concat_axis=0, tiled=True)  34 us
    all_to_all x4, waiting for transfers between devices, exchange(): return lax.all_to_all(value, axes, split_axis=0, concat_axis=0, tiled=True)  30.5 us
    all_to_all x1, blocking collectives, exchange(): return lax.all_to_all(value, axes, split_axis=0, concat_axis=0, tiled=True)  19.6 us
    pallas_call x1, Pallas kernels, local(): call(lambda *refs: main_kernel(*refs, edge_scale=edge_scale, node_scale=n...  10.2 us
    ppermute x1, starting transfers between devices, local(): lower = lax.ppermute(nodes[own_rows - BLOCK:], ROW, up)  4.97 us
    ppermute x1, starting transfers between devices, local(): upper = lax.ppermute(nodes[:BLOCK], ROW, down)  4.73 us
    ppermute x1, waiting for transfers between devices, local(): from_upper = lax.ppermute(to_lower, ROW, down)  3.11 us
    pallas_call x1, Pallas kernels, local(): call(back_kernel, (arr((n_col, slots * BLOCK, W), BF), arr((BLOCK, W), BF...  3 us
  transfers between devices with their start and end apart: 8, of which 6 were waited for; matrix products, arithmetic and copies ran while one was open for 0% of the time, Pallas kernels for 4%

profile of v1, /device:TPU:1, one launch (start us, length us, event | category | flops | bytes accessed | tf_op | source)
XLA Modules:
  0.0 124.8 jit_solution(8627471214581670720)
XLA Ops:
  1.3 0.8 copy-done
  2.2 1.5 %shard_map.215 = bf16[8,256,128]{2,1,0:T(8,128)(2,1)} custom-call(s32[2,8]{1,0:T(2,128)S(1)} %bitcast.17, s32[1,8]{1,0:T(1,128)S(1)} %copy-done.4, bf16[256,128]{1,0:T(8,128)(2,1)S(1)} %copy-done), custom_call_target="tpu_custom_call" | custom-call | bytes 600000 | tf_op jit(solution)/shard_map/pallas_call | solution.py:253
  3.7 7.8 %all-to-all-start = ((bf16[8,256,128]{2,1,0:T(8,128)(2,1)}), bf16[8,256,128]{2,1,0:T(8,128)(2,1)S(1)}, u32[]{:S(2)}, u32[]{:S(2)}) async-start(bf16[8,256,128]{2,1,0:T(8,128)(2,1)} %shard_map.215), calls=%async_computation | async-start | bytes 1048576 | tf_op jit(solution)/shard_map/all_to_all | solution.py:213
  11.5 5.0 %collective-permute-start = (bf16[128,128]{1,0:T(8,128)(2,1)S(1)}, bf16[128,128]{1,0:T(8,128)(2,1)S(1)}, u32[]{:S(2)}, u32[]{:S(2)}) collective-permute-start(bf16[128,128]{1,0:T(8,128)(2,1)S(1)} %get-tuple-element.33), channel_id=1, source_target_pairs={{0,8},{8,16},{16,24},{24,32},{32,40},{40,48},{48,56},{56,64},{64,7... | collective-permute-start | bytes 98312 | tf_op jit(solution)/shard_map/ppermute | solution.py:260
  16.5 4.7 %collective-permute-start.1 = (bf16[128,128]{1,0:T(8,128)(2,1)S(1)}, bf16[128,128]{1,0:T(8,128)(2,1)S(1)}, u32[]{:S(2)}, u32[]{:S(2)}) collective-permute-start(bf16[128,128]{1,0:T(8,128)(2,1)S(1)} %get-tuple-element.32), channel_id=1, source_target_pairs={{8,0},{16,8},{24,16},{32,24},{40,32},{48,40},{56,48},{64,56},{72,6... | collective-permute-start | bytes 98312 | tf_op jit(solution)/shard_map/ppermute | solution.py:261
  21.3 0.8 collective-permute-done.1.refs_1_
  22.1 1.6 %all-to-all-done = bf16[8,256,128]{2,1,0:T(8,128)(2,1)S(1)} async-done(((bf16[8,256,128]{2,1,0:T(8,128)(2,1)}), bf16[8,256,128]{2,1,0:T(8,128)(2,1)S(1)}, u32[]{:S(2)}, u32[]{:S(2)}) %all-to-all-start) | async-done | bytes 524320 | tf_op jit(solution)/shard_map/all_to_all | solution.py:213
  24.4 10.2 %shard_map.216 = (bf16[256,128]{1,0:T(8,128)(2,1)}, bf16[1024,128]{1,0:T(8,128)(2,1)}, bf16[1024,128]{1,0:T(8,128)(2,1)S(1)}, bf16[1024,128]{1,0:T(8,128)(2,1)S(1)}, f32[256,128]{1,0:T(8,128)S(1)}) custom-call(bf16[128,128]{1,0:T(8,128)(2,1)S(1)} %collective-permute-done.refs_0_, bf16[128,128]{1,0:T(8,128)(2,1)S(1)} %collective-permute-done.1.refs_1_, ...), custom_call_target="tpu_custom_call" | custom-call | flops 4000000000 | bytes 4000000 | tf_op jit(solution)/shard_map/pallas_call | solution.py:264
  34.5 19.6 %all_to_all.25.pieces = bf16[32,32,128]{2,1,0:T(8,128)(2,1)S(1)} all-to-all(bf16[32,32,128]{2,1,0:T(8,128)(2,1)S(1)} %bitcast.16), channel_id=1, replica_groups=mesh['x'=4,'z'=12,'c'=2,'y'=8] {'x','y'}, dimensions={0} | all-to-all | bytes 524288 | tf_op jit(solution)/shard_map/all_to_all | solution.py:213
  54.1 0.7 shard_map.219
  54.8 18.9 %all-to-all-start.3 = ((bf16[24,32,128]{2,1,0:T(8,128)(2,1)}), bf16[24,32,128]{2,1,0:T(8,128)(2,1)S(1)}, u32[]{:S(2)}, u32[]{:S(2)}) async-start(bf16[24,32,128]{2,1,0:T(8,128)(2,1)} %shard_map.219), calls=%async_computation.3 | async-start | bytes 393216 | tf_op jit(solution)/shard_map/all_to_all | solution.py:213
  73.7 3.0 %shard_map.217 = (bf16[8,256,128]{2,1,0:T(8,128)(2,1)}, bf16[128,128]{1,0:T(8,128)(2,1)S(1)}, bf16[128,128]{1,0:T(8,128)(2,1)S(1)}, f32[256,128]{1,0:T(8,128)S(1...) custom-call(s32[2,1024]{1,0:T(2,128)S(1)} %bitcast.20, s32[2,1024]{1,0:T(2,128)S(1)} %bitcast.22, ...), custom_call_target="tpu_custom_call" | custom-call | flops 1000000000 | bytes 2000000 | tf_op jit(solution)/shard_map/pallas_call | solution.py:306
  76.7 10.7 %all-to-all-done.3.pieces = bf16[24,32,128]{2,1,0:T(8,128)(2,1)S(1)} async-done(((bf16[24,32,128]{2,1,0:T(8,128)(2,1)}), bf16[24,32,128]{2,1,0:T(8,128)(2,1)S(1)}, u32[]{:S(2)}, u32[]{:S(2)}) %all-to-all-start.3) | async-done | bytes 196640 | tf_op jit(solution)/shard_map/all_to_all | solution.py:213
  87.4 3.5 %all-to-all-start.1 = ((bf16[8,256,128]{2,1,0:T(8,128)(2,1)}), bf16[8,256,128]{2,1,0:T(8,128)(2,1)S(1)}, u32[]{:S(2)}, u32[]{:S(2)}) async-start(bf16[8,256,128]{2,1,0:T(8,128)(2,1)} %get-tuple-element.22), calls=%async_computation.1 | async-start | bytes 1048576 | tf_op jit(solution)/shard_map/all_to_all | solution.py:213
  90.9 0.8 shard_map.220
  91.7 17.1 %all-to-all-done.1.slots = bf16[8,256,128]{2,1,0:T(8,128)(2,1)S(1)} async-done(((bf16[8,256,128]{2,1,0:T(8,128)(2,1)}), bf16[8,256,128]{2,1,0:T(8,128)(2,1)S(1)}, u32[]{:S(2)}, u32[]{:S(2)}) %all-to-all-start.1) | async-done | bytes 524320 | tf_op jit(solution)/shard_map/all_to_all | solution.py:213
  108.8 3.9 %all-to-all-start.4 = ((bf16[32,32,128]{2,1,0:T(8,128)(2,1)}), bf16[32,32,128]{2,1,0:T(8,128)(2,1)S(1)}, u32[]{:S(2)}, u32[]{:S(2)}) async-start(bf16[32,32,128]{2,1,0:T(8,128)(2,1)} %shard_map.220), calls=%async_computation.4 | async-start | bytes 524288 | tf_op jit(solution)/shard_map/all_to_all | solution.py:213
  112.7 1.9 %collective-permute-start.2 = (bf16[128,128]{1,0:T(8,128)(2,1)S(1)}, bf16[128,128]{1,0:T(8,128)(2,1)S(1)}, u32[]{:S(2)}, u32[]{:S(2)}) collective-permute-start(bf16[128,128]{1,0:T(8,128)(2,1)S(1)} %get-tuple-element.23), channel_id=1, source_target_pairs={{0,8},{8,16},{16,24},{24,32},{32,40},{40,48},{48,56},{56,64},{64,7... | collective-permute-start | bytes 98312 | tf_op jit(solution)/shard_map/ppermute | solution.py:320
  114.6 2.4 %collective-permute-start.3 = (bf16[128,128]{1,0:T(8,128)(2,1)S(1)}, bf16[128,128]{1,0:T(8,128)(2,1)S(1)}, u32[]{:S(2)}, u32[]{:S(2)}) collective-permute-start(bf16[128,128]{1,0:T(8,128)(2,1)S(1)} %get-tuple-element.24), channel_id=1, source_target_pairs={{8,0},{16,8},{24,16},{32,24},{40,32},{48,40},{56,48},{64,56},{72,6... | collective-permute-start | bytes 98312 | tf_op jit(solution)/shard_map/ppermute | solution.py:321
  117.0 3.1 %collective-permute-done.3.from_upper = bf16[128,128]{1,0:T(8,128)(2,1)S(1)} collective-permute-done((bf16[128,128]{1,0:T(8,128)(2,1)S(1)}, bf16[128,128]{1,0:T(8,128)(2,1)S(1)}, u32[]{:S(2)}, u32[]{:S(2)}) %collective-permute-start.3) | collective-permute-done | bytes 32800 | tf_op jit(solution)/shard_map/ppermute | solution.py:321
  120.1 1.6 %shard_map.218 = f32[256,128]{1,0:T(8,128)} custom-call(s32[2,8]{1,0:T(2,128)S(1)} %bitcast.18, s32[1,8]{1,0:T(1,128)S(1)} %copy-done.4, bf16[8,256,128]{2,1,0:T(8,128)(2,1)S(1)} %all-to-all-done.1.slots, bf16[128,128]{1,0:T(8,128)(2,1)S(1)} %collective-permute-done.2.from_lower, bf16[128,128]{1,0:T(8,128)(2,1)S(1)} %collective-permute-done.3.from_upper, ...), custom_call_target="tpu_custom_call" | custom-call | flops 100000000 | bytes 1000000 | tf_op jit(solution)/shard_map/pallas_call | solution.py:322
  121.7 1.1 all-to-all-done.4
  123.4 0.7 slice.40
  124.1 0.7 slice.42
  (37 shorter events, 2.0 us)
Async XLA Ops:
  0.6 0.7 copy-start.3
  0.6 0.7 copy-start.4
  1.3 0.8 copy-start
  3.6 7.9 %copy-start.1 = (bf16[256,128]{1,0:T(8,128)(2,1)S(1)}, bf16[256,128]{1,0:T(8,128)(2,1)}, u32[]{:S(2)}) copy-start(bf16[256,128]{1,0:T(8,128)(2,1)} %refs_3_.1) | copy-start | bytes 196612
  3.6 20.1 %copy-start.5 = (bf16[1024,128]{1,0:T(8,128)(2,1)S(1)}, bf16[1024,128]{1,0:T(8,128)(2,1)}, u32[]{:S(2)}) copy-start(bf16[1024,128]{1,0:T(8,128)(2,1)} %refs_6_.1) | copy-start | bytes 786436
  3.6 20.1 %copy-start.6 = (bf16[1024,128]{1,0:T(8,128)(2,1)S(1)}, bf16[1024,128]{1,0:T(8,128)(2,1)}, u32[]{:S(2)}) copy-start(bf16[1024,128]{1,0:T(8,128)(2,1)} %ecot.1) | copy-start | bytes 786436
  3.6 20.1 %copy-start.7 = (bf16[256,128]{1,0:T(8,128)(2,1)S(1)}, bf16[256,128]{1,0:T(8,128)(2,1)}, u32[]{:S(2)}) copy-start(bf16[256,128]{1,0:T(8,128)(2,1)} %refs_8_.1) | copy-start | bytes 196612
  3.6 20.1 %copy-start.8 = (bf16[256,128]{1,0:T(8,128)(2,1)S(1)}, bf16[256,128]{1,0:T(8,128)(2,1)}, u32[]{:S(2)}) copy-start(bf16[256,128]{1,0:T(8,128)(2,1)} %refs_13_.1) | copy-start | bytes 196612
  3.6 20.1 %copy-start.10 = (bf16[128,128]{1,0:T(8,128)(2,1)S(1)}, bf16[128,128]{1,0:T(8,128)(2,1)}, u32[]{:S(2)}) copy-start(bf16[128,128]{1,0:T(8,128)(2,1)} %refs_15_.1) | copy-start | bytes 98308
  3.6 20.1 %copy-start.15 = (f32[128]{0:T(128)S(1)}, f32[128]{0:T(128)}, u32[]{:S(2)}) copy-start(f32[128]{0:T(128)} %param.27) | copy-start | bytes 1540
  3.7 20.1 %copy-start.16 = (f32[128]{0:T(128)S(1)}, f32[128]{0:T(128)}, u32[]{:S(2)}) copy-start(f32[128]{0:T(128)} %param.29) | copy-start | bytes 1540
  3.7 20.0 %all-to-all-start = ((bf16[8,256,128]{2,1,0:T(8,128)(2,1)}), bf16[8,256,128]{2,1,0:T(8,128)(2,1)S(1)}, u32[]{:S(2)}, u32[]{:S(2)}) async-start(bf16[8,256,128]{2,1,0:T(8,128)(2,1)} %shard_map.215), calls=%async_computation | async-start | bytes 1048576 | tf_op jit(solution)/shard_map/all_to_all | solution.py:213
  11.5 12.3 %copy-start.2 = (bf16[384,128]{1,0:T(8,128)(2,1)S(1)}, bf16[384,128]{1,0:T(8,128)(2,1)}, u32[]{:S(2)}) copy-start(bf16[384,128]{1,0:T(8,128)(2,1)} %ew1.3) | copy-start | bytes 294916
  11.5 12.3 %copy-start.9 = (bf16[128,128]{1,0:T(8,128)(2,1)S(1)}, bf16[128,128]{1,0:T(8,128)(2,1)}, u32[]{:S(2)}) copy-start(bf16[128,128]{1,0:T(8,128)(2,1)} %refs_11_.1) | copy-start | bytes 98308
  11.5 12.3 %copy-start.12 = (s32[1024,2]{0,1:T(2,128)S(1)}, s32[1024,2]{0,1:T(2,128)}, u32[]{:S(2)}) copy-start(s32[1024,2]{0,1:T(2,128)} %param.19) | copy-start | bytes 24580
  11.5 12.3 %copy-start.11 = (s32[1024,2]{0,1:T(2,128)S(1)}, s32[1024,2]{0,1:T(2,128)}, u32[]{:S(2)}) copy-start(s32[1024,2]{0,1:T(2,128)} %param.18) | copy-start | bytes 24580
  11.5 9.7 %collective-permute-start = (bf16[128,128]{1,0:T(8,128)(2,1)S(1)}, bf16[128,128]{1,0:T(8,128)(2,1)S(1)}, u32[]{:S(2)}, u32[]{:S(2)}) collective-permute-start(bf16[128,128]{1,0:T(8,128)(2,1)S(1)} %get-tuple-element.33), channel_id=1, source_target_pairs={{0,8},{8,16},{16,24},{24,32},{32,40},{40,48},{48,56},{56,64},{64,7... | collective-permute-start | bytes 98312 | tf_op jit(solution)/shard_map/ppermute | solution.py:260
  16.5 5.6 %collective-permute-start.1 = (bf16[128,128]{1,0:T(8,128)(2,1)S(1)}, bf16[128,128]{1,0:T(8,128)(2,1)S(1)}, u32[]{:S(2)}, u32[]{:S(2)}) collective-permute-start(bf16[128,128]{1,0:T(8,128)(2,1)S(1)} %get-tuple-element.32), channel_id=1, source_target_pairs={{8,0},{16,8},{24,16},{32,24},{40,32},{48,40},{56,48},{64,56},{72,6... | collective-permute-start | bytes 98312 | tf_op jit(solution)/shard_map/ppermute | solution.py:261
  23.7 0.7 copy-start.14
  54.8 32.6 %all-to-all-start.3 = ((bf16[24,32,128]{2,1,0:T(8,128)(2,1)}), bf16[24,32,128]{2,1,0:T(8,128)(2,1)S(1)}, u32[]{:S(2)}, u32[]{:S(2)}) async-start(bf16[24,32,128]{2,1,0:T(8,128)(2,1)} %shard_map.219), calls=%async_computation.3 | async-start | bytes 393216 | tf_op jit(solution)/shard_map/all_to_all | solution.py:213
  87.4 21.4 %all-to-all-start.1 = ((bf16[8,256,128]{2,1,0:T(8,128)(2,1)}), bf16[8,256,128]{2,1,0:T(8,128)(2,1)S(1)}, u32[]{:S(2)}, u32[]{:S(2)}) async-start(bf16[8,256,128]{2,1,0:T(8,128)(2,1)} %get-tuple-element.22), calls=%async_computation.1 | async-start | bytes 1048576 | tf_op jit(solution)/shard_map/all_to_all | solution.py:213
  108.8 14.0 %all-to-all-start.4 = ((bf16[32,32,128]{2,1,0:T(8,128)(2,1)}), bf16[32,32,128]{2,1,0:T(8,128)(2,1)S(1)}, u32[]{:S(2)}, u32[]{:S(2)}) async-start(bf16[32,32,128]{2,1,0:T(8,128)(2,1)} %shard_map.220), calls=%async_computation.4 | async-start | bytes 524288 | tf_op jit(solution)/shard_map/all_to_all | solution.py:213
  112.7 4.3 %collective-permute-start.2 = (bf16[128,128]{1,0:T(8,128)(2,1)S(1)}, bf16[128,128]{1,0:T(8,128)(2,1)S(1)}, u32[]{:S(2)}, u32[]{:S(2)}) collective-permute-start(bf16[128,128]{1,0:T(8,128)(2,1)S(1)} %get-tuple-element.23), channel_id=1, source_target_pairs={{0,8},{8,16},{16,24},{24,32},{32,40},{40,48},{48,56},{56,64},{64,7... | collective-permute-start | bytes 98312 | tf_op jit(solution)/shard_map/ppermute | solution.py:320
  114.6 5.5 %collective-permute-start.3 = (bf16[128,128]{1,0:T(8,128)(2,1)S(1)}, bf16[128,128]{1,0:T(8,128)(2,1)S(1)}, u32[]{:S(2)}, u32[]{:S(2)}) collective-permute-start(bf16[128,128]{1,0:T(8,128)(2,1)S(1)} %get-tuple-element.24), channel_id=1, source_target_pairs={{8,0},{16,8},{24,16},{32,24},{40,32},{48,40},{56,48},{64,56},{72,6... | collective-permute-start | bytes 98312 | tf_op jit(solution)/shard_map/ppermute | solution.py:321
  (1 other events, 0.7 us)

commit v2 on v1

v2 whole, which is shorter than its diff:
```python
import jax
import jax.numpy as jnp
from jax import lax
from jax.experimental import pallas as pl
from jax.experimental.pallas import tpu as pltpu
from jax.sharding import Mesh, PartitionSpec as P

BLOCK = 128
W = 128
EPS = 1e-05
BF = jnp.bfloat16
F32 = jnp.float32

SPLIT = {"x": 4, "z": 12, "c": 2, "y": 8}
ALL = ("x", "z", "c", "y")
ROW = ("x", "z", "c")
SCATTER = ("x", "c", "y")
SPREAD = "z"
CHUNK = 256
WROWS = 1024
LABEL = 16


def dot(a, b, dims=((1,), (0,))):
    return lax.dot_general(a, b, (dims, ((), ())), preferred_element_type=F32)


TN = ((0,), (0,))
NT = ((1,), (1,))


def full(shape):
    return pl.BlockSpec(shape, memory_space=pltpu.VMEM)


SMEM = pl.BlockSpec(memory_space=pltpu.SMEM)


def row_mean(v):
    return jnp.mean(v, axis=-1, keepdims=True)


def norm_rows(second):
    centred = second - row_mean(second)
    scale = lax.rsqrt(row_mean(centred * centred) + EPS)
    return centred * scale, scale


def norm_back(along, unit, scale):
    return scale * (along - row_mean(along) - unit * row_mean(along * unit))


def silu_parts(first):
    sig = jax.nn.sigmoid(first)
    return (first * sig).astype(BF), sig * (1.0 + first * (1.0 - sig))


def two_halves(v):
    high = v.astype(BF)
    low = (v - high.astype(F32)).astype(BF)
    return high, low


def marks(node, block, shape, dim):
    spot = lax.broadcasted_iota(jnp.int32, shape, dim).astype(F32)
    return jnp.where(node == spot, block, -1.0).astype(BF)


def one_hot(mark, block):
    if not isinstance(block, int):
        block = jnp.full(mark.shape, block.astype(F32)).astype(BF)
    return jnp.where(mark == block, 1.0, 0.0).astype(BF)


def pack_kernel(blocks, counts, nodes, out):
    n_slots = blocks.shape[0]
    pair = n_slots * BLOCK
    spot = lax.broadcasted_iota(jnp.int32, (LABEL, W), 0)
    for p in range(out.shape[0]):
        label = jnp.zeros((LABEL, W), F32)
        for s in range(n_slots):
            at = pl.multiple_of(blocks[s, p] * BLOCK, BLOCK)
            live = jnp.where(s < counts[0, p], 1.0, 0.0).astype(BF)
            out[p, s * BLOCK : (s + 1) * BLOCK, :] = nodes[pl.ds(at, BLOCK), :] * live
            label = jnp.where(spot == s, blocks[s, p].astype(F32), label)
        out[p, pair:, :] = label.astype(BF)


def early_kernel(nodes, eb, en, feats, ew1, eb1, smark, upper_half, tmark, joined, partial, cols, *, half):
    rows = feats.shape[0]
    nblk = nodes.shape[0] // BLOCK
    index = jnp.concatenate([eb[...], en[...], eb[...], en[...]], axis=0).astype(F32)
    cols[...] = index.T

    def step(i, carry):
        at = pl.ds(pl.multiple_of(i * CHUNK, CHUNK), CHUNK)
        col = cols[at, :]
        block = col[:, 0:1]
        high = block >= half
        smark[at, :] = marks(col[:, 2:3], jnp.where(high, block - half, block), (CHUNK, BLOCK), 1)
        upper_half[at, :] = jnp.broadcast_to(jnp.where(high, 1.0, 0.0), (CHUNK, W)).astype(BF)
        tm = marks(col[:, 3:4], col[:, 1:2], (CHUNK, BLOCK), 1)
        tmark[at, :] = tm
        hot_t = jnp.concatenate([one_hot(tm, b) for b in range(nblk)], axis=1)
        joined[at, 0:W] = dot(hot_t, nodes[...]).astype(BF)
        joined[at, W : 2 * W] = feats[at, :]
        partial[at, :] = dot(joined[at, :], ew1[W:, :]) + eb1[...]
        return carry

    lax.fori_loop(0, rows // CHUNK, step, 0)


def main_kernel(
    lower, upper, incoming, nodes, eb, en, smark, upper_half, tmark, joined, partial, ecot, ncot,
    ew1, ew2, egain, nw1, nb1, nw2, ngain,
    node_new, edge_new, wsum, d_first_out, base,
    ext, gathered, active, unit, slope, scales, summed, dsum, g1, g2,
    *, edge_scale, node_scale,
):
    rows = joined.shape[0]
    nblk = nodes.shape[0] // BLOCK
    half = ext.shape[0] // BLOCK

    def place(b, block):
        at = (b % half) * BLOCK
        ext[at : at + BLOCK, (b // half) * W : (b // half + 1) * W] = block

    place(0, lower[...])
    for b in range(nblk):
        place(1 + b, nodes[b * BLOCK : (b + 1) * BLOCK, :])
    place(1 + nblk, upper[...])
    n_slots = 2 * (half - 1) // incoming.shape[0]
    for p in range(incoming.shape[0]):
        for k in range(n_slots):
            place(2 + nblk + n_slots * p + k, incoming[p, k * BLOCK : (k + 1) * BLOCK, :])
    summed[...] = jnp.zeros_like(summed)
    g1[...] = jnp.zeros_like(g1)
    g2[...] = jnp.zeros_like(g2)

    def target_hot(at):
        tm = tmark[at, :]
        return jnp.concatenate([one_hot(tm, b) for b in range(nblk)], axis=1)

    def forward(i, carry):
        at = pl.ds(pl.multiple_of(i * CHUNK, CHUNK), CHUNK)
        sm = smark[at, :]
        hot = jnp.concatenate([one_hot(sm, b) for b in range(half)], axis=1)
        both = dot(hot, ext[...])
        source = jnp.where(upper_half[at, :].astype(F32) > 0.5, both[:, W:], both[:, 0:W]).astype(BF)
        gathered[at, :] = source
        act, slp = silu_parts(partial[at, :] + dot(source, ew1[0:W, :]))
        active[at, :] = act
        slope[at, :] = slp
        u, s = norm_rows(dot(act, ew2[...]))
        unit[at, :] = u
        scales[at, :] = jnp.broadcast_to(s, (CHUNK, W))
        message = (u * egain[...]).astype(BF)
        edge_new[at, :] = (joined[at, W:].astype(F32) + message.astype(F32)).astype(BF)
        row = marks(en[1:2, at].astype(F32), eb[1:2, at].astype(F32), (BLOCK, CHUNK), 0)
        hot_row = jnp.concatenate([one_hot(row, b) for b in range(nblk)], axis=0)
        summed[...] += dot(hot_row, message)
        return carry

    lax.fori_loop(0, rows // CHUNK, forward, 0)

    joined_n = jnp.concatenate([nodes[...], summed[...].astype(BF)], axis=1)
    first = dot(joined_n, nw1[...]) + nb1[...]
    act, slp = silu_parts(first)
    u, s = norm_rows(dot(act, nw2[...]))
    node_new[...] = (nodes[...].astype(F32) + u * ngain[...]).astype(BF)
    upstream = ncot[...].astype(F32)
    d_second = norm_back(upstream * ngain[...], u, s).astype(BF)
    wsum[768:896, :] = (dot(act, d_second, TN) * node_scale).astype(BF)
    d_first = (dot(d_second, nw2[...], NT) * slp).astype(BF)
    wsum[512:768, :] = (dot(joined_n, d_first, TN) * node_scale).astype(BF)
    d_joined = dot(d_first, nw1[...], NT)
    base[...] = upstream + d_joined[:, 0:W]
    high, low = two_halves(d_joined[:, W:])
    dsum[:, 0:W] = high
    dsum[:, W:] = low

    def backward(i, carry):
        at = pl.ds(pl.multiple_of(i * CHUNK, CHUNK), CHUNK)
        both = dot(target_hot(at), dsum[...])
        d_message = both[:, 0:W] + both[:, W:] + ecot[at, :].astype(F32)
        d_second = norm_back(d_message * egain[...], unit[at, :], scales[at, :]).astype(BF)
        g2[...] += dot(d_second, active[at, :], TN)
        d_first = (dot(d_second, ew2[...], NT) * slope[at, :]).astype(BF)
        d_first_out[at, :] = d_first
        sources = jnp.concatenate([gathered[at, :], joined[at, :]], axis=1)
        g1[...] += dot(d_first, sources, TN)
        return carry

    lax.fori_loop(0, rows // CHUNK, backward, 0)
    wsum[0:384, :] = (g1[...].T * edge_scale).astype(BF)
    wsum[384:512, :] = (g2[...].T * edge_scale).astype(BF)
    wsum[896:, :] = jnp.zeros_like(wsum[896:, :])


def back_kernel(
    me, eb, en, incoming, d_first, ecot, ew1,
    far, near, to_lower, to_upper, own, target, edge_grad,
):
    rows = d_first.shape[0]
    d = d_first[...]
    nblk = own.shape[0] // BLOCK
    peers, n_slots = incoming.shape[0], incoming.shape[1] // BLOCK
    names = n_slots * BLOCK
    rim_blocks = nblk + 2
    block = eb[0:1, :].astype(F32)
    node = en[...].astype(F32)
    owned = block
    for p in range(peers):
        for s in range(n_slots):
            there = incoming[p, names + s : names + s + 1, 0:1].astype(F32) + float(rim_blocks + nblk * p)
            owned = jnp.where(block == float(rim_blocks + n_slots * p + s), there, owned)
    smark = marks(node[0:1, :], owned, (BLOCK, rows), 0)

    def part(b, count):
        return dot(jnp.concatenate([one_hot(smark, b + k) for k in range(count)], axis=0), d)

    for place in range(peers):
        sums = part(rim_blocks + nblk * (me[0] ^ place), nblk)
        if place < peers // 2:
            near[place] = sums
        else:
            far[place - peers // 2] = sums.astype(BF)
    to_lower[...] = part(0, 1).astype(BF)
    to_upper[...] = part(nblk + 1, 1).astype(BF)
    own[...] = part(1, nblk)
    tmark = marks(node[1:2, :], eb[1:2, :].astype(F32), (BLOCK, rows), 0)
    target[...] = dot(jnp.concatenate([one_hot(tmark, b) for b in range(nblk)], axis=0), d)
    edge_grad[...] = (ecot[...].astype(F32) + dot(d, ew1[2 * W :, :], NT)).astype(BF)


def fold_kernel(*refs):
    near, arrived, keep, send = refs[-4:]
    count = keep.shape[0]
    for k in range(2 * count):
        total = near[k] + arrived[k].astype(F32)
        if k < count:
            keep[k] = total
        else:
            send[k - count] = total.astype(BF)


def finish_kernel(near, arrived, from_lower, from_upper, own, target, base, ew1, out, total):
    nblk = own.shape[0] // BLOCK
    total[...] = own[...] + near[0] + arrived[0].astype(F32)
    total[0:BLOCK, :] += from_lower[...].astype(F32)
    total[(nblk - 1) * BLOCK :, :] += from_upper[...].astype(F32)
    source_high, source_low = two_halves(total[...])
    target_high, target_low = two_halves(target[...])
    weights = ew1[...]
    out[...] = (
        base[...]
        + dot(source_high, weights[0:W, :], NT)
        + dot(source_low, weights[0:W, :], NT)
        + dot(target_high, weights[W : 2 * W, :], NT)
        + dot(target_low, weights[W : 2 * W, :], NT)
    )


def unpack_kernel(weights, *outs):
    at = 0
    share = weights.shape[1]
    for out in outs:
        for k in range(out.shape[0] // share):
            out[k * share : (k + 1) * share, :] = weights[at].astype(F32)
            at += 1


def add_kernel(pieces, out):
    total = jnp.sum(pieces[...].astype(F32), axis=0).astype(BF)
    for k in range(out.shape[0]):
        out[k] = total


def exchange(value, axes):
    return lax.all_to_all(value, axes, split_axis=0, concat_axis=0, tiled=True)


def swap(value, bit):
    return lax.ppermute(value, "y", [(i, i ^ bit) for i in range(lax.axis_size("y"))])


def fold(after, near, arrived):
    some = [pl.BlockSpec(memory_space=pl.ANY)] * len(after)
    count, *rest = near.shape
    return call(
        fold_kernel,
        (arr((count // 2, *rest), F32), arr((count // 2, *rest), BF)),
        in_specs=some + [VM, VM],
    )(*after, near, arrived)


def call(kernel, outs, scratch=(), in_specs=None, cost=None):
    return pl.pallas_call(
        kernel,
        out_shape=outs,
        in_specs=in_specs,
        out_specs=jax.tree.map(lambda o: pl.BlockSpec(memory_space=pltpu.VMEM), outs),
        scratch_shapes=scratch,
        compiler_params=pltpu.CompilerParams(vmem_limit_bytes=60 << 20),
        cost_estimate=cost,
    )


VM = pl.BlockSpec(memory_space=pltpu.VMEM)


def arr(shape, dtype):
    return jax.ShapeDtypeStruct(shape, dtype)


def local(
    nodes, edge_feats, edge_blocks, edge_nodes, send_blocks, send_counts,
    edge_w1, edge_b1, edge_w2, edge_gain, node_w1, node_b1, node_w2, node_gain,
    node_cot, edge_cot,
):
    own_rows = nodes.shape[0]
    edges = edge_feats.shape[0]
    n_col, slots = send_blocks.shape[1:]
    n_row = lax.axis_size(ROW)
    devices = n_row * n_col
    edge_scale = float(edges * devices) ** (-0.5)
    node_scale = float(own_rows * devices) ** (-0.5)
    blocks = send_blocks[0].T
    up = [(i, i + 1) for i in range(n_row - 1)]
    down = [(i + 1, i) for i in range(n_row - 1)]
    eb = edge_blocks.T
    en = edge_nodes.T

    outgoing = call(
        pack_kernel,
        arr((n_col, slots * BLOCK + LABEL, W), BF),
        in_specs=[SMEM, SMEM, VM],
        cost=pl.CostEstimate(flops=0, bytes_accessed=600000, transcendentals=0),
    )(blocks, send_counts, nodes)
    incoming = exchange(outgoing, "y")
    lower = lax.ppermute(nodes[own_rows - BLOCK :], ROW, up)
    upper = lax.ppermute(nodes[:BLOCK], ROW, down)

    n_ext = own_rows + 2 * BLOCK + n_col * slots * BLOCK
    smark, upper_half, tmark, joined, partial = call(
        lambda *refs: early_kernel(*refs, half=n_ext // BLOCK // 2),
        (
            arr((edges, W), BF),
            arr((edges, W), BF),
            arr((edges, W), BF),
            arr((edges, 2 * W), BF),
            arr((edges, W), F32),
        ),
        scratch=[pltpu.VMEM((edges, 8), F32)],
        in_specs=[VM] * 6,
        cost=pl.CostEstimate(flops=2 * 10**8, bytes_accessed=8000000, transcendentals=0),
    )(nodes, eb, en, edge_feats, edge_w1, edge_b1[None])
    node_new, edge_new, wsum, d_first, base = call(
        lambda *refs: main_kernel(*refs, edge_scale=edge_scale, node_scale=node_scale),
        (
            arr((own_rows, W), BF),
            arr((edges, W), BF),
            arr((WROWS, W), BF),
            arr((edges, W), BF),
            arr((own_rows, W), F32),
        ),
        scratch=[
            pltpu.VMEM((n_ext // 2, 2 * W), BF),
            pltpu.VMEM((edges, W), BF),
            pltpu.VMEM((edges, W), BF),
            pltpu.VMEM((edges, W), F32),
            pltpu.VMEM((edges, W), F32),
            pltpu.VMEM((edges, W), F32),
            pltpu.VMEM((own_rows, W), F32),
            pltpu.VMEM((own_rows, 2 * W), BF),
            pltpu.VMEM((W, 3 * W), F32),
            pltpu.VMEM((W, W), F32),
        ],
        in_specs=[VM] * 20,
        cost=pl.CostEstimate(flops=4 * 10**9, bytes_accessed=4000000, transcendentals=200000),
    )(
        lower, upper, incoming, nodes, eb, en, smark, upper_half, tmark,
        joined, partial, edge_cot, node_cot,
        edge_w1, edge_w2, edge_gain[None], node_w1, node_b1[None], node_w2, node_gain[None],
    )

    members = lax.axis_size(SCATTER)
    share = WROWS // members
    spread = lax.axis_size(SPREAD)
    pieces = exchange(wsum.reshape(members, share, W), SCATTER)

    me = lax.axis_index("y").astype(jnp.int32)[None]
    far, near, to_lower, to_upper, own, target, edge_grad = call(
        back_kernel,
        (
            arr((n_col // 2, own_rows, W), BF),
            arr((n_col // 2, own_rows, W), F32),
            arr((BLOCK, W), BF),
            arr((BLOCK, W), BF),
            arr((own_rows, W), F32),
            arr((own_rows, W), F32),
            arr((edges, W), BF),
        ),
        in_specs=[SMEM] + [VM] * 6,
        cost=pl.CostEstimate(flops=10**9, bytes_accessed=2000000, transcendentals=0),
    )(me, eb, en, incoming, d_first, edge_cot, edge_w1)
    far = swap(far, 4)
    from_lower = lax.ppermute(to_upper, ROW, up)
    from_upper = lax.ppermute(to_lower, ROW, down)

    part = call(add_kernel, arr((spread, share, W), BF), in_specs=[VM])(pieces)
    pieces = exchange(part, SPREAD)
    near, far = fold((part,), near, far)
    far = swap(far, 2)
    part = call(add_kernel, arr((members, share, W), BF), in_specs=[VM])(pieces)
    weights = exchange(part, SCATTER)
    near, far = fold((part, from_lower, from_upper), near, far)
    far = swap(far, 1)
    node_grad = call(
        finish_kernel,
        arr((own_rows, W), F32),
        scratch=[pltpu.VMEM((own_rows, W), F32)],
        in_specs=[VM] * 8,
        cost=pl.CostEstimate(flops=10**8, bytes_accessed=1000000, transcendentals=0),
    )(near, far, from_lower, from_upper, own, target, base, edge_w1)
    grads = call(
        unpack_kernel,
        tuple(arr((rows, W), F32) for rows in (3 * W, W, 2 * W, W)),
        in_specs=[VM],
    )(weights)
    return (node_new, edge_new, node_grad, edge_grad) + tuple(grads)


def solution(mesh):
    fine = Mesh(mesh.devices.reshape(tuple(SPLIT.values())), tuple(SPLIT))
    whole = P()
    owned = P(ALL)
    return jax.shard_map(
        local,
        mesh=fine,
        in_specs=(owned,) * 6 + (whole,) * 8 + (owned,) * 2,
        out_specs=(owned,) * 4 + (whole,) * 4,
        check_vma=False,
    )
```

time: 127 us -> 148 us (1.17)
  Pallas kernels: 17.7 us -> 31.2 us
  waiting for transfers between devices: 34.5 us -> 24.8 us
  blocking collectives: 19.6 us -> 29.1 us
  starting transfers between devices: 48 us -> 55.6 us
    all_to_all x4 -> x3, waiting for transfers between devices: 30.5 us -> 9.69 us  [exchange(): return lax.all_to_all(value, axes, split_axis=0, concat_axis=0, tiled=True)]
    ppermute x0 -> x3, starting transfers between devices: none -> 17.6 us  [swap(): lax.ppermute(value, 'y', [(i, i ^ bit) for i in range(lax.axis_size('y'))])]
    ppermute x0 -> x3, waiting for transfers between devices: none -> 11.8 us  [swap(): lax.ppermute(value, 'y', [(i, i ^ bit) for i in range(lax.axis_size('y'))])]
    pallas_call x2 -> x6, Pallas kernels: 4.45 us -> 15.4 us  [the longest x1 4.38 us: local(): call(back_kernel, (arr((n_col // 2, own_rows, W), BF), arr((n_col // 2, o...]
    all_to_all x4 -> x3, starting transfers between devices: 34 us -> 23.5 us  [exchange(): return lax.all_to_all(value, axes, split_axis=0, concat_axis=0, tiled=True)]
    all_to_all x1, blocking collectives: 19.6 us -> 29.1 us  [exchange(): return lax.all_to_all(value, axes, split_axis=0, concat_axis=0, tiled=True)]
    slice x3 -> x0, local copies, waits for them, and re-layouts: 2.02 us -> none  [the longest x1 0.69 us: local(): weights[0:384]]
    unnamed x34 -> x26, local copies, waits for them, and re-layouts: 2.14 us -> 4.13 us
  transfers between devices with their start and end apart: 8 -> 10, of which waited for: 6 -> 4; matrix products, arithmetic and copies ran while one was open for 0% -> 0% of each run, Pallas kernels for 4% -> 10%
where the time goes in v2:
time: 148 us; the launch traced here: 146 us
  starting transfers between devices  55.6 us (38%)
  Pallas kernels  31.2 us (21%)
  blocking collectives  29.1 us (20%)
  waiting for transfers between devices  24.8 us (17%)
  local copies, waits for them, and re-layouts  4.14 us (3%)
    all_to_all x1, blocking collectives, exchange(): return lax.all_to_all(value, axes, split_axis=0, concat_axis=0, tiled=True)  29.1 us
    all_to_all x3, starting transfers between devices, exchange(): return lax.all_to_all(value, axes, split_axis=0, concat_axis=0, tiled=True)  23.5 us
    ppermute x3, starting transfers between devices, swap(): lax.ppermute(value, 'y', [(i, i ^ bit) for i in range(lax.axis_size('y'))])  17.6 us
    ppermute x3, waiting for transfers between devices, swap(): lax.ppermute(value, 'y', [(i, i ^ bit) for i in range(lax.axis_size('y'))])  11.8 us
    pallas_call x1, Pallas kernels, local(): call(lambda *refs: main_kernel(*refs, edge_scale=edge_scale, node_scale=n...  10.6 us
    all_to_all x3, waiting for transfers between devices, exchange(): return lax.all_to_all(value, axes, split_axis=0, concat_axis=0, tiled=True)  9.69 us
    ppermute x1, starting transfers between devices, local(): lower = lax.ppermute(nodes[own_rows - BLOCK:], ROW, up)  4.84 us
    ppermute x1, starting transfers between devices, local(): upper = lax.ppermute(nodes[:BLOCK], ROW, down)  4.77 us
  transfers between devices with their start and end apart: 10, of which 4 were waited for; matrix products, arithmetic and copies ran while one was open for 0% of the time, Pallas kernels for 10%

profile of v2, /device:TPU:1, one launch (start us, length us, event | category | flops | bytes accessed | tf_op | source)
XLA Modules:
  0.0 145.6 jit_solution(13392604607375443705)
XLA Ops:
  0.6 1.8 %shard_map.215 = bf16[8,272,128]{2,1,0:T(8,128)(2,1)} custom-call(s32[2,8]{1,0:T(2,128)} %bitcast.12, s32[1,8]{1,0:T(1,128)} %counts.1, bf16[256,128]{1,0:T(8,128)(2,1)} %refs_3_.3), custom_call_target="tpu_custom_call" | custom-call | bytes 600000 | tf_op jit(solution)/shard_map/pallas_call | solution.py:334
  2.4 7.8 %all-to-all-start = ((bf16[8,272,128]{2,1,0:T(8,128)(2,1)}), bf16[8,272,128]{2,1,0:T(8,128)(2,1)S(1)}, u32[]{:S(2)}, u32[]{:S(2)}) async-start(bf16[8,272,128]{2,1,0:T(8,128)(2,1)} %shard_map.215), calls=%async_computation | async-start | bytes 1114112 | tf_op jit(solution)/shard_map/all_to_all | solution.py:280
  10.2 4.8 %collective-permute-start = (bf16[128,128]{1,0:T(8,128)(2,1)S(1)}, bf16[128,128]{1,0:T(8,128)(2,1)S(1)}, u32[]{:S(2)}, u32[]{:S(2)}) collective-permute-start(bf16[128,128]{1,0:T(8,128)(2,1)S(1)} %get-tuple-element.59), channel_id=1, source_target_pairs={{0,8},{8,16},{16,24},{24,32},{32,40},{40,48},{48,56},{56,64},{64,7... | collective-permute-start | bytes 98312 | tf_op jit(solution)/shard_map/ppermute | solution.py:341
  15.0 4.8 %collective-permute-start.1 = (bf16[128,128]{1,0:T(8,128)(2,1)S(1)}, bf16[128,128]{1,0:T(8,128)(2,1)S(1)}, u32[]{:S(2)}, u32[]{:S(2)}) collective-permute-start(bf16[128,128]{1,0:T(8,128)(2,1)S(1)} %get-tuple-element.58), channel_id=1, source_target_pairs={{8,0},{16,8},{24,16},{32,24},{40,32},{48,40},{56,48},{64,56},{72,6... | collective-permute-start | bytes 98312 | tf_op jit(solution)/shard_map/ppermute | solution.py:342
  19.8 4.0 %shard_map.216 = (bf16[1024,128]{1,0:T(8,128)(2,1)}, bf16[1024,128]{1,0:T(8,128)(2,1)}, bf16[1024,128]{1,0:T(8,128)(2,1)}, bf16[1024,256]{1,0:T(8,128)(2,1)}, f32[1024,128]{1,0:T(8,128)}) custom-call(bf16[256,128]{1,0:T(8,128)(2,1)} %refs_3_.3, s32[2,1024]{1,0:T(2,128)} %bitcast.13, s32[2,1024]{1,0:T(2,128)} %bitcast.16, bf16[1024,128]{1,0:T(8,128)(2,1)} %refs_3_.2, ...), custom_call_target="tpu_custom_call" | custom-call | flops 200000000 | bytes 8000000 | tf_op jit(solution)/shard_map/pallas_call | solution.py:345
  24.7 10.6 %shard_map.217 = (bf16[256,128]{1,0:T(8,128)(2,1)}, bf16[1024,128]{1,0:T(8,128)(2,1)}, bf16[1024,128]{1,0:T(8,128)(2,1)}, bf16[1024,128]{1,0:T(8,128)(2,1)}, f32[256,128]{1,0:T(8,128)}) custom-call(bf16[128,128]{1,0:T(8,128)(2,1)} %copy-done.11, bf16[128,128]{1,0:T(8,128)(2,1)} %copy-done.12, bf16[8,272,128]{2,1,0:T(8,128)(2,1)} %copy-done.1, ...), custom_call_target="tpu_custom_call" | custom-call | flops 4000000000 | bytes 4000000 | tf_op jit(solution)/shard_map/pallas_call | solution.py:358
  35.2 29.1 %all_to_all.20.pieces = bf16[64,16,128]{2,1,0:T(8,128)(2,1)} all-to-all(bf16[64,16,128]{2,1,0:T(8,128)(2,1)} %bitcast.11), channel_id=1, replica_groups=mesh['x'=4,'z'=12,'c'=2,'y'=8] {'x','c','y'}, dimensions={0} | all-to-all | bytes 524288 | tf_op jit(solution)/shard_map/all_to_all | solution.py:280
  64.3 1.6 %shard_map.218.refs_0_ = bf16[12,16,128]{2,1,0:T(8,128)(2,1)} custom-call(bf16[64,16,128]{2,1,0:T(8,128)(2,1)} %all_to_all.20.pieces), custom_call_target="tpu_custom_call" | custom-call | tf_op jit(solution)/shard_map/pallas_call | solution.py:411
  66.0 8.3 %all-to-all-start.2 = ((bf16[12,16,128]{2,1,0:T(8,128)(2,1)}), bf16[12,16,128]{2,1,0:T(8,128)(2,1)S(1)}, u32[]{:S(2)}, u32[]{:S(2)}) async-start(bf16[12,16,128]{2,1,0:T(8,128)(2,1)} %shard_map.218.refs_0_), calls=%async_computation.2 | async-start | bytes 98304 | tf_op jit(solution)/shard_map/all_to_all | solution.py:280
  74.2 9.7 %all-to-all-done.2.pieces = bf16[12,16,128]{2,1,0:T(8,128)(2,1)S(1)} async-done(((bf16[12,16,128]{2,1,0:T(8,128)(2,1)}), bf16[12,16,128]{2,1,0:T(8,128)(2,1)S(1)}, u32[]{:S(2)}, u32[]{:S(2)}) %all-to-all-start.2) | async-done | bytes 49184 | tf_op jit(solution)/shard_map/all_to_all | solution.py:280
  86.1 7.5 %all-to-all-start.3 = ((bf16[64,16,128]{2,1,0:T(8,128)(2,1)}), bf16[64,16,128]{2,1,0:T(8,128)(2,1)S(1)}, u32[]{:S(2)}, u32[]{:S(2)}) async-start(bf16[64,16,128]{2,1,0:T(8,128)(2,1)} %shard_map.219.refs_0_), calls=%async_computation.3 | async-start | bytes 524288 | tf_op jit(solution)/shard_map/all_to_all | solution.py:280
  93.5 4.4 %shard_map.220 = (bf16[4,256,128]{2,1,0:T(8,128)(2,1)}, f32[4,256,128]{2,1,0:T(8,128)}, bf16[128,128]{1,0:T(8,128)(2,1)}, bf16[128,128]{1,0:T(8,128)(2,1)}, f32[...) custom-call(s32[1]{0:T(128)} %bitcast.9.me, s32[2,1024]{1,0:T(2,128)} %bitcast.15, ...), custom_call_target="tpu_custom_call" | custom-call | flops 1000000000 | bytes 2000000 | tf_op jit(solution)/shard_map/pallas_call | solution.py:393
  97.9 7.2 %collective-permute-start.4 = (bf16[4,256,128]{2,1,0:T(8,128)(2,1)}, bf16[4,256,128]{2,1,0:T(8,128)(2,1)S(1)}, u32[]{:S(2)}, u32[]{:S(2)}) collective-permute-start(bf16[4,256,128]{2,1,0:T(8,128)(2,1)} %get-tuple-element.45), channel_id=1, source_target_pairs={{0,4},{1,5},{2,6},{3,7},{4,0},{5,1},{6,2},{7,3},{8,12},{9,13},{10,... | collective-permute-start | bytes 786440 | tf_op jit(solution)/shard_map/ppermute | solution.py:284
  105.1 8.1 %collective-permute-done.4.refs_2_ = bf16[4,256,128]{2,1,0:T(8,128)(2,1)S(1)} collective-permute-done((bf16[4,256,128]{2,1,0:T(8,128)(2,1)}, bf16[4,256,128]{2,1,0:T(8,128)(2,1)S(1)}, u32[]{:S(2)}, u32[]{:S(2)}) %collective-permute-start.4) | collective-permute-done | bytes 262176 | tf_op jit(solution)/shard_map/ppermute | solution.py:284
  114.0 1.9 %shard_map.221 = (f32[2,256,128]{2,1,0:T(8,128)}, bf16[2,256,128]{2,1,0:T(8,128)(2,1)}) custom-call(bf16[12,16,128]{2,1,0:T(8,128)(2,1)} %shard_map.218.refs_0_, f32[4,256,128]{2,1,0:T(8,128)} %get-tuple-element.44.refs_1_, bf16[4,256,128]{2,1,0:T(8,128)(2,1)} %copy-done.2), custom_call_target="tpu_custom_call" | custom-call | tf_op jit(solution)/shard_map/pallas_call | solution.py:290
  115.8 8.5 %collective-permute-start.5 = (bf16[2,256,128]{2,1,0:T(8,128)(2,1)}, bf16[2,256,128]{2,1,0:T(8,128)(2,1)S(1)}, u32[]{:S(2)}, u32[]{:S(2)}) collective-permute-start(bf16[2,256,128]{2,1,0:T(8,128)(2,1)} %get-tuple-element.47), channel_id=1, source_target_pairs={{0,2},{1,3},{2,0},{3,1},{4,6},{5,7},{6,4},{7,5},{8,10},{9,11},{10,... | collective-permute-start | bytes 393224 | tf_op jit(solution)/shard_map/ppermute | solution.py:284
  124.4 3.0 %collective-permute-start.2 = (bf16[128,128]{1,0:T(8,128)(2,1)S(1)}, bf16[128,128]{1,0:T(8,128)(2,1)S(1)}, u32[]{:S(2)}, u32[]{:S(2)}) collective-permute-start(bf16[128,128]{1,0:T(8,128)(2,1)S(1)} %copy-done.10), channel_id=1, source_target_pairs={{0,8},{8,16},{16,24},{24,32},{32,40},{40,48},{48,56},{56,64},{64,7... | collective-permute-start | bytes 98312 | tf_op jit(solution)/shard_map/ppermute | solution.py:408
  127.4 1.9 %collective-permute-start.3 = (bf16[128,128]{1,0:T(8,128)(2,1)S(1)}, bf16[128,128]{1,0:T(8,128)(2,1)S(1)}, u32[]{:S(2)}, u32[]{:S(2)}) collective-permute-start(bf16[128,128]{1,0:T(8,128)(2,1)S(1)} %copy-done.9), channel_id=1, source_target_pairs={{8,0},{16,8},{24,16},{32,24},{40,32},{48,40},{56,48},{64,56},{72,6... | collective-permute-start | bytes 98312 | tf_op jit(solution)/shard_map/ppermute | solution.py:409
  129.3 3.3 %collective-permute-done.3.refs_2_.from_upper = bf16[128,128]{1,0:T(8,128)(2,1)S(1)} collective-permute-done((bf16[128,128]{1,0:T(8,128)(2,1)S(1)}, bf16[128,128]{1,0:T(8,128)(2,1)S(1)}, u32[]{:S(2)}, u32[]{:S(2)}) %collective-permute-start.3) | collective-permute-done | bytes 32800 | tf_op jit(solution)/shard_map/ppermute | solution.py:409
  133.3 1.7 %shard_map.222 = (f32[1,256,128]{2,1,0:T(8,128)}, bf16[1,256,128]{2,1,0:T(8,128)(2,1)}) custom-call(bf16[64,16,128]{2,1,0:T(8,128)(2,1)} %shard_map.219.refs_0_, bf16[128,128]{1,0:T(8,128)(2,1)} %copy-done.5, bf16[128,128]{1,0:T(8,128)(2,1)} %copy-done.6, f32[2,256,128]{2,1,0:T(8,128)} %get-tuple-element.46.refs_3_, bf16[2,256,128]{2,1,0:T(8,128)(2,1)} %copy-done.7), custom_call_target="tpu_custom_call" | custom-call | tf_op jit(solution)/shard_map/pallas_call | solution.py:290
  134.9 1.9 %collective-permute-start.6 = (bf16[1,256,128]{2,1,0:T(8,128)(2,1)}, bf16[1,256,128]{2,1,0:T(8,128)(2,1)S(1)}, u32[]{:S(2)}, u32[]{:S(2)}) collective-permute-start(bf16[1,256,128]{2,1,0:T(8,128)(2,1)} %get-tuple-element.49), channel_id=1, source_target_pairs={{0,1},{1,0},{2,3},{3,2},{4,5},{5,4},{6,7},{7,6},{8,9},{9,8},{10,11... | collective-permute-start | bytes 196616 | tf_op jit(solution)/shard_map/ppermute | solution.py:284
  136.8 3.7 %collective-permute-done.6.arrived = bf16[1,256,128]{2,1,0:T(8,128)(2,1)S(1)} collective-permute-done((bf16[1,256,128]{2,1,0:T(8,128)(2,1)}, bf16[1,256,128]{2,1,0:T(8,128)(2,1)S(1)}, u32[]{:S(2)}, u32[]{:S(2)}) %collective-permute-start.6) | collective-permute-done | bytes 65568 | tf_op jit(solution)/shard_map/ppermute | solution.py:284
  141.1 2.1 %shard_map.223 = f32[256,128]{1,0:T(8,128)} custom-call(f32[1,256,128]{2,1,0:T(8,128)} %get-tuple-element.48.near, bf16[1,256,128]{2,1,0:T(8,128)(2,1)} %copy-done.8, bf16[128,128]{1,0:T(8,128)(2,1)} %copy-done.5, bf16[128,128]{1,0:T(8,128)(2,1)} %copy-done.6, f32[256,128]{1,0:T(8,128)} %get-tuple-element.50.own, f32[256,128]{1,0:T(8,128)} %get-tuple-element.51.target, ...), custom_call_target="tpu_custom_call" | custom-call | flops 100000000 | bytes 1000000 | tf_op jit(solution)/shard_map/pallas_call | solution.py:419
  143.9 1.7 %shard_map.224 = (f32[384,128]{1,0:T(8,128)}, f32[128,128]{1,0:T(8,128)}, f32[256,128]{1,0:T(8,128)}, f32[128,128]{1,0:T(8,128)}) custom-call(bf16[64,16,128]{2,1,0:T(8,128)(2,1)} %copy-done), custom_call_target="tpu_custom_call" | custom-call | tf_op jit(solution)/shard_map/pallas_call | solution.py:426
  (34 shorter events, 5.7 us)
Async XLA Ops:
  2.4 7.8 %copy-start.3 = (bf16[256,128]{1,0:T(8,128)(2,1)S(1)}, bf16[256,128]{1,0:T(8,128)(2,1)}, u32[]{:S(2)}) copy-start(bf16[256,128]{1,0:T(8,128)(2,1)} %refs_3_.3) | copy-start | bytes 196612
  2.4 21.5 %all-to-all-start = ((bf16[8,272,128]{2,1,0:T(8,128)(2,1)}), bf16[8,272,128]{2,1,0:T(8,128)(2,1)S(1)}, u32[]{:S(2)}, u32[]{:S(2)}) async-start(bf16[8,272,128]{2,1,0:T(8,128)(2,1)} %shard_map.215), calls=%async_computation | async-start | bytes 1114112 | tf_op jit(solution)/shard_map/all_to_all | solution.py:280
  10.2 13.6 %collective-permute-start = (bf16[128,128]{1,0:T(8,128)(2,1)S(1)}, bf16[128,128]{1,0:T(8,128)(2,1)S(1)}, u32[]{:S(2)}, u32[]{:S(2)}) collective-permute-start(bf16[128,128]{1,0:T(8,128)(2,1)S(1)} %get-tuple-element.59), channel_id=1, source_target_pairs={{0,8},{8,16},{16,24},{24,32},{32,40},{40,48},{48,56},{56,64},{64,7... | collective-permute-start | bytes 98312 | tf_op jit(solution)/shard_map/ppermute | solution.py:341
  15.0 8.8 %collective-permute-start.1 = (bf16[128,128]{1,0:T(8,128)(2,1)S(1)}, bf16[128,128]{1,0:T(8,128)(2,1)S(1)}, u32[]{:S(2)}, u32[]{:S(2)}) collective-permute-start(bf16[128,128]{1,0:T(8,128)(2,1)S(1)} %get-tuple-element.58), channel_id=1, source_target_pairs={{8,0},{16,8},{24,16},{32,24},{40,32},{48,40},{56,48},{64,56},{72,6... | collective-permute-start | bytes 98312 | tf_op jit(solution)/shard_map/ppermute | solution.py:342
  23.8 0.6 copy-start.11
  23.8 0.6 copy-start.12
  23.9 0.8 copy-start.1
  66.0 18.0 %all-to-all-start.2 = ((bf16[12,16,128]{2,1,0:T(8,128)(2,1)}), bf16[12,16,128]{2,1,0:T(8,128)(2,1)S(1)}, u32[]{:S(2)}, u32[]{:S(2)}) async-start(bf16[12,16,128]{2,1,0:T(8,128)(2,1)} %shard_map.218.refs_0_), calls=%async_computation.2 | async-start | bytes 98304 | tf_op jit(solution)/shard_map/all_to_all | solution.py:280
  83.9 0.6 copy-start.4
  86.1 57.2 %all-to-all-start.3 = ((bf16[64,16,128]{2,1,0:T(8,128)(2,1)}), bf16[64,16,128]{2,1,0:T(8,128)(2,1)S(1)}, u32[]{:S(2)}, u32[]{:S(2)}) async-start(bf16[64,16,128]{2,1,0:T(8,128)(2,1)} %shard_map.219.refs_0_), calls=%async_computation.3 | async-start | bytes 524288 | tf_op jit(solution)/shard_map/all_to_all | solution.py:280
  97.9 15.3 %collective-permute-start.4 = (bf16[4,256,128]{2,1,0:T(8,128)(2,1)}, bf16[4,256,128]{2,1,0:T(8,128)(2,1)S(1)}, u32[]{:S(2)}, u32[]{:S(2)}) collective-permute-start(bf16[4,256,128]{2,1,0:T(8,128)(2,1)} %get-tuple-element.45), channel_id=1, source_target_pairs={{0,4},{1,5},{2,6},{3,7},{4,0},{5,1},{6,2},{7,3},{8,12},{9,13},{10,... | collective-permute-start | bytes 786440 | tf_op jit(solution)/shard_map/ppermute | solution.py:284
  113.2 0.7 copy-start.2
  113.9 10.4 %copy-start.10 = (bf16[128,128]{1,0:T(8,128)(2,1)S(1)}, bf16[128,128]{1,0:T(8,128)(2,1)}, u32[]{:S(2)}) copy-start(bf16[128,128]{1,0:T(8,128)(2,1)} %get-tuple-element.42) | copy-start | bytes 98308
  113.9 13.4 %copy-start.9 = (bf16[128,128]{1,0:T(8,128)(2,1)S(1)}, bf16[128,128]{1,0:T(8,128)(2,1)}, u32[]{:S(2)}) copy-start(bf16[128,128]{1,0:T(8,128)(2,1)} %get-tuple-element.43) | copy-start | bytes 98308
  115.8 16.8 %collective-permute-start.5 = (bf16[2,256,128]{2,1,0:T(8,128)(2,1)}, bf16[2,256,128]{2,1,0:T(8,128)(2,1)S(1)}, u32[]{:S(2)}, u32[]{:S(2)}) collective-permute-start(bf16[2,256,128]{2,1,0:T(8,128)(2,1)} %get-tuple-element.47), channel_id=1, source_target_pairs={{0,2},{1,3},{2,0},{3,1},{4,6},{5,7},{6,4},{7,5},{8,10},{9,11},{10,... | collective-permute-start | bytes 393224 | tf_op jit(solution)/shard_map/ppermute | solution.py:284
  124.4 4.9 %collective-permute-start.2 = (bf16[128,128]{1,0:T(8,128)(2,1)S(1)}, bf16[128,128]{1,0:T(8,128)(2,1)S(1)}, u32[]{:S(2)}, u32[]{:S(2)}) collective-permute-start(bf16[128,128]{1,0:T(8,128)(2,1)S(1)} %copy-done.10), channel_id=1, source_target_pairs={{0,8},{8,16},{16,24},{24,32},{32,40},{40,48},{48,56},{56,64},{64,7... | collective-permute-start | bytes 98312 | tf_op jit(solution)/shard_map/ppermute | solution.py:408
  127.4 5.2 %collective-permute-start.3 = (bf16[128,128]{1,0:T(8,128)(2,1)S(1)}, bf16[128,128]{1,0:T(8,128)(2,1)S(1)}, u32[]{:S(2)}, u32[]{:S(2)}) collective-permute-start(bf16[128,128]{1,0:T(8,128)(2,1)S(1)} %copy-done.9), channel_id=1, source_target_pairs={{8,0},{16,8},{24,16},{32,24},{40,32},{48,40},{56,48},{64,56},{72,6... | collective-permute-start | bytes 98312 | tf_op jit(solution)/shard_map/ppermute | solution.py:409
  129.3 3.3 %copy-start.5 = (bf16[128,128]{1,0:T(8,128)(2,1)}, bf16[128,128]{1,0:T(8,128)(2,1)S(1)}, u32[]{:S(2)}) copy-start(bf16[128,128]{1,0:T(8,128)(2,1)S(1)} %collective-permute-done.2.refs_1_.from_lower) | copy-start | bytes 98308
  132.6 0.6 copy-start.6
  132.6 0.7 copy-start.7
  134.9 5.6 %collective-permute-start.6 = (bf16[1,256,128]{2,1,0:T(8,128)(2,1)}, bf16[1,256,128]{2,1,0:T(8,128)(2,1)S(1)}, u32[]{:S(2)}, u32[]{:S(2)}) collective-permute-start(bf16[1,256,128]{2,1,0:T(8,128)(2,1)} %get-tuple-element.49), channel_id=1, source_target_pairs={{0,1},{1,0},{2,3},{3,2},{4,5},{5,4},{6,7},{7,6},{8,9},{9,8},{10,11... | collective-permute-start | bytes 196616 | tf_op jit(solution)/shard_map/ppermute | solution.py:284
  140.5 0.6 copy-start.8
  143.2 0.7 copy-start

commit v3 on v2

--- a/solution.py
+++ b/solution.py
@@ -70,6 +70,10 @@
     if not isinstance(block, int):
         block = jnp.full(mark.shape, block.astype(F32)).astype(BF)
     return jnp.where(mark == block, 1.0, 0.0).astype(BF)
+
+
+def place_of(away):
+    return ((away & 1) << 2) | (away & 2) | (away >> 2)
 
 
 def pack_kernel(blocks, counts, nodes, out):
@@ -198,8 +202,9 @@
 
 
 def back_kernel(
-    me, eb, en, incoming, d_first, ecot, ew1,
+    me, eb, en, upper_half, incoming, d_first, ecot, ew1,
     far, near, to_lower, to_upper, own, target, edge_grad,
+    wide, places, *, half,
 ):
     rows = d_first.shape[0]
     d = d_first[...]
@@ -212,22 +217,36 @@
     owned = block
     for p in range(peers):
         for s in range(n_slots):
-            there = incoming[p, names + s : names + s + 1, 0:1].astype(F32) + float(rim_blocks + nblk * p)
+            there = incoming[p, names + s : names + s + 1, 0:1].astype(F32)
+            there = there + float(rim_blocks + nblk * p)
             owned = jnp.where(block == float(rim_blocks + n_slots * p + s), there, owned)
+    owned = jnp.where(owned >= half, owned - half, owned)
     smark = marks(node[0:1, :], owned, (BLOCK, rows), 0)
-
-    def part(b, count):
-        return dot(jnp.concatenate([one_hot(smark, b + k) for k in range(count)], axis=0), d)
-
+    high = d * upper_half[...]
+    wide[:, 0:W] = d - high
+    wide[:, W:] = high
+
+    def store(b, sums):
+        if b == 0:
+            to_lower[...] = sums.astype(BF)
+        elif b <= nblk:
+            own[(b - 1) * BLOCK : b * BLOCK, :] = sums
+        elif b == nblk + 1:
+            to_upper[...] = sums.astype(BF)
+        else:
+            q, j = divmod(b - rim_blocks, nblk)
+            places[place_of(q ^ me[0]), j * BLOCK : (j + 1) * BLOCK, :] = sums
+
+    for b in range(0, half, 2):
+        sums = dot(jnp.concatenate([one_hot(smark, b), one_hot(smark, b + 1)], axis=0), wide[...])
+        for k in range(2):
+            store(b + k, sums[k * BLOCK : (k + 1) * BLOCK, 0:W])
+            store(b + k + half, sums[k * BLOCK : (k + 1) * BLOCK, W:])
     for place in range(peers):
-        sums = part(rim_blocks + nblk * (me[0] ^ place), nblk)
         if place < peers // 2:
-            near[place] = sums
+            near[place] = places[place]
         else:
-            far[place - peers // 2] = sums.astype(BF)
-    to_lower[...] = part(0, 1).astype(BF)
-    to_upper[...] = part(nblk + 1, 1).astype(BF)
-    own[...] = part(1, nblk)
+            far[place - peers // 2] = places[place].astype(BF)
     tmark = marks(node[1:2, :], eb[1:2, :].astype(F32), (BLOCK, rows), 0)
     target[...] = dot(jnp.concatenate([one_hot(tmark, b) for b in range(nblk)], axis=0), d)
     edge_grad[...] = (ecot[...].astype(F32) + dot(d, ew1[2 * W :, :], NT)).astype(BF)
@@ -270,7 +289,7 @@
             at += 1
 
 
-def add_kernel(pieces, out):
+def add_kernel(after, pieces, out):
     total = jnp.sum(pieces[...].astype(F32), axis=0).astype(BF)
     for k in range(out.shape[0]):
         out[k] = total
@@ -282,6 +301,14 @@
 
 def swap(value, bit):
     return lax.ppermute(value, "y", [(i, i ^ bit) for i in range(lax.axis_size("y"))])
+
+
+def add(pieces, copies, after):
+    return call(
+        add_kernel,
+        arr((copies,) + pieces.shape[1:], BF),
+        in_specs=[pl.BlockSpec(memory_space=pl.ANY), VM],
+    )(after, pieces)
 
 
 def fold(after, near, arrived):
@@ -301,7 +328,7 @@
         in_specs=in_specs,
         out_specs=jax.tree.map(lambda o: pl.BlockSpec(memory_space=pltpu.VMEM), outs),
         scratch_shapes=scratch,
-        compiler_params=pltpu.CompilerParams(vmem_limit_bytes=60 << 20),
+        compiler_params=pltpu.CompilerParams(vmem_limit_bytes=24 << 20),
         cost_estimate=cost,
     )
 
@@ -391,7 +418,7 @@
 
     me = lax.axis_index("y").astype(jnp.int32)[None]
     far, near, to_lower, to_upper, own, target, edge_grad = call(
-        back_kernel,
+        lambda *refs: back_kernel(*refs, half=n_ext // BLOCK // 2),
         (
             arr((n_col // 2, own_rows, W), BF),
             arr((n_col // 2, own_rows, W), F32),
@@ -401,21 +428,22 @@
             arr((own_rows, W), F32),
             arr((edges, W), BF),
         ),
-        in_specs=[SMEM] + [VM] * 6,
+        scratch=[pltpu.VMEM((edges, 2 * W), BF), pltpu.VMEM((n_col, own_rows, W), F32)],
+        in_specs=[SMEM] + [VM] * 7,
         cost=pl.CostEstimate(flops=10**9, bytes_accessed=2000000, transcendentals=0),
-    )(me, eb, en, incoming, d_first, edge_cot, edge_w1)
-    far = swap(far, 4)
+    )(me, eb, en, upper_half, incoming, d_first, edge_cot, edge_w1)
+    far = swap(far, 1)
     from_lower = lax.ppermute(to_upper, ROW, up)
     from_upper = lax.ppermute(to_lower, ROW, down)
 
-    part = call(add_kernel, arr((spread, share, W), BF), in_specs=[VM])(pieces)
+    part = add(pieces, spread, far)
     pieces = exchange(part, SPREAD)
     near, far = fold((part,), near, far)
     far = swap(far, 2)
-    part = call(add_kernel, arr((members, share, W), BF), in_specs=[VM])(pieces)
+    part = add(pieces, members, far)
     weights = exchange(part, SCATTER)
-    near, far = fold((part, from_lower, from_upper), near, far)
-    far = swap(far, 1)
+    near, far = fold((part,), near, far)
+    far = swap(far, 4)
     node_grad = call(
         finish_kernel,
         arr((own_rows, W), F32),

time: 148 us -> 115 us (0.78); the launches traced: 146 us -> 115 us
  blocking collectives: 29.1 us -> 0 us
  starting transfers between devices: 55.6 us -> 73.9 us
  Pallas kernels: 31.2 us -> 17.3 us
  waiting for transfers between devices: 24.8 us -> 17.4 us
    all_to_all x1 -> x0, blocking collectives: 29.1 us -> none  [exchange(): return lax.all_to_all(value, axes, split_axis=0, concat_axis=0, tiled=True)]
    all_to_all x3 -> x4, starting transfers between devices: 23.5 us -> 43.8 us  [exchange(): return lax.all_to_all(value, axes, split_axis=0, concat_axis=0, tiled=True)]
    all_to_all x3 -> x4, waiting for transfers between devices: 9.69 us -> 0.01 us  [exchange(): return lax.all_to_all(value, axes, split_axis=0, concat_axis=0, tiled=True)]
    pallas_call x3, Pallas kernels: 7.54 us -> 3.48 us  [the longest x1 2.06 us: local(): call(lambda *refs: back_kernel(*refs, half=n_ext // BLOCK // 2), (arr((n_...]
    pallas_call x2, Pallas kernels: 3.55 us -> 0.08 us  [fold(): call(fold_kernel, (arr((count // 2, *rest), F32), arr((count // 2, *rest)...]
    ppermute x3, starting transfers between devices: 17.6 us -> 15 us  [swap(): lax.ppermute(value, 'y', [(i, i ^ bit) for i in range(lax.axis_size('y'))])]
    ppermute x3, waiting for transfers between devices: 11.8 us -> 14.1 us  [swap(): lax.ppermute(value, 'y', [(i, i ^ bit) for i in range(lax.axis_size('y'))])]
    pallas_call x1, Pallas kernels: 3.99 us -> 1.85 us  [local(): call(lambda *refs: early_kernel(*refs, half=n_ext // BLOCK // 2), (arr((e...]
  transfers between devices with their start and end apart: 10 -> 11, of which waited for: 4 -> 3; matrix products, arithmetic and copies ran while one was open for 0% -> 0% of each run, Pallas kernels for 10% -> 4%
where the time goes in v3:
time: 115 us
  starting transfers between devices  73.9 us (64%)
  waiting for transfers between devices  17.4 us (15%)
  Pallas kernels  17.3 us (15%)
  local copies, waits for them, and re-layouts  5.14 us (4%)
    all_to_all x4, starting transfers between devices, exchange(): return lax.all_to_all(value, axes, split_axis=0, concat_axis=0, tiled=True)  43.8 us
    ppermute x3, starting transfers between devices, swap(): lax.ppermute(value, 'y', [(i, i ^ bit) for i in range(lax.axis_size('y'))])  15 us
    ppermute x3, waiting for transfers between devices, swap(): lax.ppermute(value, 'y', [(i, i ^ bit) for i in range(lax.axis_size('y'))])  14.1 us
    pallas_call x1, Pallas kernels, local(): call(lambda *refs: main_kernel(*refs, edge_scale=edge_scale, node_scale=n...  8.72 us
    unnamed x42, local copies, waits for them, and re-layouts  5.13 us
    ppermute x1, starting transfers between devices, local(): lower = lax.ppermute(nodes[own_rows - BLOCK:], ROW, up)  4.97 us
    ppermute x1, starting transfers between devices, local(): upper = lax.ppermute(nodes[:BLOCK], ROW, down)  4.77 us
    ppermute x1, starting transfers between devices, local(): from_lower = lax.ppermute(to_upper, ROW, up)  3.47 us
  transfers between devices with their start and end apart: 11, of which 3 were waited for; matrix products, arithmetic and copies ran while one was open for 0% of the time, Pallas kernels for 4%

profile of v3, /device:TPU:1, one launch (start us, length us, event | category | flops | bytes accessed | tf_op | source)
XLA Modules:
  0.0 114.7 jit_solution(1584581427742223794)
XLA Ops:
  1.3 0.8 copy-done
  2.2 1.5 %shard_map.215 = bf16[8,272,128]{2,1,0:T(8,128)(2,1)} custom-call(s32[2,8]{1,0:T(2,128)S(1)} %bitcast.11, s32[1,8]{1,0:T(1,128)S(1)} %copy-done.4, bf16[256,128]{1,0:T(8,128)(2,1)S(1)} %copy-done), custom_call_target="tpu_custom_call" | custom-call | bytes 600000 | tf_op jit(solution)/shard_map/pallas_call | solution.py:361
  3.6 7.8 %all-to-all-start = ((bf16[8,272,128]{2,1,0:T(8,128)(2,1)}), bf16[8,272,128]{2,1,0:T(8,128)(2,1)S(1)}, u32[]{:S(2)}, u32[]{:S(2)}) async-start(bf16[8,272,128]{2,1,0:T(8,128)(2,1)} %shard_map.215), calls=%async_computation | async-start | bytes 1114112 | tf_op jit(solution)/shard_map/all_to_all | solution.py:299
  11.5 5.0 %collective-permute-start = (bf16[128,128]{1,0:T(8,128)(2,1)S(1)}, bf16[128,128]{1,0:T(8,128)(2,1)S(1)}, u32[]{:S(2)}, u32[]{:S(2)}) collective-permute-start(bf16[128,128]{1,0:T(8,128)(2,1)S(1)} %get-tuple-element.59), channel_id=1, source_target_pairs={{0,8},{8,16},{16,24},{24,32},{32,40},{40,48},{48,56},{56,64},{64,7... | collective-permute-start | bytes 98312 | tf_op jit(solution)/shard_map/ppermute | solution.py:368
  16.4 4.8 %collective-permute-start.1 = (bf16[128,128]{1,0:T(8,128)(2,1)S(1)}, bf16[128,128]{1,0:T(8,128)(2,1)S(1)}, u32[]{:S(2)}, u32[]{:S(2)}) collective-permute-start(bf16[128,128]{1,0:T(8,128)(2,1)S(1)} %get-tuple-element.58), channel_id=1, source_target_pairs={{8,0},{16,8},{24,16},{32,24},{40,32},{48,40},{56,48},{64,56},{72,6... | collective-permute-start | bytes 98312 | tf_op jit(solution)/shard_map/ppermute | solution.py:369
  21.9 1.9 %shard_map.216 = (bf16[1024,128]{1,0:T(8,128)(2,1)S(1)}, bf16[1024,128]{1,0:T(8,128)(2,1)S(1)}, bf16[1024,128]{1,0:T(8,128)(2,1)S(1)}, bf16[1024,256]{1,0:T(8,128)(2,1)S(1)}, f32[1024,128]{1,0:T(8,128)S(1)}) custom-call(bf16[256,128]{1,0:T(8,128)(2,1)S(1)} %copy-done.1, s32[2,1024]{1,0:T(2,128)S(1)} %bitcast.12, s32[2,1024]{1,0:T(2,128)S(1)} %bitcast.15, ...), custom_call_target="tpu_custom_call" | custom-call | flops 200000000 | bytes 8000000 | tf_op jit(solution)/shard_map/pallas_call | solution.py:372
  25.2 0.9 copy-done.18
  26.1 8.7 %shard_map.217 = (bf16[256,128]{1,0:T(8,128)(2,1)}, bf16[1024,128]{1,0:T(8,128)(2,1)}, bf16[1024,128]{1,0:T(8,128)(2,1)}, bf16[1024,128]{1,0:T(8,128)(2,1)S(1)}, f32[256,128]{1,0:T(8,128)S(1)}) custom-call(bf16[128,128]{1,0:T(8,128)(2,1)S(1)} %collective-permute-done.refs_0_, bf16[128,128]{1,0:T(8,128)(2,1)S(1)} %collective-permute-done.1.refs_1_, ...), custom_call_target="tpu_custom_call" | custom-call | flops 4000000000 | bytes 4000000 | tf_op jit(solution)/shard_map/pallas_call | solution.py:385
  34.8 0.7 copy-done.19
  35.6 17.1 %all-to-all-start.1 = ((bf16[64,16,128]{2,1,0:T(8,128)(2,1)}), bf16[64,16,128]{2,1,0:T(8,128)(2,1)S(1)}, u32[]{:S(2)}, u32[]{:S(2)}) async-start(bf16[64,16,128]{2,1,0:T(8,128)(2,1)} %bitcast.9), calls=%async_computation.1 | async-start | bytes 524288 | tf_op jit(solution)/shard_map/all_to_all | solution.py:299
  52.6 2.1 %shard_map.218 = (bf16[4,256,128]{2,1,0:T(8,128)(2,1)S(1)}, f32[4,256,128]{2,1,0:T(8,128)S(1)}, bf16[128,128]{1,0:T(8,128)(2,1)S(1)}, bf16[128,128]{1,0:T(8,128)...) custom-call(s32[1]{0:T(128)} %bitcast.8.refs_0_, s32[2,1024]{1,0:T(2,128)S(1)} %bitcast.14, ...), custom_call_target="tpu_custom_call" | custom-call | flops 1000000000 | bytes 2000000 | tf_op jit(solution)/shard_map/pallas_call | solution.py:420
  54.7 3.3 %collective-permute-start.2 = (bf16[4,256,128]{2,1,0:T(8,128)(2,1)S(1)}, bf16[4,256,128]{2,1,0:T(8,128)(2,1)S(1)}, u32[]{:S(2)}, u32[]{:S(2)}) collective-permute-start(bf16[4,256,128]{2,1,0:T(8,128)(2,1)S(1)} %get-tuple-element.41), channel_id=1, source_target_pairs={{0,1},{1,0},{2,3},{3,2},{4,5},{5,4},{6,7},{7,6},{8,9},{9,8},{10,11... | collective-permute-start | bytes 786440 | tf_op jit(solution)/shard_map/ppermute | solution.py:303
  58.0 7.9 %collective-permute-done.2.after.refs_2_ = bf16[4,256,128]{2,1,0:T(8,128)(2,1)S(1)} collective-permute-done((bf16[4,256,128]{2,1,0:T(8,128)(2,1)S(1)}, bf16[4,256,128]{2,1,0:T(8,128)(2,1)S(1)}, u32[]{:S(2)}, u32[]{:S(2)}) %collective-permute-start.2) | collective-permute-done | bytes 262176 | tf_op jit(solution)/shard_map/ppermute | solution.py:303
  66.6 8.9 %all-to-all-start.2 = ((bf16[12,16,128]{2,1,0:T(8,128)(2,1)}), bf16[12,16,128]{2,1,0:T(8,128)(2,1)S(1)}, u32[]{:S(2)}, u32[]{:S(2)}) async-start(bf16[12,16,128]{2,1,0:T(8,128)(2,1)} %shard_map.219.refs_0_), calls=%async_computation.2 | async-start | bytes 98304 | tf_op jit(solution)/shard_map/all_to_all | solution.py:299
  75.5 4.6 %collective-permute-start.3 = (bf16[2,256,128]{2,1,0:T(8,128)(2,1)S(1)}, bf16[2,256,128]{2,1,0:T(8,128)(2,1)S(1)}, u32[]{:S(2)}, u32[]{:S(2)}) collective-permute-start(bf16[2,256,128]{2,1,0:T(8,128)(2,1)S(1)} %get-tuple-element.44), channel_id=1, source_target_pairs={{0,2},{1,3},{2,0},{3,1},{4,6},{5,7},{6,4},{7,5},{8,10},{9,11},{10,... | collective-permute-start | bytes 393224 | tf_op jit(solution)/shard_map/ppermute | solution.py:303
  80.1 6.2 %collective-permute-done.3.after.refs_2_ = bf16[2,256,128]{2,1,0:T(8,128)(2,1)S(1)} collective-permute-done((bf16[2,256,128]{2,1,0:T(8,128)(2,1)S(1)}, bf16[2,256,128]{2,1,0:T(8,128)(2,1)S(1)}, u32[]{:S(2)}, u32[]{:S(2)}) %collective-permute-start.3) | collective-permute-done | bytes 131104 | tf_op jit(solution)/shard_map/ppermute | solution.py:303
  86.3 0.7 shard_map.221.refs_0_
  87.0 10.0 %all-to-all-start.3 = ((bf16[64,16,128]{2,1,0:T(8,128)(2,1)}), bf16[64,16,128]{2,1,0:T(8,128)(2,1)S(1)}, u32[]{:S(2)}, u32[]{:S(2)}) async-start(bf16[64,16,128]{2,1,0:T(8,128)(2,1)} %shard_map.221.refs_0_), calls=%async_computation.3 | async-start | bytes 524288 | tf_op jit(solution)/shard_map/all_to_all | solution.py:299
  97.1 7.2 %collective-permute-start.4 = (bf16[1,256,128]{2,1,0:T(8,128)(2,1)S(1)}, bf16[1,256,128]{2,1,0:T(8,128)(2,1)S(1)}, u32[]{:S(2)}, u32[]{:S(2)}) collective-permute-start(bf16[1,256,128]{2,1,0:T(8,128)(2,1)S(1)} %get-tuple-element.47), channel_id=1, source_target_pairs={{0,4},{1,5},{2,6},{3,7},{4,0},{5,1},{6,2},{7,3},{8,12},{9,13},{10,... | collective-permute-start | bytes 196616 | tf_op jit(solution)/shard_map/ppermute | solution.py:303
  104.3 3.5 %collective-permute-start.5 = (bf16[128,128]{1,0:T(8,128)(2,1)S(1)}, bf16[128,128]{1,0:T(8,128)(2,1)S(1)}, u32[]{:S(2)}, u32[]{:S(2)}) collective-permute-start(bf16[128,128]{1,0:T(8,128)(2,1)S(1)} %get-tuple-element.48), channel_id=1, source_target_pairs={{0,8},{8,16},{16,24},{24,32},{32,40},{40,48},{48,56},{56,64},{64,7... | collective-permute-start | bytes 98312 | tf_op jit(solution)/shard_map/ppermute | solution.py:436
  107.7 1.9 %collective-permute-start.6 = (bf16[128,128]{1,0:T(8,128)(2,1)S(1)}, bf16[128,128]{1,0:T(8,128)(2,1)S(1)}, u32[]{:S(2)}, u32[]{:S(2)}) collective-permute-start(bf16[128,128]{1,0:T(8,128)(2,1)S(1)} %get-tuple-element.49), channel_id=1, source_target_pairs={{8,0},{16,8},{24,16},{32,24},{40,32},{48,40},{56,48},{64,56},{72,6... | collective-permute-start | bytes 98312 | tf_op jit(solution)/shard_map/ppermute | solution.py:437
  109.7 3.3 %collective-permute-done.6.from_upper = bf16[128,128]{1,0:T(8,128)(2,1)S(1)} collective-permute-done((bf16[128,128]{1,0:T(8,128)(2,1)S(1)}, bf16[128,128]{1,0:T(8,128)(2,1)S(1)}, u32[]{:S(2)}, u32[]{:S(2)}) %collective-permute-start.6) | collective-permute-done | bytes 32800 | tf_op jit(solution)/shard_map/ppermute | solution.py:437
  113.0 0.9 shard_map.223
  113.9 0.8 shard_map.224
  (51 shorter events, 3.4 us)
Async XLA Ops:
  1.3 0.8 copy-start
  3.6 7.8 %copy-start.1 = (bf16[256,128]{1,0:T(8,128)(2,1)S(1)}, bf16[256,128]{1,0:T(8,128)(2,1)}, u32[]{:S(2)}) copy-start(bf16[256,128]{1,0:T(8,128)(2,1)} %refs_3_.3) | copy-start | bytes 196612
  3.6 17.6 %copy-start.5 = (bf16[1024,128]{1,0:T(8,128)(2,1)S(1)}, bf16[1024,128]{1,0:T(8,128)(2,1)}, u32[]{:S(2)}) copy-start(bf16[1024,128]{1,0:T(8,128)(2,1)} %refs_3_.2) | copy-start | bytes 786436
  3.6 20.9 %all-to-all-start = ((bf16[8,272,128]{2,1,0:T(8,128)(2,1)}), bf16[8,272,128]{2,1,0:T(8,128)(2,1)S(1)}, u32[]{:S(2)}, u32[]{:S(2)}) async-start(bf16[8,272,128]{2,1,0:T(8,128)(2,1)} %shard_map.215), calls=%async_computation | async-start | bytes 1114112 | tf_op jit(solution)/shard_map/all_to_all | solution.py:299
  11.4 9.8 %copy-start.2 = (bf16[384,128]{1,0:T(8,128)(2,1)S(1)}, bf16[384,128]{1,0:T(8,128)(2,1)}, u32[]{:S(2)}) copy-start(bf16[384,128]{1,0:T(8,128)(2,1)} %ew1.1) | copy-start | bytes 294916
  11.4 9.8 %copy-start.12 = (s32[1024,2]{0,1:T(2,128)S(1)}, s32[1024,2]{0,1:T(2,128)}, u32[]{:S(2)}) copy-start(s32[1024,2]{0,1:T(2,128)} %param.19) | copy-start | bytes 24580
  11.4 9.8 %copy-start.11 = (s32[1024,2]{0,1:T(2,128)S(1)}, s32[1024,2]{0,1:T(2,128)}, u32[]{:S(2)}) copy-start(s32[1024,2]{0,1:T(2,128)} %param.18) | copy-start | bytes 24580
  11.5 13.0 %collective-permute-start = (bf16[128,128]{1,0:T(8,128)(2,1)S(1)}, bf16[128,128]{1,0:T(8,128)(2,1)S(1)}, u32[]{:S(2)}, u32[]{:S(2)}) collective-permute-start(bf16[128,128]{1,0:T(8,128)(2,1)S(1)} %get-tuple-element.59), channel_id=1, source_target_pairs={{0,8},{8,16},{16,24},{24,32},{32,40},{40,48},{48,56},{56,64},{64,7... | collective-permute-start | bytes 98312 | tf_op jit(solution)/shard_map/ppermute | solution.py:368
  16.4 8.0 %collective-permute-start.1 = (bf16[128,128]{1,0:T(8,128)(2,1)S(1)}, bf16[128,128]{1,0:T(8,128)(2,1)S(1)}, u32[]{:S(2)}, u32[]{:S(2)}) collective-permute-start(bf16[128,128]{1,0:T(8,128)(2,1)S(1)} %get-tuple-element.58), channel_id=1, source_target_pairs={{8,0},{16,8},{24,16},{32,24},{40,32},{48,40},{56,48},{64,56},{72,6... | collective-permute-start | bytes 98312 | tf_op jit(solution)/shard_map/ppermute | solution.py:369
  21.9 2.6 %copy-start.6 = (bf16[1024,128]{1,0:T(8,128)(2,1)S(1)}, bf16[1024,128]{1,0:T(8,128)(2,1)}, u32[]{:S(2)}) copy-start(bf16[1024,128]{1,0:T(8,128)(2,1)} %refs_6_.1) | copy-start | bytes 786436
  21.9 2.6 %copy-start.7 = (bf16[256,128]{1,0:T(8,128)(2,1)S(1)}, bf16[256,128]{1,0:T(8,128)(2,1)}, u32[]{:S(2)}) copy-start(bf16[256,128]{1,0:T(8,128)(2,1)} %refs_12_.1) | copy-start | bytes 196612
  21.9 2.7 %copy-start.8 = (bf16[256,128]{1,0:T(8,128)(2,1)S(1)}, bf16[256,128]{1,0:T(8,128)(2,1)}, u32[]{:S(2)}) copy-start(bf16[256,128]{1,0:T(8,128)(2,1)} %refs_16_.1) | copy-start | bytes 196612
  21.9 2.7 %copy-start.9 = (bf16[128,128]{1,0:T(8,128)(2,1)S(1)}, bf16[128,128]{1,0:T(8,128)(2,1)}, u32[]{:S(2)}) copy-start(bf16[128,128]{1,0:T(8,128)(2,1)} %refs_14_.1) | copy-start | bytes 98308
  21.9 2.7 %copy-start.10 = (bf16[128,128]{1,0:T(8,128)(2,1)S(1)}, bf16[128,128]{1,0:T(8,128)(2,1)}, u32[]{:S(2)}) copy-start(bf16[128,128]{1,0:T(8,128)(2,1)} %refs_18_.1) | copy-start | bytes 98308
  25.2 0.9 copy-start.18
  35.5 17.1 %copy-start.20 = (bf16[1024,128]{1,0:T(8,128)(2,1)S(1)}, bf16[1024,128]{1,0:T(8,128)(2,1)}, u32[]{:S(2)}) copy-start(bf16[1024,128]{1,0:T(8,128)(2,1)} %copy-done.19) | copy-start | bytes 786436
  35.6 30.3 %all-to-all-start.1 = ((bf16[64,16,128]{2,1,0:T(8,128)(2,1)}), bf16[64,16,128]{2,1,0:T(8,128)(2,1)S(1)}, u32[]{:S(2)}, u32[]{:S(2)}) async-start(bf16[64,16,128]{2,1,0:T(8,128)(2,1)} %bitcast.9), calls=%async_computation.1 | async-start | bytes 524288 | tf_op jit(solution)/shard_map/all_to_all | solution.py:299
  54.7 11.1 %collective-permute-start.2 = (bf16[4,256,128]{2,1,0:T(8,128)(2,1)S(1)}, bf16[4,256,128]{2,1,0:T(8,128)(2,1)S(1)}, u32[]{:S(2)}, u32[]{:S(2)}) collective-permute-start(bf16[4,256,128]{2,1,0:T(8,128)(2,1)S(1)} %get-tuple-element.41), channel_id=1, source_target_pairs={{0,1},{1,0},{2,3},{3,2},{4,5},{5,4},{6,7},{7,6},{8,9},{9,8},{10,11... | collective-permute-start | bytes 786440 | tf_op jit(solution)/shard_map/ppermute | solution.py:303
  66.6 19.7 %all-to-all-start.2 = ((bf16[12,16,128]{2,1,0:T(8,128)(2,1)}), bf16[12,16,128]{2,1,0:T(8,128)(2,1)S(1)}, u32[]{:S(2)}, u32[]{:S(2)}) async-start(bf16[12,16,128]{2,1,0:T(8,128)(2,1)} %shard_map.219.refs_0_), calls=%async_computation.2 | async-start | bytes 98304 | tf_op jit(solution)/shard_map/all_to_all | solution.py:299
  75.5 10.8 %collective-permute-start.3 = (bf16[2,256,128]{2,1,0:T(8,128)(2,1)S(1)}, bf16[2,256,128]{2,1,0:T(8,128)(2,1)S(1)}, u32[]{:S(2)}, u32[]{:S(2)}) collective-permute-start(bf16[2,256,128]{2,1,0:T(8,128)(2,1)S(1)} %get-tuple-element.44), channel_id=1, source_target_pairs={{0,2},{1,3},{2,0},{3,1},{4,6},{5,7},{6,4},{7,5},{8,10},{9,11},{10,... | collective-permute-start | bytes 393224 | tf_op jit(solution)/shard_map/ppermute | solution.py:303
  87.0 26.9 %all-to-all-start.3 = ((bf16[64,16,128]{2,1,0:T(8,128)(2,1)}), bf16[64,16,128]{2,1,0:T(8,128)(2,1)S(1)}, u32[]{:S(2)}, u32[]{:S(2)}) async-start(bf16[64,16,128]{2,1,0:T(8,128)(2,1)} %shard_map.221.refs_0_), calls=%async_computation.3 | async-start | bytes 524288 | tf_op jit(solution)/shard_map/all_to_all | solution.py:299
  97.1 15.9 %collective-permute-start.4 = (bf16[1,256,128]{2,1,0:T(8,128)(2,1)S(1)}, bf16[1,256,128]{2,1,0:T(8,128)(2,1)S(1)}, u32[]{:S(2)}, u32[]{:S(2)}) collective-permute-start(bf16[1,256,128]{2,1,0:T(8,128)(2,1)S(1)} %get-tuple-element.47), channel_id=1, source_target_pairs={{0,4},{1,5},{2,6},{3,7},{4,0},{5,1},{6,2},{7,3},{8,12},{9,13},{10,... | collective-permute-start | bytes 196616 | tf_op jit(solution)/shard_map/ppermute | solution.py:303
  104.3 5.4 %collective-permute-start.5 = (bf16[128,128]{1,0:T(8,128)(2,1)S(1)}, bf16[128,128]{1,0:T(8,128)(2,1)S(1)}, u32[]{:S(2)}, u32[]{:S(2)}) collective-permute-start(bf16[128,128]{1,0:T(8,128)(2,1)S(1)} %get-tuple-element.48), channel_id=1, source_target_pairs={{0,8},{8,16},{16,24},{24,32},{32,40},{40,48},{48,56},{56,64},{64,7... | collective-permute-start | bytes 98312 | tf_op jit(solution)/shard_map/ppermute | solution.py:436
  107.7 5.2 %collective-permute-start.6 = (bf16[128,128]{1,0:T(8,128)(2,1)S(1)}, bf16[128,128]{1,0:T(8,128)(2,1)S(1)}, u32[]{:S(2)}, u32[]{:S(2)}) collective-permute-start(bf16[128,128]{1,0:T(8,128)(2,1)S(1)} %get-tuple-element.49), channel_id=1, source_target_pairs={{8,0},{16,8},{24,16},{32,24},{40,32},{48,40},{56,48},{64,56},{72,6... | collective-permute-start | bytes 98312 | tf_op jit(solution)/shard_map/ppermute | solution.py:437
  (8 other events, 5.4 us)

commit v4 on v3

--- a/solution.py
+++ b/solution.py
@@ -16,8 +16,9 @@
 ROW = ("x", "z", "c")
 SCATTER = ("x", "c", "y")
 SPREAD = "z"
-CHUNK = 256
+CHUNK = 1024
 WROWS = 1024
+UPPER = 4.0
 LABEL = 16
 
 
@@ -90,7 +91,7 @@
         out[p, pair:, :] = label.astype(BF)
 
 
-def early_kernel(nodes, eb, en, feats, ew1, eb1, smark, upper_half, tmark, joined, partial, cols, *, half):
+def early_kernel(nodes, eb, en, feats, ew1, vectors, smark, tmark, joined, partial, cols, *, half):
     rows = feats.shape[0]
     nblk = nodes.shape[0] // BLOCK
     index = jnp.concatenate([eb[...], en[...], eb[...], en[...]], axis=0).astype(F32)
@@ -102,25 +103,25 @@
         block = col[:, 0:1]
         high = block >= half
         smark[at, :] = marks(col[:, 2:3], jnp.where(high, block - half, block), (CHUNK, BLOCK), 1)
-        upper_half[at, :] = jnp.broadcast_to(jnp.where(high, 1.0, 0.0), (CHUNK, W)).astype(BF)
         tm = marks(col[:, 3:4], col[:, 1:2], (CHUNK, BLOCK), 1)
-        tmark[at, :] = tm
+        tmark[at, :] = (tm.astype(F32) + jnp.where(high, UPPER, 0.0)).astype(BF)
         hot_t = jnp.concatenate([one_hot(tm, b) for b in range(nblk)], axis=1)
         joined[at, 0:W] = dot(hot_t, nodes[...]).astype(BF)
         joined[at, W : 2 * W] = feats[at, :]
-        partial[at, :] = dot(joined[at, :], ew1[W:, :]) + eb1[...]
+        partial[at, :] = dot(joined[at, :], ew1[W:, :]) + vectors[0:1, :]
         return carry
 
     lax.fori_loop(0, rows // CHUNK, step, 0)
 
 
 def main_kernel(
-    lower, upper, incoming, nodes, eb, en, smark, upper_half, tmark, joined, partial, ecot, ncot,
-    ew1, ew2, egain, nw1, nb1, nw2, ngain,
-    node_new, edge_new, wsum, d_first_out, base,
+    lower, upper, incoming, nodes, eb, en, smark, tmark, joined, partial, ecot, ncot,
+    ew1, ew2, nw1, nw2, vectors,
+    node_new, edge_new, wsum, wide, base,
     ext, gathered, active, unit, slope, scales, summed, dsum, g1, g2,
     *, edge_scale, node_scale,
 ):
+    egain, nb1, ngain = vectors.at[1:2], vectors.at[2:3], vectors.at[3:4]
     rows = joined.shape[0]
     nblk = nodes.shape[0] // BLOCK
     half = ext.shape[0] // BLOCK
@@ -141,8 +142,12 @@
     g1[...] = jnp.zeros_like(g1)
     g2[...] = jnp.zeros_like(g2)
 
+    def is_upper(at):
+        return tmark[at, :].astype(F32) > UPPER - 2.0
+
     def target_hot(at):
-        tm = tmark[at, :]
+        tm = tmark[at, :].astype(F32)
+        tm = jnp.where(tm > UPPER - 2.0, tm - UPPER, tm).astype(BF)
         return jnp.concatenate([one_hot(tm, b) for b in range(nblk)], axis=1)
 
     def forward(i, carry):
@@ -150,7 +155,7 @@
         sm = smark[at, :]
         hot = jnp.concatenate([one_hot(sm, b) for b in range(half)], axis=1)
         both = dot(hot, ext[...])
-        source = jnp.where(upper_half[at, :].astype(F32) > 0.5, both[:, W:], both[:, 0:W]).astype(BF)
+        source = jnp.where(is_upper(at), both[:, W:], both[:, 0:W]).astype(BF)
         gathered[at, :] = source
         act, slp = silu_parts(partial[at, :] + dot(source, ew1[0:W, :]))
         active[at, :] = act
@@ -190,7 +195,9 @@
         d_second = norm_back(d_message * egain[...], unit[at, :], scales[at, :]).astype(BF)
         g2[...] += dot(d_second, active[at, :], TN)
         d_first = (dot(d_second, ew2[...], NT) * slope[at, :]).astype(BF)
-        d_first_out[at, :] = d_first
+        high = jnp.where(is_upper(at), d_first.astype(F32), 0.0).astype(BF)
+        wide[at, 0:W] = d_first - high
+        wide[at, W:] = high
         sources = jnp.concatenate([gathered[at, :], joined[at, :]], axis=1)
         g1[...] += dot(d_first, sources, TN)
         return carry
@@ -202,12 +209,12 @@
 
 
 def back_kernel(
-    me, eb, en, upper_half, incoming, d_first, ecot, ew1,
+    me, eb, en, incoming, wide, ecot, ew1,
     far, near, to_lower, to_upper, own, target, edge_grad,
-    wide, places, *, half,
+    places, *, half,
 ):
-    rows = d_first.shape[0]
-    d = d_first[...]
+    rows = wide.shape[0]
+    d = wide[:, 0:W] + wide[:, W:]
     nblk = own.shape[0] // BLOCK
     peers, n_slots = incoming.shape[0], incoming.shape[1] // BLOCK
     names = n_slots * BLOCK
@@ -222,9 +229,6 @@
             owned = jnp.where(block == float(rim_blocks + n_slots * p + s), there, owned)
     owned = jnp.where(owned >= half, owned - half, owned)
     smark = marks(node[0:1, :], owned, (BLOCK, rows), 0)
-    high = d * upper_half[...]
-    wide[:, 0:W] = d - high
-    wide[:, W:] = high
 
     def store(b, sums):
         if b == 0:
@@ -289,7 +293,8 @@
             at += 1
 
 
-def add_kernel(after, pieces, out):
+def add_kernel(*refs):
+    pieces, out = refs[-2:]
     total = jnp.sum(pieces[...].astype(F32), axis=0).astype(BF)
     for k in range(out.shape[0]):
         out[k] = total
@@ -307,8 +312,8 @@
     return call(
         add_kernel,
         arr((copies,) + pieces.shape[1:], BF),
-        in_specs=[pl.BlockSpec(memory_space=pl.ANY), VM],
-    )(after, pieces)
+        in_specs=[pl.BlockSpec(memory_space=pl.ANY)] * len(after) + [VM],
+    )(*after, pieces)
 
 
 def fold(after, near, arrived):
@@ -321,14 +326,14 @@
     )(*after, near, arrived)
 
 
-def call(kernel, outs, scratch=(), in_specs=None, cost=None):
+def call(kernel, outs, scratch=(), in_specs=None, cost=None, grant=24):
     return pl.pallas_call(
         kernel,
         out_shape=outs,
         in_specs=in_specs,
         out_specs=jax.tree.map(lambda o: pl.BlockSpec(memory_space=pltpu.VMEM), outs),
         scratch_shapes=scratch,
-        compiler_params=pltpu.CompilerParams(vmem_limit_bytes=24 << 20),
+        compiler_params=pltpu.CompilerParams(vmem_limit_bytes=grant << 20),
         cost_estimate=cost,
     )
 
@@ -362,6 +367,7 @@
         pack_kernel,
         arr((n_col, slots * BLOCK + LABEL, W), BF),
         in_specs=[SMEM, SMEM, VM],
+        grant=60,
         cost=pl.CostEstimate(flops=0, bytes_accessed=600000, transcendentals=0),
     )(blocks, send_counts, nodes)
     incoming = exchange(outgoing, "y")
@@ -369,10 +375,10 @@
     upper = lax.ppermute(nodes[:BLOCK], ROW, down)
 
     n_ext = own_rows + 2 * BLOCK + n_col * slots * BLOCK
-    smark, upper_half, tmark, joined, partial = call(
+    vectors = jnp.stack([edge_b1, edge_gain, node_b1, node_gain])
+    smark, tmark, joined, partial = call(
         lambda *refs: early_kernel(*refs, half=n_ext // BLOCK // 2),
         (
-            arr((edges, W), BF),
             arr((edges, W), BF),
             arr((edges, W), BF),
             arr((edges, 2 * W), BF),
@@ -381,14 +387,14 @@
         scratch=[pltpu.VMEM((edges, 8), F32)],
         in_specs=[VM] * 6,
         cost=pl.CostEstimate(flops=2 * 10**8, bytes_accessed=8000000, transcendentals=0),
-    )(nodes, eb, en, edge_feats, edge_w1, edge_b1[None])
-    node_new, edge_new, wsum, d_first, base = call(
+    )(nodes, eb, en, edge_feats, edge_w1, vectors)
+    node_new, edge_new, wsum, wide, base = call(
         lambda *refs: main_kernel(*refs, edge_scale=edge_scale, node_scale=node_scale),
         (
             arr((own_rows, W), BF),
             arr((edges, W), BF),
             arr((WROWS, W), BF),
-            arr((edges, W), BF),
+            arr((edges, 2 * W), BF),
             arr((own_rows, W), F32),
         ),
         scratch=[
@@ -403,12 +409,12 @@
             pltpu.VMEM((W, 3 * W), F32),
             pltpu.VMEM((W, W), F32),
         ],
-        in_specs=[VM] * 20,
+        in_specs=[VM] * 17,
         cost=pl.CostEstimate(flops=4 * 10**9, bytes_accessed=4000000, transcendentals=200000),
     )(
-        lower, upper, incoming, nodes, eb, en, smark, upper_half, tmark,
+        lower, upper, incoming, nodes, eb, en, smark, tmark,
         joined, partial, edge_cot, node_cot,
-        edge_w1, edge_w2, edge_gain[None], node_w1, node_b1[None], node_w2, node_gain[None],
+        edge_w1, edge_w2, node_w1, node_w2, vectors,
     )
 
     members = lax.axis_size(SCATTER)
@@ -428,19 +434,19 @@
             arr((own_rows, W), F32),
             arr((edges, W), BF),
         ),
-        scratch=[pltpu.VMEM((edges, 2 * W), BF), pltpu.VMEM((n_col, own_rows, W), F32)],
-        in_specs=[SMEM] + [VM] * 7,
+        scratch=[pltpu.VMEM((n_col, own_rows, W), F32)],
+        in_specs=[SMEM] + [VM] * 6,
         cost=pl.CostEstimate(flops=10**9, bytes_accessed=2000000, transcendentals=0),
-    )(me, eb, en, upper_half, incoming, d_first, edge_cot, edge_w1)
+    )(me, eb, en, incoming, wide, edge_cot, edge_w1)
     far = swap(far, 1)
     from_lower = lax.ppermute(to_upper, ROW, up)
     from_upper = lax.ppermute(to_lower, ROW, down)
 
-    part = add(pieces, spread, far)
+    part = add(pieces, spread, (far, from_lower, from_upper))
     pieces = exchange(part, SPREAD)
     near, far = fold((part,), near, far)
     far = swap(far, 2)
-    part = add(pieces, members, far)
+    part = add(pieces, members, (far,))
     weights = exchange(part, SCATTER)
     near, far = fold((part,), near, far)
     far = swap(far, 4)

time: 115 us -> 109 us (0.948)
  local copies, waits for them, and re-layouts: 5.14 us -> 0.88 us
  Pallas kernels: 17.3 us -> 13.7 us
    unnamed x42 -> x32, local copies, waits for them, and re-layouts: 5.13 us -> 0.88 us
    pallas_call x1, Pallas kernels: 8.72 us -> 5.48 us  [local(): call(lambda *refs: main_kernel(*refs, edge_scale=edge_scale, node_scale=n...]
    all_to_all x4, starting transfers between devices: 43.8 us -> 45.4 us  [exchange(): return lax.all_to_all(value, axes, split_axis=0, concat_axis=0, tiled=True)]
    ppermute x1, starting transfers between devices: 3.47 us -> 1.92 us  [local(): from_lower = lax.ppermute(to_upper, ROW, up)]
    all_to_all x4, waiting for transfers between devices: 0.01 us -> 1.32 us  [exchange(): return lax.all_to_all(value, axes, split_axis=0, concat_axis=0, tiled=True)]
  transfers between devices with their start and end apart: 11 -> 11, of which waited for: 3 -> 5; matrix products, arithmetic and copies ran while one was open for 0% -> 0% of each run, Pallas kernels for 4% -> 4%
where the time goes in v4:
time: 109 us; the launch traced here: 108 us
  starting transfers between devices  73.9 us (68%)
  waiting for transfers between devices  18.4 us (17%)
  Pallas kernels  13.7 us (13%)
    all_to_all x4, starting transfers between devices, exchange(): return lax.all_to_all(value, axes, split_axis=0, concat_axis=0, tiled=True)  45.4 us
    ppermute x3, starting transfers between devices, swap(): lax.ppermute(value, 'y', [(i, i ^ bit) for i in range(lax.axis_size('y'))])  14.5 us
    ppermute x3, waiting for transfers between devices, swap(): lax.ppermute(value, 'y', [(i, i ^ bit) for i in range(lax.axis_size('y'))])  13.9 us
    pallas_call x1, Pallas kernels, local(): call(lambda *refs: main_kernel(*refs, edge_scale=edge_scale, node_scale=n...  5.48 us
    ppermute x1, starting transfers between devices, local(): lower = lax.ppermute(nodes[own_rows - BLOCK:], ROW, up)  4.97 us
    ppermute x1, starting transfers between devices, local(): upper = lax.ppermute(nodes[:BLOCK], ROW, down)  4.77 us
    ppermute x1, waiting for transfers between devices, local(): from_upper = lax.ppermute(to_lower, ROW, down)  3.11 us
    ppermute x1, starting transfers between devices, local(): from_upper = lax.ppermute(to_lower, ROW, down)  2.4 us
  transfers between devices with their start and end apart: 11, of which 5 were waited for; matrix products, arithmetic and copies ran while one was open for 0% of the time, Pallas kernels for 4%

profile of v4, /device:TPU:1, one launch (start us, length us, event | category | flops | bytes accessed | tf_op | source)
XLA Modules:
  0.0 107.9 jit_solution(5114538920787093712)
XLA Ops:
  0.6 1.8 %shard_map.215 = bf16[8,272,128]{2,1,0:T(8,128)(2,1)} custom-call(s32[2,8]{1,0:T(2,128)} %bitcast.17, s32[1,8]{1,0:T(1,128)} %counts.1, bf16[256,128]{1,0:T(8,128)(2,1)} %refs_3_.3), custom_call_target="tpu_custom_call" | custom-call | bytes 600000 | tf_op jit(solution)/shard_map/pallas_call | solution.py:366
  2.4 7.8 %all-to-all-start = ((bf16[8,272,128]{2,1,0:T(8,128)(2,1)}), bf16[8,272,128]{2,1,0:T(8,128)(2,1)S(1)}, u32[]{:S(2)}, u32[]{:S(2)}) async-start(bf16[8,272,128]{2,1,0:T(8,128)(2,1)} %shard_map.215), calls=%async_computation | async-start | bytes 1114112 | tf_op jit(solution)/shard_map/all_to_all | solution.py:304
  10.3 5.0 %collective-permute-start = (bf16[128,128]{1,0:T(8,128)(2,1)S(1)}, bf16[128,128]{1,0:T(8,128)(2,1)S(1)}, u32[]{:S(2)}, u32[]{:S(2)}) collective-permute-start(bf16[128,128]{1,0:T(8,128)(2,1)S(1)} %get-tuple-element.57), channel_id=1, source_target_pairs={{0,8},{8,16},{16,24},{24,32},{32,40},{40,48},{48,56},{56,64},{64,7... | collective-permute-start | bytes 98312 | tf_op jit(solution)/shard_map/ppermute | solution.py:374
  15.3 4.8 %collective-permute-start.1 = (bf16[128,128]{1,0:T(8,128)(2,1)S(1)}, bf16[128,128]{1,0:T(8,128)(2,1)S(1)}, u32[]{:S(2)}, u32[]{:S(2)}) collective-permute-start(bf16[128,128]{1,0:T(8,128)(2,1)S(1)} %get-tuple-element.56), channel_id=1, source_target_pairs={{8,0},{16,8},{24,16},{32,24},{40,32},{48,40},{56,48},{64,56},{72,6... | collective-permute-start | bytes 98312 | tf_op jit(solution)/shard_map/ppermute | solution.py:375
  20.2 1.3 %shard_map.216 = (bf16[1024,128]{1,0:T(8,128)(2,1)S(1)}, bf16[1024,128]{1,0:T(8,128)(2,1)S(1)}, bf16[1024,256]{1,0:T(8,128)(2,1)S(1)}, f32[1024,128]{1,0:T(8,128)S(1)}) custom-call(bf16[256,128]{1,0:T(8,128)(2,1)S(1)} %copy-done, s32[2,1024]{1,0:T(2,128)S(1)} %bitcast.11, s32[2,1024]{1,0:T(2,128)S(1)} %bitcast.14, bf16[1024,128]{1,0:T(8,128)(2,1)S(1)} %copy-done.2, ...), custom_call_target="tpu_custom_call" | custom-call | flops 200000000 | bytes 8000000 | tf_op jit(solution)/shard_map/pallas_call | solution.py:379
  21.5 1.3 %all-to-all-done.refs_2_.refs_3_ = bf16[8,272,128]{2,1,0:T(8,128)(2,1)S(1)} async-done(((bf16[8,272,128]{2,1,0:T(8,128)(2,1)}), bf16[8,272,128]{2,1,0:T(8,128)(2,1)S(1)}, u32[]{:S(2)}, u32[]{:S(2)}) %all-to-all-start) | async-done | bytes 557088 | tf_op jit(solution)/shard_map/all_to_all | solution.py:304
  22.9 5.5 %shard_map.217 = (bf16[256,128]{1,0:T(8,128)(2,1)}, bf16[1024,128]{1,0:T(8,128)(2,1)}, bf16[1024,128]{1,0:T(8,128)(2,1)}, bf16[1024,256]{1,0:T(8,128)(2,1)S(1)}, f32[256,128]{1,0:T(8,128)S(1)}) custom-call(bf16[128,128]{1,0:T(8,128)(2,1)S(1)} %collective-permute-done.refs_0_, bf16[128,128]{1,0:T(8,128)(2,1)S(1)} %collective-permute-done.1.refs_1_, ...), custom_call_target="tpu_custom_call" | custom-call | flops 4000000000 | bytes 4000000 | tf_op jit(solution)/shard_map/pallas_call | solution.py:391
  28.3 0.8 copy-done.10
  29.1 15.9 %all-to-all-start.1 = ((bf16[64,16,128]{2,1,0:T(8,128)(2,1)}), bf16[64,16,128]{2,1,0:T(8,128)(2,1)S(1)}, u32[]{:S(2)}, u32[]{:S(2)}) async-start(bf16[64,16,128]{2,1,0:T(8,128)(2,1)} %bitcast.9), calls=%async_computation.1 | async-start | bytes 524288 | tf_op jit(solution)/shard_map/all_to_all | solution.py:304
  45.0 2.0 %shard_map.218 = (bf16[4,256,128]{2,1,0:T(8,128)(2,1)S(1)}, f32[4,256,128]{2,1,0:T(8,128)S(1)}, bf16[128,128]{1,0:T(8,128)(2,1)S(1)}, bf16[128,128]{1,0:T(8,128)...) custom-call(s32[1]{0:T(128)} %bitcast.8.refs_0_, s32[2,1024]{1,0:T(2,128)S(1)} %bitcast.13, ...), custom_call_target="tpu_custom_call" | custom-call | flops 1000000000 | bytes 2000000 | tf_op jit(solution)/shard_map/pallas_call | solution.py:426
  47.0 3.3 %collective-permute-start.2 = (bf16[4,256,128]{2,1,0:T(8,128)(2,1)S(1)}, bf16[4,256,128]{2,1,0:T(8,128)(2,1)S(1)}, u32[]{:S(2)}, u32[]{:S(2)}) collective-permute-start(bf16[4,256,128]{2,1,0:T(8,128)(2,1)S(1)} %get-tuple-element.39), channel_id=1, source_target_pairs={{0,1},{1,0},{2,3},{3,2},{4,5},{5,4},{6,7},{7,6},{8,9},{9,8},{10,11... | collective-permute-start | bytes 786440 | tf_op jit(solution)/shard_map/ppermute | solution.py:308
  50.3 1.9 %collective-permute-start.3 = (bf16[128,128]{1,0:T(8,128)(2,1)S(1)}, bf16[128,128]{1,0:T(8,128)(2,1)S(1)}, u32[]{:S(2)}, u32[]{:S(2)}) collective-permute-start(bf16[128,128]{1,0:T(8,128)(2,1)S(1)} %get-tuple-element.40), channel_id=1, source_target_pairs={{0,8},{8,16},{16,24},{24,32},{32,40},{40,48},{48,56},{56,64},{64,7... | collective-permute-start | bytes 98312 | tf_op jit(solution)/shard_map/ppermute | solution.py:442
  52.2 2.4 %collective-permute-start.4 = (bf16[128,128]{1,0:T(8,128)(2,1)S(1)}, bf16[128,128]{1,0:T(8,128)(2,1)S(1)}, u32[]{:S(2)}, u32[]{:S(2)}) collective-permute-start(bf16[128,128]{1,0:T(8,128)(2,1)S(1)} %get-tuple-element.41), channel_id=1, source_target_pairs={{8,0},{16,8},{24,16},{32,24},{40,32},{48,40},{56,48},{64,56},{72,6... | collective-permute-start | bytes 98312 | tf_op jit(solution)/shard_map/ppermute | solution.py:443
  54.7 3.1 %collective-permute-done.4.refs_2_.from_upper = bf16[128,128]{1,0:T(8,128)(2,1)S(1)} collective-permute-done((bf16[128,128]{1,0:T(8,128)(2,1)S(1)}, bf16[128,128]{1,0:T(8,128)(2,1)S(1)}, u32[]{:S(2)}, u32[]{:S(2)}) %collective-permute-start.4) | collective-permute-done | bytes 32800 | tf_op jit(solution)/shard_map/ppermute | solution.py:443
  58.2 0.7 shard_map.219.refs_0_
  58.9 12.7 %all-to-all-start.2 = ((bf16[12,16,128]{2,1,0:T(8,128)(2,1)}), bf16[12,16,128]{2,1,0:T(8,128)(2,1)S(1)}, u32[]{:S(2)}, u32[]{:S(2)}) async-start(bf16[12,16,128]{2,1,0:T(8,128)(2,1)} %shard_map.219.refs_0_), calls=%async_computation.2 | async-start | bytes 98304 | tf_op jit(solution)/shard_map/all_to_all | solution.py:304
  71.7 4.0 %collective-permute-start.5 = (bf16[2,256,128]{2,1,0:T(8,128)(2,1)S(1)}, bf16[2,256,128]{2,1,0:T(8,128)(2,1)S(1)}, u32[]{:S(2)}, u32[]{:S(2)}) collective-permute-start(bf16[2,256,128]{2,1,0:T(8,128)(2,1)S(1)} %get-tuple-element.44), channel_id=1, source_target_pairs={{0,2},{1,3},{2,0},{3,1},{4,6},{5,7},{6,4},{7,5},{8,10},{9,11},{10,... | collective-permute-start | bytes 393224 | tf_op jit(solution)/shard_map/ppermute | solution.py:308
  75.7 6.3 %collective-permute-done.5.refs_0_.refs_2_ = bf16[2,256,128]{2,1,0:T(8,128)(2,1)S(1)} collective-permute-done((bf16[2,256,128]{2,1,0:T(8,128)(2,1)S(1)}, bf16[2,256,128]{2,1,0:T(8,128)(2,1)S(1)}, u32[]{:S(2)}, u32[]{:S(2)}) %collective-permute-start.5) | collective-permute-done | bytes 131104 | tf_op jit(solution)/shard_map/ppermute | solution.py:308
  81.9 0.7 shard_map.221.refs_0_
  82.7 9.1 %all-to-all-start.3 = ((bf16[64,16,128]{2,1,0:T(8,128)(2,1)}), bf16[64,16,128]{2,1,0:T(8,128)(2,1)S(1)}, u32[]{:S(2)}, u32[]{:S(2)}) async-start(bf16[64,16,128]{2,1,0:T(8,128)(2,1)} %shard_map.221.refs_0_), calls=%async_computation.3 | async-start | bytes 524288 | tf_op jit(solution)/shard_map/all_to_all | solution.py:304
  91.8 7.2 %collective-permute-start.6 = (bf16[1,256,128]{2,1,0:T(8,128)(2,1)S(1)}, bf16[1,256,128]{2,1,0:T(8,128)(2,1)S(1)}, u32[]{:S(2)}, u32[]{:S(2)}) collective-permute-start(bf16[1,256,128]{2,1,0:T(8,128)(2,1)S(1)} %get-tuple-element.47), channel_id=1, source_target_pairs={{0,4},{1,5},{2,6},{3,7},{4,0},{5,1},{6,2},{7,3},{8,12},{9,13},{10,... | collective-permute-start | bytes 196616 | tf_op jit(solution)/shard_map/ppermute | solution.py:308
  99.0 7.2 %collective-permute-done.6.arrived = bf16[1,256,128]{2,1,0:T(8,128)(2,1)S(1)} collective-permute-done((bf16[1,256,128]{2,1,0:T(8,128)(2,1)S(1)}, bf16[1,256,128]{2,1,0:T(8,128)(2,1)S(1)}, u32[]{:S(2)}, u32[]{:S(2)}) %collective-permute-start.6) | collective-permute-done | bytes 65568 | tf_op jit(solution)/shard_map/ppermute | solution.py:308
  106.2 0.9 shard_map.223
  107.1 0.8 shard_map.224
  (42 shorter events, 0.6 us)
Async XLA Ops:
  2.4 7.8 %copy-start = (bf16[256,128]{1,0:T(8,128)(2,1)S(1)}, bf16[256,128]{1,0:T(8,128)(2,1)}, u32[]{:S(2)}) copy-start(bf16[256,128]{1,0:T(8,128)(2,1)} %refs_3_.3) | copy-start | bytes 196612
  2.4 17.7 %copy-start.2 = (bf16[1024,128]{1,0:T(8,128)(2,1)S(1)}, bf16[1024,128]{1,0:T(8,128)(2,1)}, u32[]{:S(2)}) copy-start(bf16[1024,128]{1,0:T(8,128)(2,1)} %refs_3_.2) | copy-start | bytes 786436
  2.4 20.4 %all-to-all-start = ((bf16[8,272,128]{2,1,0:T(8,128)(2,1)}), bf16[8,272,128]{2,1,0:T(8,128)(2,1)S(1)}, u32[]{:S(2)}, u32[]{:S(2)}) async-start(bf16[8,272,128]{2,1,0:T(8,128)(2,1)} %shard_map.215), calls=%async_computation | async-start | bytes 1114112 | tf_op jit(solution)/shard_map/all_to_all | solution.py:304
  10.2 9.9 %copy-start.12 = (f32[128]{0:T(128)S(1)}, f32[128]{0:T(128)}, u32[]{:S(2)}) copy-start(f32[128]{0:T(128)} %param.29) | copy-start | bytes 1540
  10.2 9.9 %copy-start.13 = (f32[128]{0:T(128)S(1)}, f32[128]{0:T(128)}, u32[]{:S(2)}) copy-start(f32[128]{0:T(128)} %param.27) | copy-start | bytes 1540
  10.2 9.9 %copy-start.14 = (f32[128]{0:T(128)S(1)}, f32[128]{0:T(128)}, u32[]{:S(2)}) copy-start(f32[128]{0:T(128)} %param.25) | copy-start | bytes 1540
  10.2 9.9 %copy-start.15 = (f32[128]{0:T(128)S(1)}, f32[128]{0:T(128)}, u32[]{:S(2)}) copy-start(f32[128]{0:T(128)} %param.23) | copy-start | bytes 1540
  10.2 9.9 %copy-start.1 = (bf16[384,128]{1,0:T(8,128)(2,1)S(1)}, bf16[384,128]{1,0:T(8,128)(2,1)}, u32[]{:S(2)}) copy-start(bf16[384,128]{1,0:T(8,128)(2,1)} %ew1.1) | copy-start | bytes 294916
  10.3 11.2 %collective-permute-start = (bf16[128,128]{1,0:T(8,128)(2,1)S(1)}, bf16[128,128]{1,0:T(8,128)(2,1)S(1)}, u32[]{:S(2)}, u32[]{:S(2)}) collective-permute-start(bf16[128,128]{1,0:T(8,128)(2,1)S(1)} %get-tuple-element.57), channel_id=1, source_target_pairs={{0,8},{8,16},{16,24},{24,32},{32,40},{40,48},{48,56},{56,64},{64,7... | collective-permute-start | bytes 98312 | tf_op jit(solution)/shard_map/ppermute | solution.py:374
  15.2 4.9 %copy-start.9 = (s32[1024,2]{0,1:T(2,128)S(1)}, s32[1024,2]{0,1:T(2,128)}, u32[]{:S(2)}) copy-start(s32[1024,2]{0,1:T(2,128)} %param.19) | copy-start | bytes 24580
  15.2 4.9 %copy-start.8 = (s32[1024,2]{0,1:T(2,128)S(1)}, s32[1024,2]{0,1:T(2,128)}, u32[]{:S(2)}) copy-start(s32[1024,2]{0,1:T(2,128)} %param.18) | copy-start | bytes 24580
  15.3 6.2 %collective-permute-start.1 = (bf16[128,128]{1,0:T(8,128)(2,1)S(1)}, bf16[128,128]{1,0:T(8,128)(2,1)S(1)}, u32[]{:S(2)}, u32[]{:S(2)}) collective-permute-start(bf16[128,128]{1,0:T(8,128)(2,1)S(1)} %get-tuple-element.56), channel_id=1, source_target_pairs={{8,0},{16,8},{24,16},{32,24},{40,32},{48,40},{56,48},{64,56},{72,6... | collective-permute-start | bytes 98312 | tf_op jit(solution)/shard_map/ppermute | solution.py:375
  20.1 2.7 %copy-start.3 = (bf16[1024,128]{1,0:T(8,128)(2,1)S(1)}, bf16[1024,128]{1,0:T(8,128)(2,1)}, u32[]{:S(2)}) copy-start(bf16[1024,128]{1,0:T(8,128)(2,1)} %refs_5_.1) | copy-start | bytes 786436
  20.1 2.7 %copy-start.4 = (bf16[256,128]{1,0:T(8,128)(2,1)S(1)}, bf16[256,128]{1,0:T(8,128)(2,1)}, u32[]{:S(2)}) copy-start(bf16[256,128]{1,0:T(8,128)(2,1)} %refs_11_.1) | copy-start | bytes 196612
  20.2 2.7 %copy-start.5 = (bf16[256,128]{1,0:T(8,128)(2,1)S(1)}, bf16[256,128]{1,0:T(8,128)(2,1)}, u32[]{:S(2)}) copy-start(bf16[256,128]{1,0:T(8,128)(2,1)} %refs_14_.1) | copy-start | bytes 196612
  29.1 15.9 %copy-start.11 = (bf16[1024,256]{1,0:T(8,128)(2,1)S(1)}, bf16[1024,256]{1,0:T(8,128)(2,1)}, u32[]{:S(2)}) copy-start(bf16[1024,256]{1,0:T(8,128)(2,1)} %copy-done.10) | copy-start | bytes 1572868
  29.1 29.1 %all-to-all-start.1 = ((bf16[64,16,128]{2,1,0:T(8,128)(2,1)}), bf16[64,16,128]{2,1,0:T(8,128)(2,1)S(1)}, u32[]{:S(2)}, u32[]{:S(2)}) async-start(bf16[64,16,128]{2,1,0:T(8,128)(2,1)} %bitcast.9), calls=%async_computation.1 | async-start | bytes 524288 | tf_op jit(solution)/shard_map/all_to_all | solution.py:304
  47.0 11.2 %collective-permute-start.2 = (bf16[4,256,128]{2,1,0:T(8,128)(2,1)S(1)}, bf16[4,256,128]{2,1,0:T(8,128)(2,1)S(1)}, u32[]{:S(2)}, u32[]{:S(2)}) collective-permute-start(bf16[4,256,128]{2,1,0:T(8,128)(2,1)S(1)} %get-tuple-element.39), channel_id=1, source_target_pairs={{0,1},{1,0},{2,3},{3,2},{4,5},{5,4},{6,7},{7,6},{8,9},{9,8},{10,11... | collective-permute-start | bytes 786440 | tf_op jit(solution)/shard_map/ppermute | solution.py:308
  50.3 4.3 %collective-permute-start.3 = (bf16[128,128]{1,0:T(8,128)(2,1)S(1)}, bf16[128,128]{1,0:T(8,128)(2,1)S(1)}, u32[]{:S(2)}, u32[]{:S(2)}) collective-permute-start(bf16[128,128]{1,0:T(8,128)(2,1)S(1)} %get-tuple-element.40), channel_id=1, source_target_pairs={{0,8},{8,16},{16,24},{24,32},{32,40},{40,48},{48,56},{56,64},{64,7... | collective-permute-start | bytes 98312 | tf_op jit(solution)/shard_map/ppermute | solution.py:442
  52.2 5.5 %collective-permute-start.4 = (bf16[128,128]{1,0:T(8,128)(2,1)S(1)}, bf16[128,128]{1,0:T(8,128)(2,1)S(1)}, u32[]{:S(2)}, u32[]{:S(2)}) collective-permute-start(bf16[128,128]{1,0:T(8,128)(2,1)S(1)} %get-tuple-element.41), channel_id=1, source_target_pairs={{8,0},{16,8},{24,16},{32,24},{40,32},{48,40},{56,48},{64,56},{72,6... | collective-permute-start | bytes 98312 | tf_op jit(solution)/shard_map/ppermute | solution.py:443
  58.9 23.0 %all-to-all-start.2 = ((bf16[12,16,128]{2,1,0:T(8,128)(2,1)}), bf16[12,16,128]{2,1,0:T(8,128)(2,1)S(1)}, u32[]{:S(2)}, u32[]{:S(2)}) async-start(bf16[12,16,128]{2,1,0:T(8,128)(2,1)} %shard_map.219.refs_0_), calls=%async_computation.2 | async-start | bytes 98304 | tf_op jit(solution)/shard_map/all_to_all | solution.py:304
  71.7 10.3 %collective-permute-start.5 = (bf16[2,256,128]{2,1,0:T(8,128)(2,1)S(1)}, bf16[2,256,128]{2,1,0:T(8,128)(2,1)S(1)}, u32[]{:S(2)}, u32[]{:S(2)}) collective-permute-start(bf16[2,256,128]{2,1,0:T(8,128)(2,1)S(1)} %get-tuple-element.44), channel_id=1, source_target_pairs={{0,2},{1,3},{2,0},{3,1},{4,6},{5,7},{6,4},{7,5},{8,10},{9,11},{10,... | collective-permute-start | bytes 393224 | tf_op jit(solution)/shard_map/ppermute | solution.py:308
  82.7 24.5 %all-to-all-start.3 = ((bf16[64,16,128]{2,1,0:T(8,128)(2,1)}), bf16[64,16,128]{2,1,0:T(8,128)(2,1)S(1)}, u32[]{:S(2)}, u32[]{:S(2)}) async-start(bf16[64,16,128]{2,1,0:T(8,128)(2,1)} %shard_map.221.refs_0_), calls=%async_computation.3 | async-start | bytes 524288 | tf_op jit(solution)/shard_map/all_to_all | solution.py:304
  91.8 14.4 %collective-permute-start.6 = (bf16[1,256,128]{2,1,0:T(8,128)(2,1)S(1)}, bf16[1,256,128]{2,1,0:T(8,128)(2,1)S(1)}, u32[]{:S(2)}, u32[]{:S(2)}) collective-permute-start(bf16[1,256,128]{2,1,0:T(8,128)(2,1)S(1)} %get-tuple-element.47), channel_id=1, source_target_pairs={{0,4},{1,5},{2,6},{3,7},{4,0},{5,1},{6,2},{7,3},{8,12},{9,13},{10,... | collective-permute-start | bytes 196616 | tf_op jit(solution)/shard_map/ppermute | solution.py:308
  (3 other events, 6.1 us)

commit v5 on v4

--- a/solution.py
+++ b/solution.py
@@ -75,6 +75,11 @@
 
 def place_of(away):
     return ((away & 1) << 2) | (away & 2) | (away >> 2)
+
+
+def rim_places(me, last):
+    first_core = me[1] == 0
+    return jnp.where(first_core, last, 0), jnp.where(first_core, 0, last)
 
 
 def pack_kernel(blocks, counts, nodes, out):
@@ -115,7 +120,7 @@
 
 
 def main_kernel(
-    lower, upper, incoming, nodes, eb, en, smark, tmark, joined, partial, ecot, ncot,
+    me, near_rim, far_rim, incoming, nodes, eb, en, smark, tmark, joined, partial, ecot, ncot,
     ew1, ew2, nw1, nw2, vectors,
     node_new, edge_new, wsum, wide, base,
     ext, gathered, active, unit, slope, scales, summed, dsum, g1, g2,
@@ -130,10 +135,11 @@
         at = (b % half) * BLOCK
         ext[at : at + BLOCK, (b // half) * W : (b // half + 1) * W] = block
 
-    place(0, lower[...])
+    near_at, far_at = rim_places(me, nblk + 1)
+    ext[pl.ds(pl.multiple_of(near_at * BLOCK, BLOCK), BLOCK), 0:W] = near_rim[...]
+    ext[pl.ds(pl.multiple_of(far_at * BLOCK, BLOCK), BLOCK), 0:W] = far_rim[...]
     for b in range(nblk):
         place(1 + b, nodes[b * BLOCK : (b + 1) * BLOCK, :])
-    place(1 + nblk, upper[...])
     n_slots = 2 * (half - 1) // incoming.shape[0]
     for p in range(incoming.shape[0]):
         for k in range(n_slots):
@@ -210,8 +216,8 @@
 
 def back_kernel(
     me, eb, en, incoming, wide, ecot, ew1,
-    far, near, to_lower, to_upper, own, target, edge_grad,
-    places, *, half,
+    far, near, near_rim, far_rim, own, target, edge_grad,
+    places, rims, *, half,
 ):
     rows = wide.shape[0]
     d = wide[:, 0:W] + wide[:, W:]
@@ -230,13 +236,15 @@
     owned = jnp.where(owned >= half, owned - half, owned)
     smark = marks(node[0:1, :], owned, (BLOCK, rows), 0)
 
+    far_at, near_at = rim_places(me, BLOCK)
+
     def store(b, sums):
         if b == 0:
-            to_lower[...] = sums.astype(BF)
+            rims[pl.ds(pl.multiple_of(far_at, BLOCK), BLOCK), :] = sums
         elif b <= nblk:
             own[(b - 1) * BLOCK : b * BLOCK, :] = sums
         elif b == nblk + 1:
-            to_upper[...] = sums.astype(BF)
+            rims[pl.ds(pl.multiple_of(near_at, BLOCK), BLOCK), :] = sums
         else:
             q, j = divmod(b - rim_blocks, nblk)
             places[place_of(q ^ me[0]), j * BLOCK : (j + 1) * BLOCK, :] = sums
@@ -251,6 +259,8 @@
             near[place] = places[place]
         else:
             far[place - peers // 2] = places[place].astype(BF)
+    near_rim[...] = rims[0:BLOCK, :].astype(BF)
+    far_rim[...] = rims[BLOCK:, :].astype(BF)
     tmark = marks(node[1:2, :], eb[1:2, :].astype(F32), (BLOCK, rows), 0)
     target[...] = dot(jnp.concatenate([one_hot(tmark, b) for b in range(nblk)], axis=0), d)
     edge_grad[...] = (ecot[...].astype(F32) + dot(d, ew1[2 * W :, :], NT)).astype(BF)
@@ -267,11 +277,11 @@
             send[k - count] = total.astype(BF)
 
 
-def finish_kernel(near, arrived, from_lower, from_upper, own, target, base, ew1, out, total):
+def finish_kernel(me, near, arrived, near_rim, far_rim, own, target, base, ew1, out, total):
     nblk = own.shape[0] // BLOCK
     total[...] = own[...] + near[0] + arrived[0].astype(F32)
-    total[0:BLOCK, :] += from_lower[...].astype(F32)
-    total[(nblk - 1) * BLOCK :, :] += from_upper[...].astype(F32)
+    for at, rim in zip(rim_places(me, (nblk - 1) * BLOCK), (near_rim, far_rim)):
+        total[pl.ds(pl.multiple_of(at, BLOCK), BLOCK), :] += rim[...].astype(F32)
     source_high, source_low = two_halves(total[...])
     target_high, target_low = two_halves(target[...])
     weights = ew1[...]
@@ -358,8 +368,8 @@
     edge_scale = float(edges * devices) ** (-0.5)
     node_scale = float(own_rows * devices) ** (-0.5)
     blocks = send_blocks[0].T
-    up = [(i, i + 1) for i in range(n_row - 1)]
-    down = [(i + 1, i) for i in range(n_row - 1)]
+    cores = [(0, 1), (1, 0)]
+    chips = [pair for i in range(1, n_row - 1, 2) for pair in ((i, i + 1), (i + 1, i))]
     eb = edge_blocks.T
     en = edge_nodes.T
 
@@ -371,8 +381,11 @@
         cost=pl.CostEstimate(flops=0, bytes_accessed=600000, transcendentals=0),
     )(blocks, send_counts, nodes)
     incoming = exchange(outgoing, "y")
-    lower = lax.ppermute(nodes[own_rows - BLOCK :], ROW, up)
-    upper = lax.ppermute(nodes[:BLOCK], ROW, down)
+    me = jnp.stack([lax.axis_index("y"), lax.axis_index("c")]).astype(jnp.int32)
+    first_core = me[1] == 0
+    head, tail = nodes[:BLOCK], nodes[own_rows - BLOCK :]
+    near_rim = lax.ppermute(jnp.where(first_core, tail, head), "c", cores)
+    far_rim = lax.ppermute(jnp.where(first_core, head, tail), ROW, chips)
 
     n_ext = own_rows + 2 * BLOCK + n_col * slots * BLOCK
     vectors = jnp.stack([edge_b1, edge_gain, node_b1, node_gain])
@@ -409,10 +422,10 @@
             pltpu.VMEM((W, 3 * W), F32),
             pltpu.VMEM((W, W), F32),
         ],
-        in_specs=[VM] * 17,
+        in_specs=[SMEM] + [VM] * 17,
         cost=pl.CostEstimate(flops=4 * 10**9, bytes_accessed=4000000, transcendentals=200000),
     )(
-        lower, upper, incoming, nodes, eb, en, smark, tmark,
+        me, near_rim, far_rim, incoming, nodes, eb, en, smark, tmark,
         joined, partial, edge_cot, node_cot,
         edge_w1, edge_w2, node_w1, node_w2, vectors,
     )
@@ -422,8 +435,7 @@
     spread = lax.axis_size(SPREAD)
     pieces = exchange(wsum.reshape(members, share, W), SCATTER)
 
-    me = lax.axis_index("y").astype(jnp.int32)[None]
-    far, near, to_lower, to_upper, own, target, edge_grad = call(
+    far, near, near_back, far_back, own, target, edge_grad = call(
         lambda *refs: back_kernel(*refs, half=n_ext // BLOCK // 2),
         (
             arr((n_col // 2, own_rows, W), BF),
@@ -434,15 +446,15 @@
             arr((own_rows, W), F32),
             arr((edges, W), BF),
         ),
-        scratch=[pltpu.VMEM((n_col, own_rows, W), F32)],
+        scratch=[pltpu.VMEM((n_col, own_rows, W), F32), pltpu.VMEM((2 * BLOCK, W), F32)],
         in_specs=[SMEM] + [VM] * 6,
         cost=pl.CostEstimate(flops=10**9, bytes_accessed=2000000, transcendentals=0),
     )(me, eb, en, incoming, wide, edge_cot, edge_w1)
     far = swap(far, 1)
-    from_lower = lax.ppermute(to_upper, ROW, up)
-    from_upper = lax.ppermute(to_lower, ROW, down)
-
-    part = add(pieces, spread, (far, from_lower, from_upper))
+    near_back = lax.ppermute(near_back, "c", cores)
+    far_back = lax.ppermute(far_back, ROW, chips)
+
+    part = add(pieces, spread, (far, near_back, far_back))
     pieces = exchange(part, SPREAD)
     near, far = fold((part,), near, far)
     far = swap(far, 2)
@@ -454,9 +466,9 @@
         finish_kernel,
         arr((own_rows, W), F32),
         scratch=[pltpu.VMEM((own_rows, W), F32)],
-        in_specs=[VM] * 8,
+        in_specs=[SMEM] + [VM] * 8,
         cost=pl.CostEstimate(flops=10**8, bytes_accessed=1000000, transcendentals=0),
-    )(near, far, from_lower, from_upper, own, target, base, edge_w1)
+    )(me, near, far, near_back, far_back, own, target, base, edge_w1)
     grads = call(
         unpack_kernel,
         tuple(arr((rows, W), F32) for rows in (3 * W, W, 2 * W, W)),

time: 109 us -> 110 us (level)
  Pallas kernels: 13.7 us -> 15.4 us
  starting transfers between devices: 73.9 us -> 72.7 us
  transfers between devices with their start and end apart: 11 -> 11, of which waited for: 5 -> 4; matrix products, arithmetic and copies ran while one was open for 0% -> 0% of each run, Pallas kernels for 4% -> 5%
where the time goes in v5:
time: 110 us
  starting transfers between devices  72.7 us (66%)
  waiting for transfers between devices  19 us (17%)
  Pallas kernels  15.4 us (14%)
  local copies, waits for them, and re-layouts  1.41 us (1%)
    all_to_all x4, starting transfers between devices, exchange(): return lax.all_to_all(value, axes, split_axis=0, concat_axis=0, tiled=True)  44.7 us
    ppermute x3, starting transfers between devices, swap(): lax.ppermute(value, 'y', [(i, i ^ bit) for i in range(lax.axis_size('y'))])  14.5 us
    ppermute x3, waiting for transfers between devices, swap(): lax.ppermute(value, 'y', [(i, i ^ bit) for i in range(lax.axis_size('y'))])  14.2 us
    pallas_call x1, Pallas kernels, local(): call(lambda *refs: main_kernel(*refs, edge_scale=edge_scale, node_scale=n...  6.05 us
    ppermute x1, starting transfers between devices, local(): far_rim = lax.ppermute(jnp.where(first_core, head, tail), ROW, chips)  4.97 us
    ppermute x1, starting transfers between devices, local(): near_rim = lax.ppermute(jnp.where(first_core, tail, head), 'c', cores)  4.15 us
    ppermute x1, waiting for transfers between devices, local(): far_back = lax.ppermute(far_back, ROW, chips)  3.33 us
    pallas_call x1, Pallas kernels, local(): call(lambda *refs: back_kernel(*refs, half=n_ext // BLOCK // 2), (arr((n_...  2.58 us
  transfers between devices with their start and end apart: 11, of which 4 were waited for; matrix products, arithmetic and copies ran while one was open for 0% of the time, Pallas kernels for 5%

profile of v5, /device:TPU:1, one launch (start us, length us, event | category | flops | bytes accessed | tf_op | source)
XLA Modules:
  0.0 109.5 jit_solution(2065012518042929572)
XLA Ops:
  0.6 1.8 %shard_map.215 = bf16[8,272,128]{2,1,0:T(8,128)(2,1)} custom-call(s32[2,8]{1,0:T(2,128)} %bitcast.18, s32[1,8]{1,0:T(1,128)} %counts.1, bf16[256,128]{1,0:T(8,128)(2,1)} %refs_4_.3), custom_call_target="tpu_custom_call" | custom-call | bytes 600000 | tf_op jit(solution)/shard_map/pallas_call | solution.py:376
  2.4 7.8 %all-to-all-start = ((bf16[8,272,128]{2,1,0:T(8,128)(2,1)}), bf16[8,272,128]{2,1,0:T(8,128)(2,1)S(1)}, u32[]{:S(2)}, u32[]{:S(2)}) async-start(bf16[8,272,128]{2,1,0:T(8,128)(2,1)} %shard_map.215), calls=%async_computation | async-start | bytes 1114112 | tf_op jit(solution)/shard_map/all_to_all | solution.py:314
  10.3 5.0 %collective-permute-start.1 = (bf16[128,128]{1,0:T(8,128)(2,1)S(1)}, bf16[128,128]{1,0:T(8,128)(2,1)S(1)}, u32[]{:S(2)}, u32[]{:S(2)}) collective-permute-start(bf16[128,128]{1,0:T(8,128)(2,1)S(1)} %get-tuple-element.56), channel_id=1, source_target_pairs={{8,16},{16,8},{24,32},{32,24},{40,48},{48,40},{56,64},{64,56},{72,... | collective-permute-start | bytes 98312 | tf_op jit(solution)/shard_map/ppermute | solution.py:388
  15.2 4.1 %collective-permute-start = (bf16[128,128]{1,0:T(8,128)(2,1)S(1)}, bf16[128,128]{1,0:T(8,128)(2,1)S(1)}, u32[]{:S(2)}, u32[]{:S(2)}) collective-permute-start(bf16[128,128]{1,0:T(8,128)(2,1)S(1)} %get-tuple-element.57), channel_id=1, source_target_pairs={{0,8},{8,0},{1,9},{9,1},{2,10},{10,2},{3,11},{11,3},{4,12},{12,4},... | collective-permute-start | bytes 98312 | tf_op jit(solution)/shard_map/ppermute | solution.py:387
  20.1 1.3 %shard_map.216 = (bf16[1024,128]{1,0:T(8,128)(2,1)S(1)}, bf16[1024,128]{1,0:T(8,128)(2,1)S(1)}, bf16[1024,256]{1,0:T(8,128)(2,1)S(1)}, f32[1024,128]{1,0:T(8,128)S(1)}) custom-call(bf16[256,128]{1,0:T(8,128)(2,1)S(1)} %copy-done, s32[2,1024]{1,0:T(2,128)S(1)} %bitcast.12, s32[2,1024]{1,0:T(2,128)S(1)} %bitcast.15, bf16[1024,128]{1,0:T(8,128)(2,1)S(1)} %copy-done.2, ...), custom_call_target="tpu_custom_call" | custom-call | flops 200000000 | bytes 8000000 | tf_op jit(solution)/shard_map/pallas_call | solution.py:392
  21.5 1.4 %all-to-all-done.refs_3_ = bf16[8,272,128]{2,1,0:T(8,128)(2,1)S(1)} async-done(((bf16[8,272,128]{2,1,0:T(8,128)(2,1)}), bf16[8,272,128]{2,1,0:T(8,128)(2,1)S(1)}, u32[]{:S(2)}, u32[]{:S(2)}) %all-to-all-start) | async-done | bytes 557088 | tf_op jit(solution)/shard_map/all_to_all | solution.py:314
  22.9 6.1 %shard_map.217 = (bf16[256,128]{1,0:T(8,128)(2,1)}, bf16[1024,128]{1,0:T(8,128)(2,1)}, bf16[1024,128]{1,0:T(8,128)(2,1)}, bf16[1024,256]{1,0:T(8,128)(2,1)S(1)}, f32[256,128]{1,0:T(8,128)S(1)}) custom-call(s32[2]{0:T(128)S(1)} %pad_add_fusion.refs_0_.me, bf16[128,128]{1,0:T(8,128)(2,1)S(1)} %collective-permute-done.refs_1_, ...), custom_call_target="tpu_custom_call" | custom-call | flops 4000000000 | bytes 4000000 | tf_op jit(solution)/shard_map/pallas_call | solution.py:404
  28.9 0.8 copy-done.10
  29.7 16.4 %all-to-all-start.1 = ((bf16[64,16,128]{2,1,0:T(8,128)(2,1)}), bf16[64,16,128]{2,1,0:T(8,128)(2,1)S(1)}, u32[]{:S(2)}, u32[]{:S(2)}) async-start(bf16[64,16,128]{2,1,0:T(8,128)(2,1)} %bitcast.10), calls=%async_computation.1 | async-start | bytes 524288 | tf_op jit(solution)/shard_map/all_to_all | solution.py:314
  46.2 2.6 %shard_map.218 = (bf16[4,256,128]{2,1,0:T(8,128)(2,1)S(1)}, f32[4,256,128]{2,1,0:T(8,128)S(1)}, bf16[128,128]{1,0:T(8,128)(2,1)S(1)}, bf16[128,128]{1,0:T(8,128)...) custom-call(s32[2]{0:T(128)S(1)} %pad_add_fusion.refs_0_.me, ...), custom_call_target="tpu_custom_call" | custom-call | flops 1000000000 | bytes 2000000 | tf_op jit(solution)/shard_map/pallas_call | solution.py:438
  48.8 3.3 %collective-permute-start.2 = (bf16[4,256,128]{2,1,0:T(8,128)(2,1)S(1)}, bf16[4,256,128]{2,1,0:T(8,128)(2,1)S(1)}, u32[]{:S(2)}, u32[]{:S(2)}) collective-permute-start(bf16[4,256,128]{2,1,0:T(8,128)(2,1)S(1)} %get-tuple-element.39), channel_id=1, source_target_pairs={{0,1},{1,0},{2,3},{3,2},{4,5},{5,4},{6,7},{7,6},{8,9},{9,8},{10,11... | collective-permute-start | bytes 786440 | tf_op jit(solution)/shard_map/ppermute | solution.py:318
  52.0 2.5 %collective-permute-start.3 = (bf16[128,128]{1,0:T(8,128)(2,1)S(1)}, bf16[128,128]{1,0:T(8,128)(2,1)S(1)}, u32[]{:S(2)}, u32[]{:S(2)}) collective-permute-start(bf16[128,128]{1,0:T(8,128)(2,1)S(1)} %get-tuple-element.40), channel_id=1, source_target_pairs={{0,8},{8,0},{1,9},{9,1},{2,10},{10,2},{3,11},{11,3},{4,12},{12,4},... | collective-permute-start | bytes 98312 | tf_op jit(solution)/shard_map/ppermute | solution.py:454
  54.6 1.9 %collective-permute-start.4 = (bf16[128,128]{1,0:T(8,128)(2,1)S(1)}, bf16[128,128]{1,0:T(8,128)(2,1)S(1)}, u32[]{:S(2)}, u32[]{:S(2)}) collective-permute-start(bf16[128,128]{1,0:T(8,128)(2,1)S(1)} %get-tuple-element.41), channel_id=1, source_target_pairs={{8,16},{16,8},{24,32},{32,24},{40,48},{48,40},{56,64},{64,56},{72,... | collective-permute-start | bytes 98312 | tf_op jit(solution)/shard_map/ppermute | solution.py:455
  56.5 3.3 %collective-permute-done.4.refs_2_.far_rim = bf16[128,128]{1,0:T(8,128)(2,1)S(1)} collective-permute-done((bf16[128,128]{1,0:T(8,128)(2,1)S(1)}, bf16[128,128]{1,0:T(8,128)(2,1)S(1)}, u32[]{:S(2)}, u32[]{:S(2)}) %collective-permute-start.4) | collective-permute-done | bytes 32800 | tf_op jit(solution)/shard_map/ppermute | solution.py:455
  59.9 0.7 shard_map.219.refs_0_
  60.6 11.1 %all-to-all-start.2 = ((bf16[12,16,128]{2,1,0:T(8,128)(2,1)}), bf16[12,16,128]{2,1,0:T(8,128)(2,1)S(1)}, u32[]{:S(2)}, u32[]{:S(2)}) async-start(bf16[12,16,128]{2,1,0:T(8,128)(2,1)} %shard_map.219.refs_0_), calls=%async_computation.2 | async-start | bytes 98304 | tf_op jit(solution)/shard_map/all_to_all | solution.py:314
  71.7 4.0 %collective-permute-start.5 = (bf16[2,256,128]{2,1,0:T(8,128)(2,1)S(1)}, bf16[2,256,128]{2,1,0:T(8,128)(2,1)S(1)}, u32[]{:S(2)}, u32[]{:S(2)}) collective-permute-start(bf16[2,256,128]{2,1,0:T(8,128)(2,1)S(1)} %get-tuple-element.44), channel_id=1, source_target_pairs={{0,2},{1,3},{2,0},{3,1},{4,6},{5,7},{6,4},{7,5},{8,10},{9,11},{10,... | collective-permute-start | bytes 393224 | tf_op jit(solution)/shard_map/ppermute | solution.py:318
  75.7 7.0 %collective-permute-done.5.refs_0_.refs_2_ = bf16[2,256,128]{2,1,0:T(8,128)(2,1)S(1)} collective-permute-done((bf16[2,256,128]{2,1,0:T(8,128)(2,1)S(1)}, bf16[2,256,128]{2,1,0:T(8,128)(2,1)S(1)}, u32[]{:S(2)}, u32[]{:S(2)}) %collective-permute-start.5) | collective-permute-done | bytes 131104 | tf_op jit(solution)/shard_map/ppermute | solution.py:318
  82.7 0.7 shard_map.221.refs_0_
  83.5 9.4 %all-to-all-start.3 = ((bf16[64,16,128]{2,1,0:T(8,128)(2,1)}), bf16[64,16,128]{2,1,0:T(8,128)(2,1)S(1)}, u32[]{:S(2)}, u32[]{:S(2)}) async-start(bf16[64,16,128]{2,1,0:T(8,128)(2,1)} %shard_map.221.refs_0_), calls=%async_computation.3 | async-start | bytes 524288 | tf_op jit(solution)/shard_map/all_to_all | solution.py:314
  92.9 7.2 %collective-permute-start.6 = (bf16[1,256,128]{2,1,0:T(8,128)(2,1)S(1)}, bf16[1,256,128]{2,1,0:T(8,128)(2,1)S(1)}, u32[]{:S(2)}, u32[]{:S(2)}) collective-permute-start(bf16[1,256,128]{2,1,0:T(8,128)(2,1)S(1)} %get-tuple-element.47), channel_id=1, source_target_pairs={{0,4},{1,5},{2,6},{3,7},{4,0},{5,1},{6,2},{7,3},{8,12},{9,13},{10,... | collective-permute-start | bytes 196616 | tf_op jit(solution)/shard_map/ppermute | solution.py:318
  100.1 7.2 %collective-permute-done.6.arrived = bf16[1,256,128]{2,1,0:T(8,128)(2,1)S(1)} collective-permute-done((bf16[1,256,128]{2,1,0:T(8,128)(2,1)S(1)}, bf16[1,256,128]{2,1,0:T(8,128)(2,1)S(1)}, u32[]{:S(2)}, u32[]{:S(2)}) %collective-permute-start.6) | collective-permute-done | bytes 65568 | tf_op jit(solution)/shard_map/ppermute | solution.py:318
  107.3 1.5 %shard_map.223 = f32[256,128]{1,0:T(8,128)} custom-call(s32[2]{0:T(128)S(1)} %pad_add_fusion.refs_0_.me, f32[1,256,128]{2,1,0:T(8,128)S(1)} %get-tuple-element.46.near, bf16[1,256,128]{2,1,0:T(8,128)(2,1)S(1)} %collective-permute-done.6.arrived, bf16[128,128]{1,0:T(8,128)(2,1)S(1)} %collective-permute-done.3.refs_1_.near_rim, ...), custom_call_target="tpu_custom_call" | custom-call | flops 100000000 | bytes 1000000 | tf_op jit(solution)/shard_map/pallas_call | solution.py:465
  108.8 0.8 shard_map.224
  (43 shorter events, 0.8 us)
Async XLA Ops:
  2.4 7.8 %copy-start = (bf16[256,128]{1,0:T(8,128)(2,1)S(1)}, bf16[256,128]{1,0:T(8,128)(2,1)}, u32[]{:S(2)}) copy-start(bf16[256,128]{1,0:T(8,128)(2,1)} %refs_4_.3) | copy-start | bytes 196612
  2.4 17.2 %copy-start.2 = (bf16[1024,128]{1,0:T(8,128)(2,1)S(1)}, bf16[1024,128]{1,0:T(8,128)(2,1)}, u32[]{:S(2)}) copy-start(bf16[1024,128]{1,0:T(8,128)(2,1)} %refs_3_.1) | copy-start | bytes 786436
  2.4 20.4 %all-to-all-start = ((bf16[8,272,128]{2,1,0:T(8,128)(2,1)}), bf16[8,272,128]{2,1,0:T(8,128)(2,1)S(1)}, u32[]{:S(2)}, u32[]{:S(2)}) async-start(bf16[8,272,128]{2,1,0:T(8,128)(2,1)} %shard_map.215), calls=%async_computation | async-start | bytes 1114112 | tf_op jit(solution)/shard_map/all_to_all | solution.py:314
  10.2 9.4 %copy-start.1 = (bf16[384,128]{1,0:T(8,128)(2,1)S(1)}, bf16[384,128]{1,0:T(8,128)(2,1)}, u32[]{:S(2)}) copy-start(bf16[384,128]{1,0:T(8,128)(2,1)} %ew1.1) | copy-start | bytes 294916
  10.2 9.2 %copy-start.12 = (f32[128]{0:T(128)S(1)}, f32[128]{0:T(128)}, u32[]{:S(2)}) copy-start(f32[128]{0:T(128)} %param.29) | copy-start | bytes 1540
  10.2 9.2 %copy-start.13 = (f32[128]{0:T(128)S(1)}, f32[128]{0:T(128)}, u32[]{:S(2)}) copy-start(f32[128]{0:T(128)} %param.27) | copy-start | bytes 1540
  10.2 9.2 %copy-start.14 = (f32[128]{0:T(128)S(1)}, f32[128]{0:T(128)}, u32[]{:S(2)}) copy-start(f32[128]{0:T(128)} %param.25) | copy-start | bytes 1540
  10.2 9.2 %copy-start.15 = (f32[128]{0:T(128)S(1)}, f32[128]{0:T(128)}, u32[]{:S(2)}) copy-start(f32[128]{0:T(128)} %param.23) | copy-start | bytes 1540
  10.3 11.2 %collective-permute-start.1 = (bf16[128,128]{1,0:T(8,128)(2,1)S(1)}, bf16[128,128]{1,0:T(8,128)(2,1)S(1)}, u32[]{:S(2)}, u32[]{:S(2)}) collective-permute-start(bf16[128,128]{1,0:T(8,128)(2,1)S(1)} %get-tuple-element.56), channel_id=1, source_target_pairs={{8,16},{16,8},{24,32},{32,24},{40,48},{48,40},{56,64},{64,56},{72,... | collective-permute-start | bytes 98312 | tf_op jit(solution)/shard_map/ppermute | solution.py:388
  15.2 6.2 %collective-permute-start = (bf16[128,128]{1,0:T(8,128)(2,1)S(1)}, bf16[128,128]{1,0:T(8,128)(2,1)S(1)}, u32[]{:S(2)}, u32[]{:S(2)}) collective-permute-start(bf16[128,128]{1,0:T(8,128)(2,1)S(1)} %get-tuple-element.57), channel_id=1, source_target_pairs={{0,8},{8,0},{1,9},{9,1},{2,10},{10,2},{3,11},{11,3},{4,12},{12,4},... | collective-permute-start | bytes 98312 | tf_op jit(solution)/shard_map/ppermute | solution.py:387
  20.1 2.7 %copy-start.3 = (bf16[1024,128]{1,0:T(8,128)(2,1)S(1)}, bf16[1024,128]{1,0:T(8,128)(2,1)}, u32[]{:S(2)}) copy-start(bf16[1024,128]{1,0:T(8,128)(2,1)} %refs_5_.1) | copy-start | bytes 786436
  20.1 2.7 %copy-start.4 = (bf16[256,128]{1,0:T(8,128)(2,1)S(1)}, bf16[256,128]{1,0:T(8,128)(2,1)}, u32[]{:S(2)}) copy-start(bf16[256,128]{1,0:T(8,128)(2,1)} %refs_12_.1) | copy-start | bytes 196612
  20.1 2.7 %copy-start.5 = (bf16[256,128]{1,0:T(8,128)(2,1)S(1)}, bf16[256,128]{1,0:T(8,128)(2,1)}, u32[]{:S(2)}) copy-start(bf16[256,128]{1,0:T(8,128)(2,1)} %refs_15_.1) | copy-start | bytes 196612
  20.1 2.7 %copy-start.6 = (bf16[128,128]{1,0:T(8,128)(2,1)S(1)}, bf16[128,128]{1,0:T(8,128)(2,1)}, u32[]{:S(2)}) copy-start(bf16[128,128]{1,0:T(8,128)(2,1)} %refs_14_.1) | copy-start | bytes 98308
  20.1 2.7 %copy-start.7 = (bf16[128,128]{1,0:T(8,128)(2,1)S(1)}, bf16[128,128]{1,0:T(8,128)(2,1)}, u32[]{:S(2)}) copy-start(bf16[128,128]{1,0:T(8,128)(2,1)} %refs_16_.1) | copy-start | bytes 98308
  29.7 16.5 %copy-start.11 = (bf16[1024,256]{1,0:T(8,128)(2,1)S(1)}, bf16[1024,256]{1,0:T(8,128)(2,1)}, u32[]{:S(2)}) copy-start(bf16[1024,256]{1,0:T(8,128)(2,1)} %copy-done.10) | copy-start | bytes 1572868
  29.7 30.2 %all-to-all-start.1 = ((bf16[64,16,128]{2,1,0:T(8,128)(2,1)}), bf16[64,16,128]{2,1,0:T(8,128)(2,1)S(1)}, u32[]{:S(2)}, u32[]{:S(2)}) async-start(bf16[64,16,128]{2,1,0:T(8,128)(2,1)} %bitcast.10), calls=%async_computation.1 | async-start | bytes 524288 | tf_op jit(solution)/shard_map/all_to_all | solution.py:314
  48.8 11.1 %collective-permute-start.2 = (bf16[4,256,128]{2,1,0:T(8,128)(2,1)S(1)}, bf16[4,256,128]{2,1,0:T(8,128)(2,1)S(1)}, u32[]{:S(2)}, u32[]{:S(2)}) collective-permute-start(bf16[4,256,128]{2,1,0:T(8,128)(2,1)S(1)} %get-tuple-element.39), channel_id=1, source_target_pairs={{0,1},{1,0},{2,3},{3,2},{4,5},{5,4},{6,7},{7,6},{8,9},{9,8},{10,11... | collective-permute-start | bytes 786440 | tf_op jit(solution)/shard_map/ppermute | solution.py:318
  52.0 4.5 %collective-permute-start.3 = (bf16[128,128]{1,0:T(8,128)(2,1)S(1)}, bf16[128,128]{1,0:T(8,128)(2,1)S(1)}, u32[]{:S(2)}, u32[]{:S(2)}) collective-permute-start(bf16[128,128]{1,0:T(8,128)(2,1)S(1)} %get-tuple-element.40), channel_id=1, source_target_pairs={{0,8},{8,0},{1,9},{9,1},{2,10},{10,2},{3,11},{11,3},{4,12},{12,4},... | collective-permute-start | bytes 98312 | tf_op jit(solution)/shard_map/ppermute | solution.py:454
  54.6 5.3 %collective-permute-start.4 = (bf16[128,128]{1,0:T(8,128)(2,1)S(1)}, bf16[128,128]{1,0:T(8,128)(2,1)S(1)}, u32[]{:S(2)}, u32[]{:S(2)}) collective-permute-start(bf16[128,128]{1,0:T(8,128)(2,1)S(1)} %get-tuple-element.41), channel_id=1, source_target_pairs={{8,16},{16,8},{24,32},{32,24},{40,48},{48,40},{56,64},{64,56},{72,... | collective-permute-start | bytes 98312 | tf_op jit(solution)/shard_map/ppermute | solution.py:455
  60.6 22.2 %all-to-all-start.2 = ((bf16[12,16,128]{2,1,0:T(8,128)(2,1)}), bf16[12,16,128]{2,1,0:T(8,128)(2,1)S(1)}, u32[]{:S(2)}, u32[]{:S(2)}) async-start(bf16[12,16,128]{2,1,0:T(8,128)(2,1)} %shard_map.219.refs_0_), calls=%async_computation.2 | async-start | bytes 98304 | tf_op jit(solution)/shard_map/all_to_all | solution.py:314
  71.7 11.0 %collective-permute-start.5 = (bf16[2,256,128]{2,1,0:T(8,128)(2,1)S(1)}, bf16[2,256,128]{2,1,0:T(8,128)(2,1)S(1)}, u32[]{:S(2)}, u32[]{:S(2)}) collective-permute-start(bf16[2,256,128]{2,1,0:T(8,128)(2,1)S(1)} %get-tuple-element.44), channel_id=1, source_target_pairs={{0,2},{1,3},{2,0},{3,1},{4,6},{5,7},{6,4},{7,5},{8,10},{9,11},{10,... | collective-permute-start | bytes 393224 | tf_op jit(solution)/shard_map/ppermute | solution.py:318
  83.5 25.3 %all-to-all-start.3 = ((bf16[64,16,128]{2,1,0:T(8,128)(2,1)}), bf16[64,16,128]{2,1,0:T(8,128)(2,1)S(1)}, u32[]{:S(2)}, u32[]{:S(2)}) async-start(bf16[64,16,128]{2,1,0:T(8,128)(2,1)} %shard_map.221.refs_0_), calls=%async_computation.3 | async-start | bytes 524288 | tf_op jit(solution)/shard_map/all_to_all | solution.py:314
  92.9 14.4 %collective-permute-start.6 = (bf16[1,256,128]{2,1,0:T(8,128)(2,1)S(1)}, bf16[1,256,128]{2,1,0:T(8,128)(2,1)S(1)}, u32[]{:S(2)}, u32[]{:S(2)}) collective-permute-start(bf16[1,256,128]{2,1,0:T(8,128)(2,1)S(1)} %get-tuple-element.47), channel_id=1, source_target_pairs={{0,4},{1,5},{2,6},{3,7},{4,0},{5,1},{6,2},{7,3},{8,12},{9,13},{10,... | collective-permute-start | bytes 196616 | tf_op jit(solution)/shard_map/ppermute | solution.py:318
  (3 other events, 2.2 us)

commit v6 on v4

--- a/solution.py
+++ b/solution.py
@@ -14,8 +14,8 @@
 SPLIT = {"x": 4, "z": 12, "c": 2, "y": 8}
 ALL = ("x", "z", "c", "y")
 ROW = ("x", "z", "c")
-SCATTER = ("x", "c", "y")
-SPREAD = "z"
+SCATTER = ("x", "y")
+SPREAD = ("z", "c")
 CHUNK = 1024
 WROWS = 1024
 UPPER = 4.0
@@ -74,7 +74,7 @@
 
 
 def place_of(away):
-    return ((away & 1) << 2) | (away & 2) | (away >> 2)
+    return ((away & 1) << 2) | ((away & 4) >> 1) | ((away & 2) >> 1)
 
 
 def pack_kernel(blocks, counts, nodes, out):
@@ -445,11 +445,11 @@
     part = add(pieces, spread, (far, from_lower, from_upper))
     pieces = exchange(part, SPREAD)
     near, far = fold((part,), near, far)
-    far = swap(far, 2)
+    far = swap(far, 4)
     part = add(pieces, members, (far,))
     weights = exchange(part, SCATTER)
     near, far = fold((part,), near, far)
-    far = swap(far, 4)
+    far = swap(far, 2)
     node_grad = call(
         finish_kernel,
         arr((own_rows, W), F32),

time: 109 us -> 110 us (level)
  the two profiles are of different devices: /device:TPU:1 before, /device:TPU:64 now
where the time goes in v6:
time: 110 us; the launch traced here: 109 us
  starting transfers between devices  64 us (58%)
  waiting for transfers between devices  29.3 us (27%)
  Pallas kernels  13.7 us (12%)
    all_to_all x4, starting transfers between devices, exchange(): return lax.all_to_all(value, axes, split_axis=0, concat_axis=0, tiled=True)  38.1 us
    ppermute x3, starting transfers between devices, swap(): lax.ppermute(value, 'y', [(i, i ^ bit) for i in range(lax.axis_size('y'))])  14.7 us
    ppermute x3, waiting for transfers between devices, swap(): lax.ppermute(value, 'y', [(i, i ^ bit) for i in range(lax.axis_size('y'))])  13.8 us
    all_to_all x4, waiting for transfers between devices, exchange(): return lax.all_to_all(value, axes, split_axis=0, concat_axis=0, tiled=True)  13.8 us
    pallas_call x1, Pallas kernels, local(): call(lambda *refs: main_kernel(*refs, edge_scale=edge_scale, node_scale=n...  5.48 us
    ppermute x1, starting transfers between devices, local(): upper = lax.ppermute(nodes[:BLOCK], ROW, down)  3.64 us
    ppermute x1, starting transfers between devices, local(): from_upper = lax.ppermute(to_lower, ROW, down)  3.64 us
  transfers between devices with their start and end apart: 11, of which 7 were waited for; matrix products, arithmetic and copies ran while one was open for 0% of the time, Pallas kernels for 4%

profile of v6, /device:TPU:64, one launch (start us, length us, event | category | flops | bytes accessed | tf_op | source)
XLA Modules:
  0.0 108.9 jit_solution(3949243584147131445)
XLA Ops:
  0.6 1.8 %shard_map.215 = bf16[8,272,128]{2,1,0:T(8,128)(2,1)} custom-call(s32[2,8]{1,0:T(2,128)} %bitcast.17, s32[1,8]{1,0:T(1,128)} %counts.1, bf16[256,128]{1,0:T(8,128)(2,1)} %refs_3_.3), custom_call_target="tpu_custom_call" | custom-call | bytes 600000 | tf_op jit(solution)/shard_map/pallas_call | solution.py:366
  2.4 7.2 %all-to-all-start = ((bf16[8,272,128]{2,1,0:T(8,128)(2,1)}), bf16[8,272,128]{2,1,0:T(8,128)(2,1)S(1)}, u32[]{:S(2)}, u32[]{:S(2)}) async-start(bf16[8,272,128]{2,1,0:T(8,128)(2,1)} %shard_map.215), calls=%async_computation | async-start | bytes 1114112 | tf_op jit(solution)/shard_map/all_to_all | solution.py:304
  9.7 2.1 %collective-permute-start = (bf16[128,128]{1,0:T(8,128)(2,1)S(1)}, bf16[128,128]{1,0:T(8,128)(2,1)S(1)}, u32[]{:S(2)}, u32[]{:S(2)}) collective-permute-start(bf16[128,128]{1,0:T(8,128)(2,1)S(1)} %get-tuple-element.57), channel_id=1, source_target_pairs={{0,8},{8,16},{16,24},{24,32},{32,40},{40,48},{48,56},{56,64},{64,7... | collective-permute-start | bytes 98312 | tf_op jit(solution)/shard_map/ppermute | solution.py:374
  11.8 3.6 %collective-permute-start.1 = (bf16[128,128]{1,0:T(8,128)(2,1)S(1)}, bf16[128,128]{1,0:T(8,128)(2,1)S(1)}, u32[]{:S(2)}, u32[]{:S(2)}) collective-permute-start(bf16[128,128]{1,0:T(8,128)(2,1)S(1)} %get-tuple-element.56), channel_id=1, source_target_pairs={{8,0},{16,8},{24,16},{32,24},{40,32},{48,40},{56,48},{64,56},{72,6... | collective-permute-start | bytes 98312 | tf_op jit(solution)/shard_map/ppermute | solution.py:375
  15.6 1.3 %shard_map.216 = (bf16[1024,128]{1,0:T(8,128)(2,1)S(1)}, bf16[1024,128]{1,0:T(8,128)(2,1)S(1)}, bf16[1024,256]{1,0:T(8,128)(2,1)S(1)}, f32[1024,128]{1,0:T(8,128)S(1)}) custom-call(bf16[256,128]{1,0:T(8,128)(2,1)S(1)} %copy-done, s32[2,1024]{1,0:T(2,128)S(1)} %bitcast.11, s32[2,1024]{1,0:T(2,128)S(1)} %bitcast.14, bf16[1024,128]{1,0:T(8,128)(2,1)S(1)} %copy-done.2, ...), custom_call_target="tpu_custom_call" | custom-call | flops 200000000 | bytes 8000000 | tf_op jit(solution)/shard_map/pallas_call | solution.py:379
  17.0 10.8 %all-to-all-done.refs_2_.refs_3_ = bf16[8,272,128]{2,1,0:T(8,128)(2,1)S(1)} async-done(((bf16[8,272,128]{2,1,0:T(8,128)(2,1)}), bf16[8,272,128]{2,1,0:T(8,128)(2,1)S(1)}, u32[]{:S(2)}, u32[]{:S(2)}) %all-to-all-start) | async-done | bytes 557088 | tf_op jit(solution)/shard_map/all_to_all | solution.py:304
  27.9 5.5 %shard_map.217 = (bf16[256,128]{1,0:T(8,128)(2,1)}, bf16[1024,128]{1,0:T(8,128)(2,1)}, bf16[1024,128]{1,0:T(8,128)(2,1)}, bf16[1024,256]{1,0:T(8,128)(2,1)S(1)}, f32[256,128]{1,0:T(8,128)S(1)}) custom-call(bf16[128,128]{1,0:T(8,128)(2,1)S(1)} %collective-permute-done.refs_0_, bf16[128,128]{1,0:T(8,128)(2,1)S(1)} %collective-permute-done.1.refs_1_, ...), custom_call_target="tpu_custom_call" | custom-call | flops 4000000000 | bytes 4000000 | tf_op jit(solution)/shard_map/pallas_call | solution.py:391
  33.3 0.8 copy-done.10
  34.1 4.8 %all-to-all-start.1 = ((bf16[32,32,128]{2,1,0:T(8,128)(2,1)}), bf16[32,32,128]{2,1,0:T(8,128)(2,1)S(1)}, u32[]{:S(2)}, u32[]{:S(2)}) async-start(bf16[32,32,128]{2,1,0:T(8,128)(2,1)} %bitcast.9), calls=%async_computation.1 | async-start | bytes 524288 | tf_op jit(solution)/shard_map/all_to_all | solution.py:304
  39.0 2.0 %shard_map.218 = (bf16[4,256,128]{2,1,0:T(8,128)(2,1)S(1)}, f32[4,256,128]{2,1,0:T(8,128)S(1)}, bf16[128,128]{1,0:T(8,128)(2,1)S(1)}, bf16[128,128]{1,0:T(8,128)...) custom-call(s32[1]{0:T(128)} %bitcast.8.refs_0_, s32[2,1024]{1,0:T(2,128)S(1)} %bitcast.13, ...), custom_call_target="tpu_custom_call" | custom-call | flops 1000000000 | bytes 2000000 | tf_op jit(solution)/shard_map/pallas_call | solution.py:426
  41.0 3.7 %collective-permute-start.2 = (bf16[4,256,128]{2,1,0:T(8,128)(2,1)S(1)}, bf16[4,256,128]{2,1,0:T(8,128)(2,1)S(1)}, u32[]{:S(2)}, u32[]{:S(2)}) collective-permute-start(bf16[4,256,128]{2,1,0:T(8,128)(2,1)S(1)} %get-tuple-element.39), channel_id=1, source_target_pairs={{0,1},{1,0},{2,3},{3,2},{4,5},{5,4},{6,7},{7,6},{8,9},{9,8},{10,11... | collective-permute-start | bytes 786440 | tf_op jit(solution)/shard_map/ppermute | solution.py:308
  44.7 1.9 %collective-permute-start.3 = (bf16[128,128]{1,0:T(8,128)(2,1)S(1)}, bf16[128,128]{1,0:T(8,128)(2,1)S(1)}, u32[]{:S(2)}, u32[]{:S(2)}) collective-permute-start(bf16[128,128]{1,0:T(8,128)(2,1)S(1)} %get-tuple-element.40), channel_id=1, source_target_pairs={{0,8},{8,16},{16,24},{24,32},{32,40},{40,48},{48,56},{56,64},{64,7... | collective-permute-start | bytes 98312 | tf_op jit(solution)/shard_map/ppermute | solution.py:442
  46.6 3.6 %collective-permute-start.4 = (bf16[128,128]{1,0:T(8,128)(2,1)S(1)}, bf16[128,128]{1,0:T(8,128)(2,1)S(1)}, u32[]{:S(2)}, u32[]{:S(2)}) collective-permute-start(bf16[128,128]{1,0:T(8,128)(2,1)S(1)} %get-tuple-element.41), channel_id=1, source_target_pairs={{8,0},{16,8},{24,16},{32,24},{40,32},{48,40},{56,48},{64,56},{72,6... | collective-permute-start | bytes 98312 | tf_op jit(solution)/shard_map/ppermute | solution.py:443
  50.3 1.6 %collective-permute-done.4.refs_2_.from_upper = bf16[128,128]{1,0:T(8,128)(2,1)S(1)} collective-permute-done((bf16[128,128]{1,0:T(8,128)(2,1)S(1)}, bf16[128,128]{1,0:T(8,128)(2,1)S(1)}, u32[]{:S(2)}, u32[]{:S(2)}) %collective-permute-start.4) | collective-permute-done | bytes 32800 | tf_op jit(solution)/shard_map/ppermute | solution.py:443
  53.1 16.7 %all-to-all-start.2 = ((bf16[24,32,128]{2,1,0:T(8,128)(2,1)}), bf16[24,32,128]{2,1,0:T(8,128)(2,1)S(1)}, u32[]{:S(2)}, u32[]{:S(2)}) async-start(bf16[24,32,128]{2,1,0:T(8,128)(2,1)} %shard_map.219.refs_0_), calls=%async_computation.2 | async-start | bytes 393216 | tf_op jit(solution)/shard_map/all_to_all | solution.py:304
  69.9 6.4 %collective-permute-start.5 = (bf16[2,256,128]{2,1,0:T(8,128)(2,1)S(1)}, bf16[2,256,128]{2,1,0:T(8,128)(2,1)S(1)}, u32[]{:S(2)}, u32[]{:S(2)}) collective-permute-start(bf16[2,256,128]{2,1,0:T(8,128)(2,1)S(1)} %get-tuple-element.44), channel_id=1, source_target_pairs={{0,4},{1,5},{2,6},{3,7},{4,0},{5,1},{6,2},{7,3},{8,12},{9,13},{10,... | collective-permute-start | bytes 393224 | tf_op jit(solution)/shard_map/ppermute | solution.py:308
  76.3 7.0 %collective-permute-done.5.refs_0_.refs_2_ = bf16[2,256,128]{2,1,0:T(8,128)(2,1)S(1)} collective-permute-done((bf16[2,256,128]{2,1,0:T(8,128)(2,1)S(1)}, bf16[2,256,128]{2,1,0:T(8,128)(2,1)S(1)}, u32[]{:S(2)}, u32[]{:S(2)}) %collective-permute-start.5) | collective-permute-done | bytes 131104 | tf_op jit(solution)/shard_map/ppermute | solution.py:308
  83.3 0.7 shard_map.221.refs_0_
  84.0 9.3 %all-to-all-start.3 = ((bf16[32,32,128]{2,1,0:T(8,128)(2,1)}), bf16[32,32,128]{2,1,0:T(8,128)(2,1)S(1)}, u32[]{:S(2)}, u32[]{:S(2)}) async-start(bf16[32,32,128]{2,1,0:T(8,128)(2,1)} %shard_map.221.refs_0_), calls=%async_computation.3 | async-start | bytes 524288 | tf_op jit(solution)/shard_map/all_to_all | solution.py:304
  93.4 4.6 %collective-permute-start.6 = (bf16[1,256,128]{2,1,0:T(8,128)(2,1)S(1)}, bf16[1,256,128]{2,1,0:T(8,128)(2,1)S(1)}, u32[]{:S(2)}, u32[]{:S(2)}) collective-permute-start(bf16[1,256,128]{2,1,0:T(8,128)(2,1)S(1)} %get-tuple-element.47), channel_id=1, source_target_pairs={{0,2},{1,3},{2,0},{3,1},{4,6},{5,7},{6,4},{7,5},{8,10},{9,11},{10,... | collective-permute-start | bytes 196616 | tf_op jit(solution)/shard_map/ppermute | solution.py:308
  98.0 6.3 %collective-permute-done.6.arrived = bf16[1,256,128]{2,1,0:T(8,128)(2,1)S(1)} collective-permute-done((bf16[1,256,128]{2,1,0:T(8,128)(2,1)S(1)}, bf16[1,256,128]{2,1,0:T(8,128)(2,1)S(1)}, u32[]{:S(2)}, u32[]{:S(2)}) %collective-permute-start.6) | collective-permute-done | bytes 65568 | tf_op jit(solution)/shard_map/ppermute | solution.py:308
  104.3 0.9 shard_map.223
  105.1 3.0 %all-to-all-done.3.weights = bf16[32,32,128]{2,1,0:T(8,128)(2,1)S(1)} async-done(((bf16[32,32,128]{2,1,0:T(8,128)(2,1)}), bf16[32,32,128]{2,1,0:T(8,128)(2,1)S(1)}, u32[]{:S(2)}, u32[]{:S(2)}) %all-to-all-start.3) | async-done | bytes 262176 | tf_op jit(solution)/shard_map/all_to_all | solution.py:304
  108.1 0.8 shard_map.224
  (42 shorter events, 1.6 us)
Async XLA Ops:
  2.4 7.2 %copy-start = (bf16[256,128]{1,0:T(8,128)(2,1)S(1)}, bf16[256,128]{1,0:T(8,128)(2,1)}, u32[]{:S(2)}) copy-start(bf16[256,128]{1,0:T(8,128)(2,1)} %refs_3_.3) | copy-start | bytes 196612
  2.4 13.1 %copy-start.2 = (bf16[1024,128]{1,0:T(8,128)(2,1)S(1)}, bf16[1024,128]{1,0:T(8,128)(2,1)}, u32[]{:S(2)}) copy-start(bf16[1024,128]{1,0:T(8,128)(2,1)} %refs_3_.2) | copy-start | bytes 786436
  2.4 25.4 %all-to-all-start = ((bf16[8,272,128]{2,1,0:T(8,128)(2,1)}), bf16[8,272,128]{2,1,0:T(8,128)(2,1)S(1)}, u32[]{:S(2)}, u32[]{:S(2)}) async-start(bf16[8,272,128]{2,1,0:T(8,128)(2,1)} %shard_map.215), calls=%async_computation | async-start | bytes 1114112 | tf_op jit(solution)/shard_map/all_to_all | solution.py:304
  9.6 5.8 %copy-start.12 = (f32[128]{0:T(128)S(1)}, f32[128]{0:T(128)}, u32[]{:S(2)}) copy-start(f32[128]{0:T(128)} %param.29) | copy-start | bytes 1540
  9.6 5.8 %copy-start.13 = (f32[128]{0:T(128)S(1)}, f32[128]{0:T(128)}, u32[]{:S(2)}) copy-start(f32[128]{0:T(128)} %param.27) | copy-start | bytes 1540
  9.7 5.8 %copy-start.14 = (f32[128]{0:T(128)S(1)}, f32[128]{0:T(128)}, u32[]{:S(2)}) copy-start(f32[128]{0:T(128)} %param.25) | copy-start | bytes 1540
  9.7 5.8 %copy-start.15 = (f32[128]{0:T(128)S(1)}, f32[128]{0:T(128)}, u32[]{:S(2)}) copy-start(f32[128]{0:T(128)} %param.23) | copy-start | bytes 1540
  9.7 5.8 %copy-start.1 = (bf16[384,128]{1,0:T(8,128)(2,1)S(1)}, bf16[384,128]{1,0:T(8,128)(2,1)}, u32[]{:S(2)}) copy-start(bf16[384,128]{1,0:T(8,128)(2,1)} %ew1.1) | copy-start | bytes 294916
  9.7 7.2 %collective-permute-start = (bf16[128,128]{1,0:T(8,128)(2,1)S(1)}, bf16[128,128]{1,0:T(8,128)(2,1)S(1)}, u32[]{:S(2)}, u32[]{:S(2)}) collective-permute-start(bf16[128,128]{1,0:T(8,128)(2,1)S(1)} %get-tuple-element.57), channel_id=1, source_target_pairs={{0,8},{8,16},{16,24},{24,32},{32,40},{40,48},{48,56},{56,64},{64,7... | collective-permute-start | bytes 98312 | tf_op jit(solution)/shard_map/ppermute | solution.py:374
  11.8 5.2 %collective-permute-start.1 = (bf16[128,128]{1,0:T(8,128)(2,1)S(1)}, bf16[128,128]{1,0:T(8,128)(2,1)S(1)}, u32[]{:S(2)}, u32[]{:S(2)}) collective-permute-start(bf16[128,128]{1,0:T(8,128)(2,1)S(1)} %get-tuple-element.56), channel_id=1, source_target_pairs={{8,0},{16,8},{24,16},{32,24},{40,32},{48,40},{56,48},{64,56},{72,6... | collective-permute-start | bytes 98312 | tf_op jit(solution)/shard_map/ppermute | solution.py:375
  15.5 12.3 %copy-start.3 = (bf16[1024,128]{1,0:T(8,128)(2,1)S(1)}, bf16[1024,128]{1,0:T(8,128)(2,1)}, u32[]{:S(2)}) copy-start(bf16[1024,128]{1,0:T(8,128)(2,1)} %refs_5_.1) | copy-start | bytes 786436
  15.5 12.3 %copy-start.4 = (bf16[256,128]{1,0:T(8,128)(2,1)S(1)}, bf16[256,128]{1,0:T(8,128)(2,1)}, u32[]{:S(2)}) copy-start(bf16[256,128]{1,0:T(8,128)(2,1)} %refs_11_.1) | copy-start | bytes 196612
  15.6 12.3 %copy-start.5 = (bf16[256,128]{1,0:T(8,128)(2,1)S(1)}, bf16[256,128]{1,0:T(8,128)(2,1)}, u32[]{:S(2)}) copy-start(bf16[256,128]{1,0:T(8,128)(2,1)} %refs_14_.1) | copy-start | bytes 196612
  15.6 12.3 %copy-start.6 = (bf16[128,128]{1,0:T(8,128)(2,1)S(1)}, bf16[128,128]{1,0:T(8,128)(2,1)}, u32[]{:S(2)}) copy-start(bf16[128,128]{1,0:T(8,128)(2,1)} %refs_13_.1) | copy-start | bytes 98308
  15.6 12.3 %copy-start.7 = (bf16[128,128]{1,0:T(8,128)(2,1)S(1)}, bf16[128,128]{1,0:T(8,128)(2,1)}, u32[]{:S(2)}) copy-start(bf16[128,128]{1,0:T(8,128)(2,1)} %refs_15_.1) | copy-start | bytes 98308
  34.1 4.8 %copy-start.11 = (bf16[1024,256]{1,0:T(8,128)(2,1)S(1)}, bf16[1024,256]{1,0:T(8,128)(2,1)}, u32[]{:S(2)}) copy-start(bf16[1024,256]{1,0:T(8,128)(2,1)} %copy-done.10) | copy-start | bytes 1572868
  34.1 18.3 %all-to-all-start.1 = ((bf16[32,32,128]{2,1,0:T(8,128)(2,1)}), bf16[32,32,128]{2,1,0:T(8,128)(2,1)S(1)}, u32[]{:S(2)}, u32[]{:S(2)}) async-start(bf16[32,32,128]{2,1,0:T(8,128)(2,1)} %bitcast.9), calls=%async_computation.1 | async-start | bytes 524288 | tf_op jit(solution)/shard_map/all_to_all | solution.py:304
  41.0 11.4 %collective-permute-start.2 = (bf16[4,256,128]{2,1,0:T(8,128)(2,1)S(1)}, bf16[4,256,128]{2,1,0:T(8,128)(2,1)S(1)}, u32[]{:S(2)}, u32[]{:S(2)}) collective-permute-start(bf16[4,256,128]{2,1,0:T(8,128)(2,1)S(1)} %get-tuple-element.39), channel_id=1, source_target_pairs={{0,1},{1,0},{2,3},{3,2},{4,5},{5,4},{6,7},{7,6},{8,9},{9,8},{10,11... | collective-permute-start | bytes 786440 | tf_op jit(solution)/shard_map/ppermute | solution.py:308
  44.7 5.6 %collective-permute-start.3 = (bf16[128,128]{1,0:T(8,128)(2,1)S(1)}, bf16[128,128]{1,0:T(8,128)(2,1)S(1)}, u32[]{:S(2)}, u32[]{:S(2)}) collective-permute-start(bf16[128,128]{1,0:T(8,128)(2,1)S(1)} %get-tuple-element.40), channel_id=1, source_target_pairs={{0,8},{8,16},{16,24},{24,32},{32,40},{40,48},{48,56},{56,64},{64,7... | collective-permute-start | bytes 98312 | tf_op jit(solution)/shard_map/ppermute | solution.py:442
  46.6 5.2 %collective-permute-start.4 = (bf16[128,128]{1,0:T(8,128)(2,1)S(1)}, bf16[128,128]{1,0:T(8,128)(2,1)S(1)}, u32[]{:S(2)}, u32[]{:S(2)}) collective-permute-start(bf16[128,128]{1,0:T(8,128)(2,1)S(1)} %get-tuple-element.41), channel_id=1, source_target_pairs={{8,0},{16,8},{24,16},{32,24},{40,32},{48,40},{56,48},{64,56},{72,6... | collective-permute-start | bytes 98312 | tf_op jit(solution)/shard_map/ppermute | solution.py:443
  53.1 30.2 %all-to-all-start.2 = ((bf16[24,32,128]{2,1,0:T(8,128)(2,1)}), bf16[24,32,128]{2,1,0:T(8,128)(2,1)S(1)}, u32[]{:S(2)}, u32[]{:S(2)}) async-start(bf16[24,32,128]{2,1,0:T(8,128)(2,1)} %shard_map.219.refs_0_), calls=%async_computation.2 | async-start | bytes 393216 | tf_op jit(solution)/shard_map/all_to_all | solution.py:304
  69.9 13.4 %collective-permute-start.5 = (bf16[2,256,128]{2,1,0:T(8,128)(2,1)S(1)}, bf16[2,256,128]{2,1,0:T(8,128)(2,1)S(1)}, u32[]{:S(2)}, u32[]{:S(2)}) collective-permute-start(bf16[2,256,128]{2,1,0:T(8,128)(2,1)S(1)} %get-tuple-element.44), channel_id=1, source_target_pairs={{0,4},{1,5},{2,6},{3,7},{4,0},{5,1},{6,2},{7,3},{8,12},{9,13},{10,... | collective-permute-start | bytes 393224 | tf_op jit(solution)/shard_map/ppermute | solution.py:308
  84.0 24.1 %all-to-all-start.3 = ((bf16[32,32,128]{2,1,0:T(8,128)(2,1)}), bf16[32,32,128]{2,1,0:T(8,128)(2,1)S(1)}, u32[]{:S(2)}, u32[]{:S(2)}) async-start(bf16[32,32,128]{2,1,0:T(8,128)(2,1)} %shard_map.221.refs_0_), calls=%async_computation.3 | async-start | bytes 524288 | tf_op jit(solution)/shard_map/all_to_all | solution.py:304
  93.4 10.9 %collective-permute-start.6 = (bf16[1,256,128]{2,1,0:T(8,128)(2,1)S(1)}, bf16[1,256,128]{2,1,0:T(8,128)(2,1)S(1)}, u32[]{:S(2)}, u32[]{:S(2)}) collective-permute-start(bf16[1,256,128]{2,1,0:T(8,128)(2,1)S(1)} %get-tuple-element.47), channel_id=1, source_target_pairs={{0,2},{1,3},{2,0},{3,1},{4,6},{5,7},{6,4},{7,5},{8,10},{9,11},{10,... | collective-permute-start | bytes 196616 | tf_op jit(solution)/shard_map/ppermute | solution.py:308
  (3 other events, 8.3 us)
